TPU v7x, 256 devices: a whole 4x4x8 slice. The times are simulated.
256 devices in a mesh: dp: 4 (over y), head: 64 (over x, z, core).
Axes of the slice: x: 4, y: 4, z: 8, core: 2. Of those that a mesh axis runs over, the one named last changes fastest.
Arguments:
- unfinished: int32 [128], P('dp'), may hold values from 0 to 255, as said below
- states: bfloat16 [256, 64, 128, 128], P(('dp', 'head')), may hold values from -6 to 6
- qkv_rows: bfloat16 [256, 64, 4, 3, 128], P(('dp', 'head')), may hold values from -6 to 6
- decay_rate: float32 [64], P('head'), may hold values from 0.02 to 2
- out_weight: bfloat16 [8192, 6144], P('head'), may hold values from -0.1875 to 0.1875
- hidden_in: bfloat16 [6144, 128, 4], P('head', 'dp'), may hold values from -6 to 6
- routes: int32 [128, 4, 2], P('dp'), may hold values from 0 to 31, as said below
- route_weight: float32 [128, 4, 2], P('dp'), may hold values from 0.2 to 1
- expert_up: bfloat16 [4, 6144, 2, 9216], P('dp', None, None, 'head'), may hold values from -0.078125 to 0.078125
- expert_down: bfloat16 [4, 9216, 6144], P('dp', 'head'), may hold values from -0.1875 to 0.1875
Outputs:
- mixed: bfloat16 [6144, 128, 4], P('head', 'dp')
Inputs may be any that keep to these rules, and one draw needn't show every extreme that they name: `unfinished`: entries are distinct, in no particular order. Data group g owns slots g * 64 to (g + 1) * 64 - 1; at most 48 entries fall in one group's slots, and exactly 48 in some group. `routes`: A token's two experts differ and at most one of them is below 4. Among the 128 tokens of one data group (aligned blocks of rows), each expert below 4 is named at most 16 times, and one of them exactly 16 times.
All inputs are finite; a program needn't handle non-finite values.
Results may differ from a plain program's by a relative error of at most 0.0044.
Values may be sent and summed in bfloat16 or wider, within the bound.
No kernel may reach another device: no remote copies, remote signals or barrier semaphores. Data moves between devices by JAX's collectives and lax.ppermute only.
A program may use at most 64 MiB of HBM per device.

v0:
```python
import jax
import jax.numpy as jnp
from jax import lax
from jax.sharding import PartitionSpec as P

EPSILON_HEAD = 1e-06
EPSILON_NORM = 1e-05


def lightning(state_rows, input_rows, rate_vec):
    factor = jnp.exp(-rate_vec)[None, :, None, None]
    memory = state_rows.astype(jnp.float32)
    outputs = []
    for step_index in range(input_rows.shape[2]):
        query_vec = jax.nn.silu(input_rows[:, :, step_index, 0].astype(jnp.float32))
        key_vec = jax.nn.silu(input_rows[:, :, step_index, 1].astype(jnp.float32))
        value_vec = input_rows[:, :, step_index, 2].astype(jnp.float32)
        memory = factor * memory + key_vec[..., :, None] * value_vec[..., None, :]
        outputs.append(
            jnp.einsum("rhe,rhef->rhf", query_vec, memory, precision=lax.Precision.HIGHEST)
        )
    stacked = jnp.stack(outputs, 2)
    scaled = stacked * lax.rsqrt(jnp.mean(stacked * stacked, -1, keepdims=True) + EPSILON_HEAD)
    return scaled.astype(jnp.bfloat16)


def per_device(
    unfinished,
    states,
    qkv_rows,
    decay_rate,
    out_weight,
    hidden_in,
    routes,
    route_weight,
    expert_up,
    expert_down,
):
    n_groups = lax.axis_size("dp")
    n_heads_axis = lax.axis_size("head")
    my_group = lax.axis_index("dp")
    row_grp = unfinished.shape[0]
    steps_count = qkv_rows.shape[2]
    slot_grp = states.shape[0] * n_heads_axis
    d_local = hidden_in.shape[0]
    d_model = d_local * n_heads_axis
    tok_grp = row_grp * steps_count
    heads_here = decay_rate.shape[0]
    rows_all = lax.all_gather(unfinished, "dp", axis=0, tiled=True)
    owner_group = rows_all // slot_grp
    local_states, local_inputs = (
        lax.all_to_all(states, "head", split_axis=1, concat_axis=0, tiled=True),
        lax.all_to_all(qkv_rows, "head", split_axis=1, concat_axis=0, tiled=True),
    )
    cap_rows = slot_grp * 3 // 4
    is_mine = (owner_group == my_group).astype(jnp.int32)
    mine_rank = jnp.cumsum(is_mine) - is_mine
    matched = (is_mine[:, None] == 1) & (mine_rank[:, None] == jnp.arange(cap_rows)[None, :])
    local_slot = rows_all - my_group * slot_grp
    slot_index = jnp.sum(jnp.where(matched, local_slot[:, None], 0), 0)
    attended = lightning(
        jnp.take(local_states, slot_index, 0), jnp.take(local_inputs, slot_index, 0), decay_rate
    )
    placing = matched.astype(jnp.bfloat16)
    outgoing = jnp.dot(
        placing, attended.reshape(cap_rows, -1), preferred_element_type=jnp.float32
    ).astype(jnp.bfloat16)
    arrived = lax.all_to_all(
        outgoing.reshape(n_groups, row_grp, -1), "dp", split_axis=0, concat_axis=0, tiled=True
    )
    head_rows = jnp.sum(arrived.astype(jnp.float32), 0).astype(jnp.bfloat16)
    head_rows = head_rows.reshape(row_grp, heads_here, steps_count, -1)
    head_flat = head_rows.transpose(0, 2, 1, 3).reshape(tok_grp, -1)
    columns = out_weight
    projected = lax.psum_scatter(
        lax.dot_general(
            columns, head_flat, (((0,), (1,)), ((), ())), preferred_element_type=jnp.float32
        ),
        "head",
        scatter_dimension=0,
        tiled=True,
    )
    residual = hidden_in.reshape(d_local, tok_grp).astype(jnp.float32) + projected
    square_sum = lax.psum(jnp.sum(residual * residual, 0), "head")
    normed = (residual * lax.rsqrt(square_sum / d_model + EPSILON_NORM)[None, :]).astype(
        jnp.bfloat16
    )
    cap_expert = tok_grp // 8
    flat_routes = routes.reshape(tok_grp * 2)
    one_hot = (flat_routes[:, None] == jnp.arange(n_groups)[None, :]).astype(jnp.int32)
    ranking = jnp.sum((jnp.cumsum(one_hot, 0) - one_hot) * one_hot, 1)
    in_flight = flat_routes < n_groups
    position = jnp.where(in_flight, flat_routes * cap_expert + ranking, -1).reshape(tok_grp, 2)
    matches = jnp.arange(n_groups * cap_expert)[:, None, None] == position[None, :, :]
    selector = jnp.any(matches, 2).astype(jnp.bfloat16)
    combiner = jnp.sum(jnp.where(matches, route_weight.reshape(tok_grp, 2)[None, :, :], 0.0), 2)
    all_features = lax.all_gather(normed, "head", axis=0, tiled=True)
    packed = jnp.dot(all_features, selector.T, preferred_element_type=jnp.float32).astype(
        jnp.bfloat16
    )
    expert_inputs = lax.all_to_all(packed, "dp", split_axis=1, concat_axis=1, tiled=True)
    hidden_local = expert_up.shape[3]
    weight_in = expert_up[0].reshape(d_model, 2 * hidden_local)
    gate_up = lax.dot_general(
        expert_inputs, weight_in, (((0,), (0,)), ((), ())), preferred_element_type=jnp.float32
    )
    expert_hidden = (jax.nn.silu(gate_up[:, :hidden_local]) * gate_up[:, hidden_local:]).astype(
        jnp.bfloat16
    )
    weight_out = expert_down[0]
    columns = weight_out
    expert_result = lax.psum_scatter(
        lax.dot_general(
            columns, expert_hidden, (((0,), (1,)), ((), ())), preferred_element_type=jnp.float32
        ),
        "head",
        scatter_dimension=0,
        tiled=True,
    ).astype(jnp.bfloat16)
    returned = lax.all_to_all(expert_result, "dp", split_axis=1, concat_axis=1, tiled=True)
    expert_mix = jnp.dot(returned.astype(jnp.float32), combiner, precision=lax.Precision.HIGHEST)
    mixed = (residual + expert_mix).astype(jnp.bfloat16)
    return mixed.reshape(d_local, row_grp, steps_count)


def solution(mesh):
    return jax.shard_map(
        per_device,
        mesh=mesh,
        in_specs=(
            P("dp"),
            P(("dp", "head"), None, None, None),
            P(("dp", "head"), None, None, None, None),
            P("head"),
            P("head", None),
            P("head", "dp", None),
            P("dp", None, None),
            P("dp", None, None),
            P("dp", None, None, "head"),
            P("dp", "head", None),
        ),
        out_specs=P("head", "dp", None),
        check_vma=False,
    )
```

profile of v0, /device:TPU:2, one launch (start us, length us, event | category | flops | bytes accessed | tf_op | source)
XLA Modules:
  0.0 652.7 jit_solution(6625087530407316131)
XLA Ops:
  6.5 22.6 %all_to_all.53 = bf16[1,64,4,3,128]{4,2,3,0,1:T(4,128)(2,1)} all-to-all(bf16[1,64,4,3,128]{4,2,3,0,1:T(4,128)(2,1)} %bitcast.160), channel_id=1, replica_groups=mesh['dp'=4,'head'=64] {'head'}, dimensions={1} | all-to-all | bytes 393216 | tf_op jit(solution)/shard_map/all_to_all | solution.py:53
  29.2 6.6 %all-to-all-start.1 = ((bf16[1,64,128,128]{3,2,0,1:T(8,128)(2,1)}), bf16[1,64,128,128]{3,2,0,1:T(8,128)(2,1)}, u32[]{:S(2)}, u32[]{:S(2)}) async-start(bf16[1,64,128,128]{3,2,0,1:T(8,128)(2,1)} %bitcast.155), calls=%async_computation.1 | async-start | bytes 4194304 | tf_op jit(solution)/shard_map/all_to_all | solution.py:52
  35.8 0.6 dynamic-slice
  37.1 0.2 dynamic-update-slice
  37.3 9.0 %all-reduce = s32[128]{0:T(128)S(1)} all-reduce(s32[128]{0:T(128)S(1)} %dynamic-update-slice), channel_id=1, replica_groups=mesh['dp'=4,'head'=64] {'dp'}, use_global_device_ids=true, to_apply=%add | all-reduce | flops 128 | bytes 1024
  46.4 0.7 copy.130
  47.1 1.6 reduce-window.19
  48.7 0.9 reduce.2
  50.4 0.7 broadcast_subtract_fusion
  51.2 2.3 gather_fusion
  53.5 1.1 bitcast_select_fusion
  54.6 0.8 fusion.75
  55.4 0.6 convert_multiply_fusion.6
  56.0 0.6 divide_multiply_fusion
  56.6 0.6 convert_multiply_fusion.4
  57.3 0.6 convert_multiply_fusion.2
  57.9 0.6 convert_multiply_fusion
  58.5 26.7 %all-to-all-done.1 = bf16[1,64,128,128]{3,2,0,1:T(8,128)(2,1)} async-done(((bf16[1,64,128,128]{3,2,0,1:T(8,128)(2,1)}), bf16[1,64,128,128]{3,2,0,1:T(8,128)(2,1)}, u32[]{:S(2)}, u32[]{:S(2)}) %all-to-all-start.1) | async-done | bytes 2097184 | tf_op jit(solution)/shard_map/all_to_all | solution.py:52
  85.2 3.5 gather_fusion.1
  88.8 4.6 fusion.35
  93.5 4.5 fusion.34
  98.1 6.0 fusion.33
  104.2 7.6 %fusion.36 = f32[48,1,1,128]{3,2,0,1:T(1,128)S(1)} fusion(f32[48,128,1]{1,2,0:T(1,128)S(1)} %bitcast.176, f32[48,128]{1,0:T(8,128)S(1)} %bitcast.174, f32[48,128]{1,0:T(8,128)S(1)} %copy-done.8, f32[48,128]{1,0:T(8,128)S(1)} %bitcast.169, f32[48,128]{1,0:T(8,128)S(1)} %copy-done.12, f32[48,128]{1,0:T(8,128)S(1)} %bitcast.167, f32[48,128]{1,0:T(8,128)S(1)} %copy-done.10, ...), kind=kOutput, calls=%fused_computation.47 | convolution fusion | flops 20447232 | bytes 1818676 | tf_op jit(solution)/shard_map/rhe,rhef->rhf/dot_general | solution.py:20
  111.8 0.2 multiply_reduce_fusion
  112.1 0.2 convolution_convert_fusion.1
  112.4 10.8 %all_to_all.54 = bf16[4,32,512]{2,1,0:T(8,128)(2,1)} all-to-all(bf16[4,32,512]{2,1,0:T(8,128)(2,1)S(1)} %bitcast.157), channel_id=1, replica_groups=mesh['dp'=4,'head'=64] {'dp'}, dimensions={0} | all-to-all | bytes 262144 | tf_op jit(solution)/shard_map/all_to_all | solution.py:68
  123.2 1.5 reduce_sum.64
  124.7 1.4 reshape_transpose_reshape.3
  126.1 3.7 convolution_bitcast_fusion
  129.8 3.5 copy.161
  133.4 1.5 copy.142
  134.9 135.9 %reduce-scatter.7.cloned.1.call-done = f32[96,128]{1,0:T(8,128)} async-done(((f32[6144,128]{1,0:T(8,128)}), f32[96,128]{1,0:T(8,128)}) %reduce-scatter.7.cloned.1.call-update) | async-done | bytes 49168 | tf_op jit(solution)/shard_map/reduce_scatter | solution.py:75
  270.8 1.4 multiply_reduce_fusion.1
  272.2 104.7 %psum.7 = f32[128]{0:T(128)S(1)} all-reduce(f32[128]{0:T(128)S(1)} %get-tuple-element.5), channel_id=1, replica_groups=mesh['dp'=4,'head'=64] {'head'}, use_global_device_ids=true, to_apply=%region_6.7 | all-reduce | flops 128 | bytes 1024 | tf_op jit(solution)/shard_map/psum | solution.py:84
  376.9 1.4 multiply_convert_fusion
  378.4 0.7 copy.146
  379.1 1.0 eq.73
  380.1 1.0 eq.69
  381.1 1.2 reduce-window.20
  382.4 0.7 copy.148
  383.1 0.7 reduce-window.21
  383.8 0.6 slice.61
  384.4 0.8 copy.149
  385.2 0.8 reduce_sum.67
  386.0 0.9 copy.150
  386.9 0.7 copy.145
  387.6 1.4 mul.286
  389.3 0.7 add_select_fusion
  390.0 0.5 copy-done.15
  390.5 77.9 %all-gather.2.cloned.1.call-done = bf16[6144,128]{1,0:T(8,128)(2,1)} async-done(((bf16[96,128]{1,0:T(8,128)(2,1)}), bf16[6144,128]{1,0:T(8,128)(2,1)}) %all-gather.2.cloned.1.call-update) | async-done | bytes 1572880 | tf_op jit(solution)/shard_map/all_gather | solution.py:97
  468.4 2.1 convolution_convert_fusion
  470.4 16.9 %all_to_all.55 = bf16[6144,4,16]{0,2,1:T(8,128)(2,1)S(1)} all-to-all(bf16[6144,4,16]{0,2,1:T(8,128)(2,1)S(1)} %bitcast.153), channel_id=1, replica_groups=mesh['dp'=4,'head'=64] {'dp'}, dimensions={1} | all-to-all | bytes 1572864 | tf_op jit(solution)/shard_map/all_to_all | solution.py:101
  487.4 1.3 fusion.76
  488.7 1.6 convolution_bitcast_fusion.1
  490.3 3.3 copy.163
  493.6 0.7 copy.151
  494.3 1.5 broadcast_in_dim.74
  495.7 136.2 %reduce-scatter.9.cloned.1.call-done = f32[96,64]{1,0:T(8,128)} async-done(((f32[6144,64]{1,0:T(8,128)}), f32[96,64]{1,0:T(8,128)}) %reduce-scatter.9.cloned.1.call-update) | async-done | bytes 24592
  631.9 1.5 copy.164
  633.4 4.3 all-to-all-start.4
  637.7 1.3 select_reduce_fusion
  639.0 4.1 all-to-all-done.4
  643.0 1.6 fusion.32
  644.7 1.5 copy.152
  (64 shorter events, 1.0 us)
Async XLA Ops:
  6.5 480.8 %copy-start = (bf16[1,6144,2,144]{1,3,2,0:T(8,128)(2,1)S(1)}, bf16[1,6144,2,144]{1,3,2,0:T(8,128)(2,1)}, u32[]{:S(2)}) copy-start(bf16[1,6144,2,144]{1,3,2,0:T(8,128)(2,1)} %param.18) | copy-start | bytes 10616836
  6.5 29.3 %copy-start.19 = (u32[256]{0:T(256)S(1)}, u32[256]{0:T(256)}, u32[]{:S(2)}) copy-start(u32[256]{0:T(256)} %constant.98) | copy-start | bytes 3076
  6.5 30.5 %copy-start.18 = (s32[32]{0:T(128)S(1)}, s32[32]{0:T(128)}, u32[]{:S(2)}) copy-start(s32[32]{0:T(128)} %param.10) | copy-start | bytes 388
  29.2 56.1 %all-to-all-start.1 = ((bf16[1,64,128,128]{3,2,0,1:T(8,128)(2,1)}), bf16[1,64,128,128]{3,2,0,1:T(8,128)(2,1)}, u32[]{:S(2)}, u32[]{:S(2)}) async-start(bf16[1,64,128,128]{3,2,0,1:T(8,128)(2,1)} %bitcast.155), calls=%async_computation.1 | async-start | bytes 4194304 | tf_op jit(solution)/shard_map/all_to_all | solution.py:52
  35.8 235.0 %reduce-scatter.7.cloned.1.call-start = ((), (), s32[]{:S(2)}) async-start(), calls=%async_computation.8 | async-start | bytes 3194880 | tf_op jit(solution)/shard_map/reduce_scatter | solution.py:75
  46.4 2.4 copy-start.17
  88.8 4.7 copy-start.2
  88.8 4.7 copy-start.4
  88.8 4.7 copy-start.6
  88.8 4.7 copy-start.9
  88.8 4.7 copy-start.10
  88.8 4.7 copy-start.13
  93.5 4.5 copy-start.5
  93.5 4.5 copy-start.12
  93.5 4.5 copy-start.14
  98.1 6.1 copy-start.7
  98.1 6.1 copy-start.8
  98.1 6.1 copy-start.11
  133.3 245.1 %copy-start.3 = (s32[32,4,2]{0,2,1:T(2,128)S(1)}, s32[32,4,2]{0,2,1:T(2,128)}, u32[]{:S(2)}) copy-start(s32[32,4,2]{0,2,1:T(2,128)} %param.16) | copy-start | bytes 3076
  133.4 335.0 %all-gather.2.cloned.1.call-start = ((), (), s32[]{:S(2)}) async-start(), calls=%async_computation.7 | async-start | bytes 1597440 | tf_op jit(solution)/shard_map/all_gather | solution.py:97
  378.4 253.5 %reduce-scatter.9.cloned.1.call-start = ((), (), s32[]{:S(2)}) async-start(), calls=%async_computation.9 | async-start | bytes 3194880
  390.0 0.5 copy-start.15
  470.4 18.2 %copy-start.1 = (bf16[1,144,6144]{2,1,0:T(8,128)(2,1)S(1)}, bf16[1,144,6144]{2,1,0:T(8,128)(2,1)}, u32[]{:S(2)}) copy-start(bf16[1,144,6144]{2,1,0:T(8,128)(2,1)} %param.19) | copy-start | bytes 5308420
  490.3 3.3 copy-start.16
  633.4 9.7 %all-to-all-start.4 = ((bf16[96,4,16]{0,2,1:T(8,128)(2,1)}), bf16[96,4,16]{0,2,1:T(8,128)(2,1)S(1)}, u32[]{:S(2)}, u32[]{:S(2)}) async-start(bf16[96,4,16]{0,2,1:T(8,128)(2,1)} %bitcast.163), calls=%async_computation.4 | async-start | bytes 32768 | tf_op jit(solution)/shard_map/all_to_all | solution.py:120
Sparse Core Ops, SparseCore 0:
  133.5 137.2 reduce-scatter.6
  378.5 89.8 all-gather.1
  493.7 138.1 reduce-scatter.8
where the time goes:
time: 654 us; the launch traced here: 653 us
  waiting for transfers between devices  381 us (58%)
  blocking collectives  164 us (25%)
  matrix products  33.3 us (5%)
  local copies, waits for them, and re-layouts  31.7 us (5%)
  other arithmetic  17 us (3%)
  between operations  14.8 us (2%)
  starting transfers between devices  11 us (2%)
    unnamed x4, waiting for transfers between devices  136 us
    reduce_scatter x1, waiting for transfers between devices, per_device(): lax.psum_scatter(lax.dot_general(columns, head_flat, (((0,), (1,)), ((),...  136 us
    psum x1, blocking collectives, per_device(): square_sum = lax.psum(jnp.sum(residual * residual, 0), 'head')  105 us
    all_gather x1, waiting for transfers between devices, per_device(): all_features = lax.all_gather(normed, 'head', axis=0, tiled=True)  77.9 us
    all_to_all x1, waiting for transfers between devices, per_device(): lax.all_to_all(states, 'head', split_axis=1, concat_axis=0, tiled=True)  26.7 us
    dot_general x4, matrix products, lightning(): jnp.einsum('rhe,rhef->rhf', query_vec, memory, precision=lax.Precision.HI...  22.8 us
    all_to_all x1, blocking collectives, per_device(): lax.all_to_all(qkv_rows, 'head', split_axis=1, concat_axis=0, tiled=True)  22.6 us
    all_to_all x1, blocking collectives, per_device(): lax.all_to_all(packed, 'dp', split_axis=1, concat_axis=1, tiled=True)  16.9 us
  transfers between devices with their start and end apart: 5, of which 5 were waited for; matrix products, arithmetic and copies ran while one was open for 4% of the time, Pallas kernels for 0%

commit v1 on v0

v1 whole, which is shorter than its diff:
```python
import functools

import jax
import jax.numpy as jnp
from jax import lax
from jax.experimental import pallas as pl
from jax.experimental.pallas import tpu as pltpu
from jax.sharding import Mesh, PartitionSpec as P

EPSILON_HEAD = 1e-06
EPSILON_NORM = 1e-05
BF16, F32 = jnp.bfloat16, jnp.float32
NX, NZ, NC = 4, 8, 2
EVERY = ("dp", "x", "z", "core")
HEAD = ("x", "z", "core")
MIB = 1 << 20


def vmem_spec():
    return pl.BlockSpec(memory_space=pltpu.VMEM)


def params(mib=48):
    return pltpu.CompilerParams(vmem_limit_bytes=mib * MIB)


def nt_dot(left, right):
    return lax.dot_general(left, right, (((1,), (1,)), ((), ())), preferred_element_type=F32)


def silu(value):
    return value / (1.0 + jnp.exp(-value))


def attend_kernel(state_ref, input_ref, base_ref, cross_ref):
    heads = state_ref.shape[0]
    query = silu(input_ref[:, 0].astype(F32))
    key = silu(input_ref[:, 1].astype(F32))
    value = input_ref[:, 2].astype(F32)
    high = query.astype(BF16)
    low = (query - high.astype(F32)).astype(BF16)
    for head in range(heads):
        state = state_ref[head]
        base_ref[head] = jnp.dot(high[head], state, preferred_element_type=F32) + jnp.dot(
            low[head], state, preferred_element_type=F32
        )
    for source in range(4):
        weight = jnp.sum(query * key[:, source : source + 1], -1, keepdims=True)
        cross_ref[source] = weight * value[:, source : source + 1]


def attend(states, inputs):
    heads, block = states.shape[0], 8
    return pl.pallas_call(
        attend_kernel,
        grid=(heads // block,),
        in_specs=[
            pl.BlockSpec((block, 128, 128), lambda i: (i, 0, 0)),
            pl.BlockSpec((block, 3, 4, 128), lambda i: (i, 0, 0, 0)),
        ],
        out_specs=[
            pl.BlockSpec((block, 4, 128), lambda i: (i, 0, 0)),
            pl.BlockSpec((4, block, 4, 128), lambda i: (0, i, 0, 0)),
        ],
        out_shape=[
            jax.ShapeDtypeStruct((heads, 4, 128), F32),
            jax.ShapeDtypeStruct((4, heads, 4, 128), F32),
        ],
        cost_estimate=pl.CostEstimate(flops=2 * 8 * 64 * 128 * 128, bytes_accessed=3 * MIB, transcendentals=65536),
        compiler_params=params(),
        name="attend",
    )(states, inputs)


def decay_kernel(base_ref, cross_ref, rate_ref, out_ref):
    rate = rate_ref[...]
    shape = base_ref.shape
    step = lax.broadcasted_iota(jnp.int32, shape, 1)
    stepf = step.astype(F32)
    attn = jnp.exp(-rate * (stepf + 1.0)) * base_ref[...]
    for source in range(4):
        lag = jnp.maximum(stepf - source, 0.0)
        attn += jnp.where(step >= source, jnp.exp(-rate * lag), 0.0) * cross_ref[source]
    scaled = attn * lax.rsqrt(jnp.mean(attn * attn, -1, keepdims=True) + EPSILON_HEAD)
    scaled = scaled.astype(BF16)
    for copy in range(out_ref.shape[0]):
        out_ref[copy] = scaled


def decay_heads(base, cross, rates, copies):
    return pl.pallas_call(
        decay_kernel,
        in_specs=[vmem_spec()] * 3,
        out_specs=vmem_spec(),
        out_shape=jax.ShapeDtypeStruct((copies,) + base.shape, BF16),
        compiler_params=params(),
        name="decay_heads",
    )(base, cross, rates)


def split_out_kernel(core_ref, weight_ref, keep_ref, send_ref):
    core = core_ref[0]
    weight = weight_ref[...]
    row = lax.broadcasted_iota(jnp.int32, (192, 384), 0)
    lane = lax.broadcasted_iota(jnp.int32, (192, 384), 1)
    for parity, out_ref in ((core, keep_ref), (1 - core, send_ref)):
        source = (row // 96) * 192 + row % 96 + parity * 96
        pick = (lane == source).astype(F32).astype(BF16)
        out_ref[...] = nt_dot(pick, weight).astype(BF16).reshape(out_ref.shape)


def split_out(core, weight):
    shape = jax.ShapeDtypeStruct((32, 96, 128), BF16)
    return pl.pallas_call(
        split_out_kernel,
        grid=(16,),
        in_specs=[
            pl.BlockSpec(memory_space=pltpu.SMEM),
            pl.BlockSpec((128, 384), lambda i: (0, i)),
        ],
        out_specs=[pl.BlockSpec((2, 96, 128), lambda i: (i, 0, 0))] * 2,
        out_shape=[shape, shape],
        cost_estimate=pl.CostEstimate(flops=2 * 16 * 384 * 384 * 128, bytes_accessed=3 * MIB, transcendentals=0),
        compiler_params=params(),
        name="split_out",
    )(core, weight)


def split_down_kernel(core_ref, weight_ref, keep_ref, send_ref):
    core = core_ref[0]
    weight = weight_ref[...]
    row = lax.broadcasted_iota(jnp.int32, (384, 256), 0)
    lane = lax.broadcasted_iota(jnp.int32, (384, 256), 1)
    for parity, out_ref in ((core, keep_ref), (1 - core, send_ref)):
        source = (lane // 128) * 192 + lane % 128 + parity * 96
        pick = ((row == source) & (lane % 128 < 96)).astype(F32).astype(BF16)
        out_ref[...] = jnp.dot(weight, pick, preferred_element_type=F32).astype(BF16)


def split_down(core, weight):
    hidden = weight.shape[0]
    shape = jax.ShapeDtypeStruct((hidden, 4096), BF16)
    return pl.pallas_call(
        split_down_kernel,
        grid=(16,),
        in_specs=[
            pl.BlockSpec(memory_space=pltpu.SMEM),
            pl.BlockSpec((hidden, 384), lambda i: (0, i)),
        ],
        out_specs=[pl.BlockSpec((hidden, 256), lambda i: (0, i))] * 2,
        out_shape=[shape, shape],
        cost_estimate=pl.CostEstimate(flops=2 * 16 * 384 * 512 * 144, bytes_accessed=4 * MIB, transcendentals=0),
        compiler_params=params(),
        name="split_down",
    )(core, weight)


def project_kernel(keep_ref, other_ref, mine_ref, theirs_ref, out_ref):
    blocks = keep_ref.shape[0]
    mine = mine_ref[...]
    theirs = theirs_ref[...]
    mine = jnp.concatenate([mine, mine[128:]], 0)
    theirs = jnp.concatenate([theirs, theirs[128:]], 0)
    total = nt_dot(keep_ref[...].reshape(blocks * 96, 128), mine) + nt_dot(
        other_ref[...].reshape(blocks * 96, 128), theirs
    )
    total = total.reshape(blocks, 96, 256)
    left = lax.broadcasted_iota(jnp.int32, (blocks, 48, 128), 2) < 64
    out_ref[:, :96] = total[:, :, :128].astype(BF16)
    out_ref[:, 96:] = jnp.where(left, total[:, :48, 128:], total[:, 48:, 128:]).astype(BF16)


def project(keep, other, mine, theirs):
    block = 8
    weights = pl.BlockSpec((block, 96, 128), lambda i: (i, 0, 0))
    tokens = pl.BlockSpec((192, 128), lambda i: (0, 0))
    return pl.pallas_call(
        project_kernel,
        grid=(32 // block,),
        in_specs=[weights, weights, tokens, tokens],
        out_specs=pl.BlockSpec((block, 144, 128), lambda i: (i, 0, 0)),
        out_shape=jax.ShapeDtypeStruct((32, 144, 128), BF16),
        compiler_params=params(),
        name="project",
    )(keep, other, mine, theirs)


def add_kernel(in_ref, out_ref):
    out_ref[...] = jnp.sum(in_ref[...].astype(F32), 0).astype(BF16)


def add_parts(parts):
    block = parts.shape[1] // 4
    return pl.pallas_call(
        add_kernel,
        grid=(4,),
        in_specs=[pl.BlockSpec((parts.shape[0], block, 128), lambda i: (0, i, 0))],
        out_specs=pl.BlockSpec((block, 128), lambda i: (i, 0)),
        out_shape=jax.ShapeDtypeStruct(parts.shape[1:], BF16),
        compiler_params=params(),
        name="add_parts",
    )(parts)


def residual_kernel(in_ref, hidden_ref, own_ref, send_ref):
    total = jnp.sum(in_ref[...].astype(F32), 0)
    own_ref[...] = total[:96]
    routed = (total[96:] + hidden_ref[...]).astype(BF16)
    for copy in range(send_ref.shape[0]):
        send_ref[copy] = routed


def residual_parts(parts, hidden, copies):
    return pl.pallas_call(
        residual_kernel,
        in_specs=[vmem_spec()] * 2,
        out_specs=[vmem_spec()] * 2,
        out_shape=[
            jax.ShapeDtypeStruct((96, 128), F32),
            jax.ShapeDtypeStruct((copies, 48, 128), BF16),
        ],
        compiler_params=params(),
        name="residual_parts",
    )(parts, hidden)


def up_kernel(core_ref, mine_ref, theirs_ref, weight_ref, out_ref, total_ref, square_ref):
    index = pl.program_id(0)
    even = core_ref[0] == 0
    blocks = mine_ref.shape[0]
    mine, theirs = mine_ref[...], theirs_ref[...]
    first = jnp.where(even, mine, theirs)
    second = jnp.where(even, theirs, mine)
    left = lax.broadcasted_iota(jnp.int32, (48, 128), 1) < 64
    zero = jnp.zeros((48, 128), BF16)
    pieces = []
    for block in range(blocks):
        for part in (first, second):
            pieces += [jnp.where(left, part[block], zero), jnp.where(left, zero, part[block])]
    tokens = jnp.concatenate(pieces, 0)

    @pl.when(index == 0)
    def _():
        total_ref[...] = jnp.zeros_like(total_ref)
        square_ref[...] = jnp.zeros_like(square_ref)

    total_ref[...] += jnp.dot(weight_ref[...], tokens, preferred_element_type=F32)
    wide = tokens.astype(F32)
    square_ref[...] += jnp.sum((wide * wide).reshape(-1, 8, 128), 0)

    @pl.when(index == pl.num_programs(0) - 1)
    def _():
        total, square = total_ref[...], jnp.sum(square_ref[...], 0, keepdims=True)
        total = total[:, :64] + total[:, 64:]
        square = square[:, :64] + square[:, 64:]
        total = total * lax.rsqrt(square / 6144.0 + EPSILON_NORM)
        half = total.shape[0] // 2
        out_ref[...] = (silu(total[:half]) * total[half:]).astype(BF16)


def up_project(core, mine, theirs, weight):
    rows, width = weight.shape
    steps = 4
    tokens = pl.BlockSpec((32 // steps, 48, 128), lambda i: (i, 0, 0))
    return pl.pallas_call(
        up_kernel,
        grid=(steps,),
        in_specs=[
            pl.BlockSpec(memory_space=pltpu.SMEM),
            tokens,
            tokens,
            pl.BlockSpec((rows, width // steps), lambda i: (0, i)),
        ],
        out_specs=pl.BlockSpec((rows // 2, 64), lambda i: (0, 0)),
        out_shape=jax.ShapeDtypeStruct((rows // 2, 64), BF16),
        scratch_shapes=[pltpu.VMEM((rows, 128), F32), pltpu.VMEM((8, 128), F32)],
        compiler_params=params(),
        name="up_project",
    )(core, mine, theirs, weight)


def down_kernel(mine_ref, theirs_ref, keep_ref, other_ref, out_ref):
    dims = (((0,), (0,)), ((), ()))
    total = lax.dot_general(
        mine_ref[...], keep_ref[...], dims, preferred_element_type=F32
    ) + lax.dot_general(theirs_ref[...], other_ref[...], dims, preferred_element_type=F32)
    total = total.astype(BF16)
    for block in range(out_ref.shape[1]):
        out_ref[:, block] = total[:, block * 128 : block * 128 + 128].reshape(4, 16, 128)


def down_project(mine, theirs, keep, other):
    hidden = mine.shape[0]
    steps = 4
    tokens = pl.BlockSpec((hidden, 64), lambda i: (0, 0))
    weights = pl.BlockSpec((hidden, 4096 // steps), lambda i: (0, i))
    return pl.pallas_call(
        down_kernel,
        grid=(steps,),
        in_specs=[tokens, tokens, weights, weights],
        out_specs=pl.BlockSpec((4, 32 // steps, 16, 128), lambda i: (0, i, 0, 0)),
        out_shape=jax.ShapeDtypeStruct((4, 32, 16, 128), BF16),
        compiler_params=params(),
        name="down_project",
    )(mine, theirs, keep, other)


def combine_kernel(parts_ref, place_ref, weight_ref, residual_ref, out_ref):
    result = jnp.sum(parts_ref[...].astype(F32), 1).astype(BF16).reshape(64, 128)
    fetched = jnp.dot(place_ref[...], result, preferred_element_type=F32)
    out_ref[...] = (residual_ref[...] + weight_ref[...] * fetched[:, :96]).astype(BF16)


def combine(parts, place, weight, residual):
    return pl.pallas_call(
        combine_kernel,
        in_specs=[vmem_spec()] * 4,
        out_specs=vmem_spec(),
        out_shape=jax.ShapeDtypeStruct((128, 96), BF16),
        compiler_params=params(),
        name="combine",
    )(parts, place, weight, residual)


def per_device(
    unfinished, states, qkv_rows, decay_rate, out_weight, hidden_in, routes, route_weight, expert_up, expert_down
):
    core = lax.axis_index("core").astype(jnp.int32).reshape(1)
    swap = functools.partial(lax.ppermute, axis_name="core", perm=[(0, 1), (1, 0)])

    with jax.named_scope("rates"):
        rates = lax.all_to_all(jnp.broadcast_to(decay_rate[:, None, None], (64, 1, 128)), HEAD, 0, 0, tiled=True)
    with jax.named_scope("attention"):
        base, cross = attend(states[0], qkv_rows[0].transpose(0, 2, 1, 3))

    with jax.named_scope("routing"):
        hidden = hidden_in.transpose(1, 2, 0).reshape(128, 96)
        pair = routes.reshape(128, 2)
        flying = pair < 4
        expert = jnp.min(pair, 1)
        weight = jnp.sum(jnp.where(flying, route_weight.reshape(128, 2), 0.0), 1, keepdims=True)
        named = (expert[:, None] == jnp.arange(4)[None, :]).astype(F32)
        before = jnp.arange(128)[:, None] > jnp.arange(128)[None, :]
        ranks = jnp.dot(before.astype(BF16), named.astype(BF16), preferred_element_type=F32)
        rank = jnp.sum(ranks * named, 1).astype(jnp.int32)
        position = jnp.where(expert < 4, expert * 16 + rank, -1)
        place = (position[:, None] == jnp.arange(64)[None, :]).astype(BF16)
        slots = jnp.repeat(unfinished, 4)
        steps = jnp.tile(jnp.arange(4), 32)
        facts = jnp.concatenate(
            [
                hidden,
                slots[:, None].astype(BF16),
                steps[:, None].astype(BF16),
                jnp.zeros((128, 30), BF16),
            ],
            1,
        )
        packed = lax.dot_general(place, facts, (((0,), (0,)), ((), ())), preferred_element_type=F32).astype(BF16)
        routed = lax.all_to_all(packed.reshape(4, 16, 128), "dp", 0, 0, tiled=True).reshape(64, 128)
        routed_index = (routed[:, 96].astype(F32) * 4.0 + routed[:, 97].astype(F32)).astype(jnp.int32)
        index = jnp.concatenate([slots * 4 + steps, routed_index])
        pick = (index[:, None] == jnp.arange(1024)[None, :]).astype(BF16)
        routed_hidden = routed[:, :96].astype(F32).T
        routed_hidden = jnp.concatenate([routed_hidden[:48], routed_hidden[48:]], 1)

    with jax.named_scope("weights"):
        keep_out, send_out = split_out(core, out_weight)
        other_out = swap(send_out)
        keep_down, send_down = split_down(core, expert_down[0])
        other_down = swap(send_down)

    with jax.named_scope("heads"):
        head_out = decay_heads(base, cross, rates, 4).reshape(256, 4, 128)
        head_rows = lax.all_to_all(head_out, EVERY, 0, 0, tiled=True).reshape(1024, 128)
        mine = jnp.dot(pick, head_rows, preferred_element_type=F32).astype(BF16)
        theirs = swap(mine)
    with jax.named_scope("projection"):
        partial = project(keep_out, other_out, mine, theirs)
        over_x = lax.all_to_all(partial.reshape(NX, NZ * 144, 128), "x", 0, 0, tiled=True)
        over_z = lax.all_to_all(add_parts(over_x).reshape(NZ, 144, 128), "z", 0, 0, tiled=True)
        own, routed_send = residual_parts(over_z, routed_hidden, NX * NZ)
    with jax.named_scope("expert"):
        features = lax.all_to_all(routed_send, ("x", "z"), 0, 0, tiled=True)
        up = expert_up[0].transpose(1, 2, 0).reshape(288, 6144)
        expert_hidden = up_project(core, features, swap(features), up)
        results = down_project(expert_hidden, swap(expert_hidden), keep_down, other_down)
        returned = lax.all_to_all(results.reshape(128, 16, 128), ("dp", "x", "z"), 0, 0, tiled=True)
    with jax.named_scope("output"):
        residual = own.T + hidden.astype(F32)
        mixed = combine(returned.reshape(4, 32, 16, 128), place, weight, residual)
        return mixed.reshape(32, 4, 96).transpose(2, 0, 1)


def solution(mesh):
    grid = Mesh(mesh.devices.reshape(mesh.shape["dp"], NX, NZ, NC), EVERY)
    return jax.shard_map(
        per_device,
        mesh=grid,
        in_specs=(
            P("dp"),
            P(EVERY, None, None, None),
            P(EVERY, None, None, None, None),
            P(HEAD),
            P(HEAD, None),
            P(HEAD, "dp", None),
            P("dp", None, None),
            P("dp", None, None),
            P("dp", None, None, HEAD),
            P("dp", HEAD, None),
        ),
        out_specs=P(HEAD, "dp", None),
        check_vma=False,
    )
```

time: 654 us -> 154 us (0.24)
  waiting for transfers between devices: 381 us -> 53.7 us
  blocking collectives: 164 us -> 16.4 us
  starting transfers between devices: 11 us -> 42.3 us
  matrix products: 33.3 us -> 2.09 us
  Pallas kernels: 0 us -> 25.2 us
  local copies, waits for them, and re-layouts: 31.7 us -> 8.24 us
  other arithmetic: 17 us -> 2.67 us
  between operations: 14.8 us -> 0.85 us
    unnamed x4 -> x0, waiting for transfers between devices: 136 us -> none
    reduce_scatter x1 -> x0, waiting for transfers between devices: 136 us -> none  [per_device(): lax.psum_scatter(lax.dot_general(columns, head_flat, (((0,), (1,)), ((),...]
    psum x1 -> x0, blocking collectives: 105 us -> none  [per_device(): square_sum = lax.psum(jnp.sum(residual * residual, 0), 'head')]
    all_gather x1 -> x0, waiting for transfers between devices: 77.9 us -> none  [per_device(): all_features = lax.all_gather(normed, 'head', axis=0, tiled=True)]
    all_to_all x3 -> x1, blocking collectives: 50.4 us -> 16.4 us  [per_device(): features = lax.all_to_all(routed_send, ('x', 'z'), 0, 0, tiled=True)]
    dot_general x10 -> x3, matrix products: 33.3 us -> 2.09 us  [the longest x1 1.62 us: per_device(): lax.dot_general(place, facts, (((0,), (0,)), ((), ())), preferred_element...]
    all_to_all x2 -> x6, starting transfers between devices: 10.9 us -> 41.7 us  [the longest x1 12 us: per_device(): lax.all_to_all(jnp.broadcast_to(decay_rate[:, None, None], (64, 1, 128)),...]
    pallas_call x0 -> x10, Pallas kernels: none -> 25.2 us  [the longest x1 7.87 us: split_down(): pl.pallas_call(split_down_kernel, grid=(16,), in_specs=[pl.BlockSpec(memo...]
  transfers between devices with their start and end apart: 5 -> 11, of which waited for: 5 -> 8; matrix products, arithmetic and copies ran while one was open for 4% -> 4% of each run, Pallas kernels for 0% -> 13%
where the time goes in v1:
time: 154 us; the launch traced here: 151 us
  waiting for transfers between devices  53.7 us (35%)
  starting transfers between devices  42.3 us (27%)
  Pallas kernels  25.2 us (16%)
  blocking collectives  16.4 us (11%)
  local copies, waits for them, and re-layouts  8.24 us (5%)
  other arithmetic  2.67 us (2%)
  matrix products  2.09 us (1%)
    all_to_all x1, waiting for transfers between devices, per_device(): lax.all_to_all(results.reshape(128, 16, 128), ('dp', 'x', 'z'), 0, 0, til...  18.2 us
    all_to_all x1, blocking collectives, per_device(): features = lax.all_to_all(routed_send, ('x', 'z'), 0, 0, tiled=True)  16.4 us
    all_to_all x1, starting transfers between devices, per_device(): lax.all_to_all(jnp.broadcast_to(decay_rate[:, None, None], (64, 1, 128)),...  12 us
    all_to_all x1, waiting for transfers between devices, per_device(): lax.all_to_all(add_parts(over_x).reshape(NZ, 144, 128), 'z', 0, 0, tiled=...  11.4 us
    all_to_all x1, waiting for transfers between devices, per_device(): lax.all_to_all(head_out, EVERY, 0, 0, tiled=True).reshape(1024, 128)  9.72 us
    all_to_all x1, starting transfers between devices, per_device(): lax.all_to_all(head_out, EVERY, 0, 0, tiled=True).reshape(1024, 128)  8.6 us
    all_to_all x1, starting transfers between devices, per_device(): lax.all_to_all(results.reshape(128, 16, 128), ('dp', 'x', 'z'), 0, 0, til...  8.27 us
    pallas_call x1, Pallas kernels, split_down(): pl.pallas_call(split_down_kernel, grid=(16,), in_specs=[pl.BlockSpec(memo...  7.87 us
  transfers between devices with their start and end apart: 11, of which 8 were waited for; matrix products, arithmetic and copies ran while one was open for 4% of the time, Pallas kernels for 13%

profile of v1, /device:TPU:2, one launch (start us, length us, event | category | flops | bytes accessed | tf_op | source)
XLA Modules:
  0.0 151.4 jit_solution(6846509738282780360)
XLA Ops:
  0.7 0.6 broadcast_in_dim.40
  1.3 12.0 %all-to-all-start.1 = ((f32[64,1,128]{2,1,0:T(1,128)}), f32[64,1,128]{2,1,0:T(1,128)S(1)}, u32[]{:S(2)}, u32[]{:S(2)}) async-start(f32[64,1,128]{2,1,0:T(1,128)} %broadcast_in_dim.40), calls=%async_computation.1 | async-start | bytes 65536 | tf_op jit(solution)/shard_map/rates/all_to_all | solution.py:332
  13.3 0.1 convert_element_type.87
  13.4 0.7 broadcast_multiply_fusion
  14.1 0.1 broadcast_in_dim.37
  14.2 0.1 convert_element_type.86
  14.3 0.7 reduce_min.11
  15.0 0.1 copy.26
  15.1 0.1 reduce_min.12
  15.2 0.1 fusion
  15.4 0.0 copy-start.8
  15.4 0.1 pad.7.clone
  15.5 1.6 %convolution_convert_fusion.1 = bf16[64,128]{1,0:T(8,128)(2,1)} fusion(bf16[128,1]{1,0:T(8,128)(2,1)S(1)} %convert_element_type.87, bf16[128,1]{1,0:T(8,128)(2,1)S(1)} %convert_element_type.86, bf16[128,96]{1,0:T(8,128)(2,1)} %bitcast.41, s32[128]{0:T(128)S(1)} %compare_select_fusion.1, bf16[128]{0:T(256)(128)(2,1)S(1)} %pad.7.clone), kind=kOutput, calls=%fused_computation.1 | convolution fusion | flops 2244608 | bytes 42240 | tf_op jit(solution)/shard_map/routing/dot_general | solution.py:359
  17.1 4.7 %all-to-all-done.1.rate_ref = f32[64,1,128]{2,1,0:T(1,128)S(1)} async-done(((f32[64,1,128]{2,1,0:T(1,128)}), f32[64,1,128]{2,1,0:T(1,128)S(1)}, u32[]{:S(2)}, u32[]{:S(2)}) %all-to-all-start.1) | async-done | bytes 32800 | tf_op jit(solution)/shard_map/rates/all_to_all | solution.py:332
  21.8 4.5 %all-to-all-start = ((bf16[4,16,128]{2,1,0:T(8,128)(2,1)}), bf16[4,16,128]{2,1,0:T(8,128)(2,1)S(1)}, u32[]{:S(2)}, u32[]{:S(2)}) async-start(bf16[4,16,128]{2,1,0:T(8,128)(2,1)} %bitcast.3), calls=%async_computation | async-start | bytes 32768 | tf_op jit(solution)/shard_map/routing/all_to_all | solution.py:360
  26.3 1.6 %copy-done.1 = bf16[1,64,128,128]{3,2,1,0:T(8,128)(2,1)S(1)} copy-done((bf16[1,64,128,128]{3,2,1,0:T(8,128)(2,1)S(1)}, bf16[1,64,128,128]{3,2,1,0:T(8,128)(2,1)}, u32[]{:S(2)}) %copy-start.1) | copy-done | bytes 2097176
  27.9 0.9 copy-done.2
  28.8 2.1 %attend.1 = (f32[64,4,128]{2,1,0:T(4,128)S(1)}, f32[4,64,4,128]{3,2,1,0:T(4,128)S(1)}) custom-call(bf16[64,128,128]{2,1,0:T(8,128)(2,1)S(1)} %bitcast.34, bf16[64,3,4,128]{3,2,1,0:T(4,128)(2,1)S(1)} %bitcast.36), custom_call_target="tpu_custom_call" | custom-call | flops 16777216 | bytes 3145728 | tf_op jit(solution)/shard_map/attention/attend/pallas_call | solution.py:54
  30.9 0.0 copy-done.8
  30.9 1.1 decay_heads.1
  32.0 0.0 all-to-all-done
  32.0 8.6 %all-to-all-start.2 = ((bf16[256,4,128]{2,1,0:T(4,128)(2,1)}), bf16[256,4,128]{2,1,0:T(4,128)(2,1)S(1)}, u32[]{:S(2)}, u32[]{:S(2)}) async-start(bf16[256,4,128]{2,1,0:T(4,128)(2,1)} %bitcast.9), calls=%async_computation.2 | async-start | bytes 524288 | tf_op jit(solution)/shard_map/heads/all_to_all | solution.py:375
  40.6 0.0 copy-done.4
  40.6 4.6 %split_out.1 = (bf16[32,96,128]{2,1,0:T(8,128)(2,1)S(1)}, bf16[32,96,128]{2,1,0:T(8,128)(2,1)S(1)}) custom-call(s32[1]{0:T(128)} %bitcast.core_ref, bf16[128,6144]{1,0:T(8,128)(2,1)S(1)} %copy-done.4), custom_call_target="tpu_custom_call" | custom-call | flops 603979776 | bytes 3145728 | tf_op jit(solution)/shard_map/weights/split_out/pallas_call | solution.py:114
  45.2 0.2 collective-permute-start
  45.4 0.1 iota_add_fusion
  45.5 0.1 add.21
  45.6 0.2 convert_reduce_fusion
  45.8 9.7 %all-to-all-done.2 = bf16[256,4,128]{2,1,0:T(4,128)(2,1)S(1)} async-done(((bf16[256,4,128]{2,1,0:T(4,128)(2,1)}), bf16[256,4,128]{2,1,0:T(4,128)(2,1)S(1)}, u32[]{:S(2)}, u32[]{:S(2)}) %all-to-all-start.2) | async-done | bytes 262176 | tf_op jit(solution)/shard_map/heads/all_to_all | solution.py:375
  55.5 0.3 convolution_convert_fusion.mine_ref
  55.9 0.1 collective-permute-start.1
  56.0 1.2 collective-permute-done.1.theirs_ref
  57.2 0.0 collective-permute-done.other_ref
  57.2 2.5 %project.1 = bf16[32,144,128]{2,1,0:T(8,128)(2,1)} custom-call(bf16[32,96,128]{2,1,0:T(8,128)(2,1)S(1)} %get-tuple-element.13.keep_ref, bf16[32,96,128]{2,1,0:T(8,128)(2,1)S(1)} %collective-permute-done.other_ref, bf16[192,128]{1,0:T(8,128)(2,1)S(1)} %convolution_convert_fusion.mine_ref, bf16[192,128]{1,0:T(8,128)(2,1)S(1)} %collective-permute-done.1.theirs_ref), custom_call_target="tpu_custom_call" | custom-call | tf_op jit(solution)/shard_map/projection/project/pallas_call | solution.py:177
  59.7 4.9 %all-to-all-start.3 = ((bf16[4,1152,128]{2,1,0:T(8,128)(2,1)}), bf16[4,1152,128]{2,1,0:T(8,128)(2,1)S(1)}, u32[]{:S(2)}, u32[]{:S(2)}) async-start(bf16[4,1152,128]{2,1,0:T(8,128)(2,1)} %bitcast.11), calls=%async_computation.3 | async-start | bytes 2359296 | tf_op jit(solution)/shard_map/projection/all_to_all | solution.py:380
  64.7 1.5 copy-done.3
  66.2 7.9 %split_down.1 = (bf16[144,4096]{1,0:T(8,128)(2,1)S(1)}, bf16[144,4096]{1,0:T(8,128)(2,1)}) custom-call(s32[1]{0:T(128)} %bitcast.core_ref, bf16[144,6144]{1,0:T(8,128)(2,1)S(1)} %bitcast.37), custom_call_target="tpu_custom_call" | custom-call | flops 905969664 | bytes 4194304 | tf_op jit(solution)/shard_map/weights/split_down/pallas_call | solution.py:143
  74.0 0.0 collective-permute-start.4
  74.0 0.7 copy.33
  74.7 5.6 %all-to-all-done.3.in_ref = bf16[4,1152,128]{2,1,0:T(8,128)(2,1)S(1)} async-done(((bf16[4,1152,128]{2,1,0:T(8,128)(2,1)}), bf16[4,1152,128]{2,1,0:T(8,128)(2,1)S(1)}, u32[]{:S(2)}, u32[]{:S(2)}) %all-to-all-start.3) | async-done | bytes 1179680 | tf_op jit(solution)/shard_map/projection/all_to_all | solution.py:380
  80.3 1.5 add_parts.1
  81.8 3.4 %all-to-all-start.4 = ((bf16[8,144,128]{2,1,0:T(8,128)(2,1)}), bf16[8,144,128]{2,1,0:T(8,128)(2,1)S(1)}, u32[]{:S(2)}, u32[]{:S(2)}) async-start(bf16[8,144,128]{2,1,0:T(8,128)(2,1)} %bitcast.12), calls=%async_computation.4 | async-start | bytes 589824 | tf_op jit(solution)/shard_map/projection/all_to_all | solution.py:381
  85.2 0.7 convert_bitcast_fusion
  86.0 0.1 pad_maximum_fusion.hidden_ref
  86.1 11.4 %all-to-all-done.4.in_ref = bf16[8,144,128]{2,1,0:T(8,128)(2,1)S(1)} async-done(((bf16[8,144,128]{2,1,0:T(8,128)(2,1)}), bf16[8,144,128]{2,1,0:T(8,128)(2,1)S(1)}, u32[]{:S(2)}, u32[]{:S(2)}) %all-to-all-start.4) | async-done | bytes 294944 | tf_op jit(solution)/shard_map/projection/all_to_all | solution.py:381
  97.5 0.1 residual_parts.1
  97.6 16.4 %all_to_all.35.mine_ref = bf16[32,48,128]{2,1,0:T(8,128)(2,1)S(1)} all-to-all(bf16[32,48,128]{2,1,0:T(8,128)(2,1)S(1)} %get-tuple-element.17), channel_id=1, replica_groups=mesh['dp'=4,'x'=4,'z'=8,'core'=2] {'x','z'}, dimensions={0} | all-to-all | bytes 786432 | tf_op jit(solution)/shard_map/expert/all_to_all | solution.py:384
  114.0 0.0 collective-permute-start.2
  114.0 1.7 %collective-permute-done.2.theirs_ref = bf16[32,48,128]{2,1,0:T(8,128)(2,1)S(1)} collective-permute-done((bf16[32,48,128]{2,1,0:T(8,128)(2,1)S(1)}, bf16[32,48,128]{2,1,0:T(8,128)(2,1)S(1)}, u32[]{:S(2)}, u32[]{:S(2)}) %collective-permute-start.2) | collective-permute-done | bytes 393248 | tf_op jit(solution)/shard_map/expert/ppermute | solution.py:386
  115.7 2.0 %copy-done = bf16[1,6144,2,144]{1,3,2,0:T(8,128)(2,1)S(1)} copy-done((bf16[1,6144,2,144]{1,3,2,0:T(8,128)(2,1)S(1)}, bf16[1,6144,2,144]{1,3,2,0:T(8,128)(2,1)}, u32[]{:S(2)}) %copy-start) | copy-done | bytes 3538968
  117.7 2.4 %up_project.1.mine_ref = bf16[144,64]{1,0:T(8,128)(2,1)S(1)} custom-call(s32[1]{0:T(128)} %bitcast.core_ref, bf16[32,48,128]{2,1,0:T(8,128)(2,1)S(1)} %all_to_all.35.mine_ref, bf16[32,48,128]{2,1,0:T(8,128)(2,1)S(1)} %collective-permute-done.2.theirs_ref, bf16[288,6144]{1,0:T(8,128)(2,1)S(1)} %bitcast.33), custom_call_target="tpu_custom_call" | custom-call | tf_op jit(solution)/shard_map/expert/up_project/pallas_call | solution.py:265
  120.1 0.2 collective-permute-start.3
  120.3 0.0 collective-permute-done.4.other_ref
  120.3 1.1 collective-permute-done.3.theirs_ref
  121.4 2.3 %down_project.1 = bf16[4,32,16,128]{3,2,1,0:T(8,128)(2,1)} custom-call(bf16[144,64]{1,0:T(8,128)(2,1)S(1)} %up_project.1.mine_ref, bf16[144,64]{1,0:T(8,128)(2,1)S(1)} %collective-permute-done.3.theirs_ref, bf16[144,4096]{1,0:T(8,128)(2,1)S(1)} %get-tuple-element.18.keep_ref, bf16[144,4096]{1,0:T(8,128)(2,1)S(1)} %collective-permute-done.4.other_ref), custom_call_target="tpu_custom_call" | custom-call | tf_op jit(solution)/shard_map/expert/down_project/pallas_call | solution.py:297
  123.6 8.3 %all-to-all-start.6 = ((bf16[128,16,128]{2,1,0:T(8,128)(2,1)}), bf16[128,16,128]{2,1,0:T(8,128)(2,1)S(1)}, u32[]{:S(2)}, u32[]{:S(2)}) async-start(bf16[128,16,128]{2,1,0:T(8,128)(2,1)} %bitcast.18), calls=%async_computation.6 | async-start | bytes 1048576 | tf_op jit(solution)/shard_map/expert/all_to_all | solution.py:388
  131.9 0.0 copy-done.6
  132.0 0.1 copy.30
  132.1 0.1 broadcast_in_dim.43.weight_ref
  132.1 0.0 copy-done.9
  132.1 0.1 fusion.2.place_ref
  132.2 0.1 copy.31
  132.4 18.2 %all-to-all-done.6 = bf16[128,16,128]{2,1,0:T(8,128)(2,1)S(1)} async-done(((bf16[128,16,128]{2,1,0:T(8,128)(2,1)}), bf16[128,16,128]{2,1,0:T(8,128)(2,1)S(1)}, u32[]{:S(2)}, u32[]{:S(2)}) %all-to-all-start.6) | async-done | bytes 524320 | tf_op jit(solution)/shard_map/expert/all_to_all | solution.py:388
  150.6 0.8 combine.1
  (18 shorter events, 0.1 us)
Async XLA Ops:
  1.3 20.5 %all-to-all-start.1 = ((f32[64,1,128]{2,1,0:T(1,128)}), f32[64,1,128]{2,1,0:T(1,128)S(1)}, u32[]{:S(2)}, u32[]{:S(2)}) async-start(f32[64,1,128]{2,1,0:T(1,128)} %broadcast_in_dim.40), calls=%async_computation.1 | async-start | bytes 65536 | tf_op jit(solution)/shard_map/rates/all_to_all | solution.py:332
  15.4 15.5 %copy-start.8 = (s32[128]{0:T(128)}, s32[128]{0:T(128)S(1)}, u32[]{:S(2)}) copy-start(s32[128]{0:T(128)S(1)} %compare_select_fusion.1) | copy-start | bytes 1540
  21.8 10.1 %all-to-all-start = ((bf16[4,16,128]{2,1,0:T(8,128)(2,1)}), bf16[4,16,128]{2,1,0:T(8,128)(2,1)S(1)}, u32[]{:S(2)}, u32[]{:S(2)}) async-start(bf16[4,16,128]{2,1,0:T(8,128)(2,1)} %bitcast.3), calls=%async_computation | async-start | bytes 32768 | tf_op jit(solution)/shard_map/routing/all_to_all | solution.py:360
  26.3 1.6 %copy-start.1 = (bf16[1,64,128,128]{3,2,1,0:T(8,128)(2,1)S(1)}, bf16[1,64,128,128]{3,2,1,0:T(8,128)(2,1)}, u32[]{:S(2)}) copy-start(bf16[1,64,128,128]{3,2,1,0:T(8,128)(2,1)} %param.11) | copy-start | bytes 6291460
  27.9 0.9 copy-start.2
  28.8 11.8 %copy-start.4 = (bf16[128,6144]{1,0:T(8,128)(2,1)S(1)}, bf16[128,6144]{1,0:T(8,128)(2,1)}, u32[]{:S(2)}) copy-start(bf16[128,6144]{1,0:T(8,128)(2,1)} %weight_ref.1) | copy-start | bytes 4718596
  32.0 23.6 %all-to-all-start.2 = ((bf16[256,4,128]{2,1,0:T(4,128)(2,1)}), bf16[256,4,128]{2,1,0:T(4,128)(2,1)S(1)}, u32[]{:S(2)}, u32[]{:S(2)}) async-start(bf16[256,4,128]{2,1,0:T(4,128)(2,1)} %bitcast.9), calls=%async_computation.2 | async-start | bytes 524288 | tf_op jit(solution)/shard_map/heads/all_to_all | solution.py:375
  45.2 12.0 %collective-permute-start = (bf16[32,96,128]{2,1,0:T(8,128)(2,1)S(1)}, bf16[32,96,128]{2,1,0:T(8,128)(2,1)S(1)}, u32[]{:S(2)}, u32[]{:S(2)}) collective-permute-start(bf16[32,96,128]{2,1,0:T(8,128)(2,1)S(1)} %get-tuple-element.14), channel_id=1, source_target_pairs={{0,1},{1,0},{2,3},{3,2},{4,5},{5,4},{6,7},{7,6},{8,9},{9,8},{10,11... | collective-permute-start | bytes 2359304 | tf_op jit(solution)/shard_map/weights/ppermute | solution.py:369
  55.9 1.3 collective-permute-start.1
  59.7 20.6 %all-to-all-start.3 = ((bf16[4,1152,128]{2,1,0:T(8,128)(2,1)}), bf16[4,1152,128]{2,1,0:T(8,128)(2,1)S(1)}, u32[]{:S(2)}, u32[]{:S(2)}) async-start(bf16[4,1152,128]{2,1,0:T(8,128)(2,1)} %bitcast.11), calls=%async_computation.3 | async-start | bytes 2359296 | tf_op jit(solution)/shard_map/projection/all_to_all | solution.py:380
  64.7 1.5 copy-start.3
  74.0 46.3 %collective-permute-start.4 = (bf16[144,4096]{1,0:T(8,128)(2,1)}, bf16[144,4096]{1,0:T(8,128)(2,1)S(1)}, u32[]{:S(2)}, u32[]{:S(2)}) collective-permute-start(bf16[144,4096]{1,0:T(8,128)(2,1)} %get-tuple-element.19), channel_id=1, source_target_pairs={{0,1},{1,0},{2,3},{3,2},{4,5},{5,4},{6,7},{7,6},{8,9},{9,8},{10,11... | collective-permute-start | bytes 3538952 | tf_op jit(solution)/shard_map/weights/ppermute | solution.py:371
  81.8 15.7 %all-to-all-start.4 = ((bf16[8,144,128]{2,1,0:T(8,128)(2,1)}), bf16[8,144,128]{2,1,0:T(8,128)(2,1)S(1)}, u32[]{:S(2)}, u32[]{:S(2)}) async-start(bf16[8,144,128]{2,1,0:T(8,128)(2,1)} %bitcast.12), calls=%async_computation.4 | async-start | bytes 589824 | tf_op jit(solution)/shard_map/projection/all_to_all | solution.py:381
  114.0 1.7 %collective-permute-start.2 = (bf16[32,48,128]{2,1,0:T(8,128)(2,1)S(1)}, bf16[32,48,128]{2,1,0:T(8,128)(2,1)S(1)}, u32[]{:S(2)}, u32[]{:S(2)}) collective-permute-start(bf16[32,48,128]{2,1,0:T(8,128)(2,1)S(1)} %all_to_all.35.mine_ref), channel_id=1, source_target_pairs={{0,1},{1,0},{2,3},{3,2},{4,5},{5,4},{6,7},{7,6},{8,9},{9,8},{10,11... | collective-permute-start | bytes 1179656 | tf_op jit(solution)/shard_map/expert/ppermute | solution.py:386
  115.7 2.0 %copy-start = (bf16[1,6144,2,144]{1,3,2,0:T(8,128)(2,1)S(1)}, bf16[1,6144,2,144]{1,3,2,0:T(8,128)(2,1)}, u32[]{:S(2)}) copy-start(bf16[1,6144,2,144]{1,3,2,0:T(8,128)(2,1)} %param.18) | copy-start | bytes 10616836
  120.1 1.3 collective-permute-start.3
  121.4 10.6 %copy-start.6 = (s32[32,4,2]{0,2,1:T(2,128)S(1)}, s32[32,4,2]{0,2,1:T(2,128)}, u32[]{:S(2)}) copy-start(s32[32,4,2]{0,2,1:T(2,128)} %param.16) | copy-start | bytes 3076
  121.4 10.6 %copy-start.7 = (f32[32,4,2]{0,2,1:T(2,128)S(1)}, f32[32,4,2]{0,2,1:T(2,128)}, u32[]{:S(2)}) copy-start(f32[32,4,2]{0,2,1:T(2,128)} %param.17) | copy-start | bytes 3076
  121.4 10.8 %copy-start.9 = (s32[128]{0:T(128)S(1)}, s32[128]{0:T(128)}, u32[]{:S(2)}) copy-start(s32[128]{0:T(128)} %copy-done.8) | copy-start | bytes 1540
  123.6 8.7 %copy-start.5 = (bf16[96,32,4]{0,2,1:T(4,128)(2,1)S(1)}, bf16[96,32,4]{0,2,1:T(4,128)(2,1)}, u32[]{:S(2)}) copy-start(bf16[96,32,4]{0,2,1:T(4,128)(2,1)} %param.15) | copy-start | bytes 73732
  123.6 26.9 %all-to-all-start.6 = ((bf16[128,16,128]{2,1,0:T(8,128)(2,1)}), bf16[128,16,128]{2,1,0:T(8,128)(2,1)S(1)}, u32[]{:S(2)}, u32[]{:S(2)}) async-start(bf16[128,16,128]{2,1,0:T(8,128)(2,1)} %bitcast.18), calls=%async_computation.6 | async-start | bytes 1048576 | tf_op jit(solution)/shard_map/expert/all_to_all | solution.py:388

commit v2 on v1

v2 whole, which is shorter than its diff:
```python
import functools

import jax
import jax.numpy as jnp
from jax import lax
from jax.experimental import pallas as pl
from jax.experimental.pallas import tpu as pltpu
from jax.sharding import Mesh, PartitionSpec as P

EPSILON_HEAD = 1e-06
EPSILON_NORM = 1e-05
BF16, F32 = jnp.bfloat16, jnp.float32
NX, NZ, NC = 4, 8, 2
EVERY = ("dp", "x", "z", "core")
HEAD = ("x", "z", "core")
MIB = 1 << 20


def vmem_spec():
    return pl.BlockSpec(memory_space=pltpu.VMEM)


def smem_spec():
    return pl.BlockSpec(memory_space=pltpu.SMEM)


def any_spec():
    return pl.BlockSpec(memory_space=pl.ANY)


def in_hbm(value):
    return pltpu.with_memory_space_constraint(value, pltpu.HBM)


def params(mib=12):
    return pltpu.CompilerParams(vmem_limit_bytes=mib * MIB)


def cost(flops, size):
    return pl.CostEstimate(flops=flops, bytes_accessed=size, transcendentals=0)


def shape(dims, dtype=BF16):
    return jax.ShapeDtypeStruct(dims, dtype)


def nt_dot(left, right):
    return lax.dot_general(left, right, (((1,), (1,)), ((), ())), preferred_element_type=F32)


def tn_dot(left, right):
    return lax.dot_general(left, right, (((0,), (0,)), ((), ())), preferred_element_type=F32)


def silu(value):
    return value / (1.0 + jnp.exp(-value))


def one_hot(mask):
    return mask.astype(F32).astype(BF16)


def attend_kernel(state_ref, input_ref, out_ref):
    heads = state_ref.shape[0]
    query = silu(input_ref[:, 0].astype(F32))
    key = silu(input_ref[:, 1].astype(F32))
    high = query.astype(BF16).astype(F32)
    both = jnp.concatenate([high, query - high], 1).astype(BF16)
    for head in range(heads):
        base = jnp.dot(both[head], state_ref[head], preferred_element_type=F32)
        out_ref[head, 0] = (base[:4] + base[4:]).astype(BF16)
    out_ref[:, 1] = input_ref[:, 2]
    lane = lax.broadcasted_iota(jnp.int32, query.shape, 2)
    cross = jnp.zeros(query.shape, F32)
    for source in range(4):
        weight = jnp.sum(query * key[:, source : source + 1], -1, keepdims=True)
        whole = weight.astype(BF16).astype(F32)
        cross = jnp.where(lane == source, whole, cross)
        cross = jnp.where(lane == source + 4, weight - whole, cross)
    out_ref[:, 2] = cross.astype(BF16)


def attend(states, inputs):
    heads, block = states.shape[0], 16
    return pl.pallas_call(
        attend_kernel,
        grid=(heads // block,),
        in_specs=[
            pl.BlockSpec((block, 128, 128), lambda i: (i, 0, 0)),
            pl.BlockSpec((block, 3, 4, 128), lambda i: (i, 0, 0, 0)),
        ],
        out_specs=pl.BlockSpec((block, 3, 4, 128), lambda i: (i, 0, 0, 0)),
        out_shape=shape((heads, 3, 4, 128)),
        cost_estimate=cost(2 * 8 * 64 * 128 * 128, 3 * MIB),
        compiler_params=params(),
        name="attend",
    )(in_hbm(states), inputs)


def decay_kernel(rate_ref, parts_ref, facts_ref, after_ref, out_ref):
    slots = parts_ref.shape[0]
    rate = jnp.full((4, 128), rate_ref[0], F32)
    step = lax.broadcasted_iota(jnp.int32, (4, 128), 0).astype(F32)
    value = parts_ref[:, 1].astype(F32)
    cross = parts_ref[:, 2].astype(F32)
    cross += pltpu.roll(cross, 124, 2)
    attn = jnp.exp(-rate * (step + 1.0)) * parts_ref[:, 0].astype(F32)
    for source in range(4):
        factor = jnp.where(step >= source, jnp.exp(-rate * jnp.maximum(step - source, 0.0)), 0.0)
        attn += (factor * cross[:, :, source : source + 1]) * value[:, source : source + 1]
    scaled = attn * lax.rsqrt(jnp.mean(attn * attn, -1, keepdims=True) + EPSILON_HEAD)
    scaled = scaled.astype(BF16)
    for group in range(out_ref.shape[0]):
        out_ref[group, :slots] = scaled
        out_ref[group, slots:] = facts_ref[group]


def decay_heads(rate, parts, facts, after):
    slots = parts.shape[0]
    return pl.pallas_call(
        decay_kernel,
        in_specs=[smem_spec(), vmem_spec(), vmem_spec(), any_spec()],
        out_specs=vmem_spec(),
        out_shape=shape((4, slots + 4, 4, 128)),
        cost_estimate=cost(4 * MIB, MIB),
        compiler_params=params(),
        name="decay_heads",
    )(rate, parts, facts, after)


def route_kernel(pair_ref, weight_ref, hidden_ref, row_ref, place_ref, factor_ref, out_ref):
    pair = pair_ref[...]
    expert = jnp.min(pair, 1, keepdims=True)
    factor_ref[...] = jnp.sum(jnp.where(pair < 4, weight_ref[...], 0.0), 1, keepdims=True)
    token = lax.broadcasted_iota(jnp.int32, (128, 128), 0)
    lane = lax.broadcasted_iota(jnp.int32, (128, 128), 1)
    named = (lane == expert).astype(F32)
    ranks = jnp.dot(one_hot(token > lane), named.astype(BF16), preferred_element_type=F32)
    rank = jnp.sum(ranks * named, 1, keepdims=True).astype(jnp.int32)
    position = jnp.where(expert < 4, expert * 16 + rank, -1)
    place = one_hot(lane == position)
    place_ref[...] = place
    row = row_ref[...].astype(F32)
    facts = hidden_ref[...].astype(F32)
    facts = jnp.where(lane == 96, row, jnp.where(lane == 97, (token % 4).astype(F32), facts))
    slots = jnp.where(lane == 98, row, 0.0)
    quarter = one_hot((token % 16 < 8) & (lane == (token // 16 * 8 + token % 16) * 4))
    packed = tn_dot(place, facts.astype(BF16)) + jnp.dot(quarter, slots.astype(BF16), preferred_element_type=F32)
    out_ref[...] = packed[:64].reshape(4, 4, 4, 128).astype(BF16)


def route(pair, weight, hidden, row):
    return pl.pallas_call(
        route_kernel,
        in_specs=[vmem_spec()] * 4,
        out_specs=[vmem_spec()] * 3,
        out_shape=[shape((128, 128)), shape((128, 1), F32), shape((4, 4, 4, 128))],
        cost_estimate=cost(8 * MIB, MIB // 2),
        compiler_params=params(),
        name="route",
    )(pair, weight, hidden, row)


def select_kernel(rows_ref, out_ref, hidden_ref):
    span = rows_ref.shape[0] // 4
    steps = span - 16
    facts = jnp.concatenate([rows_ref[group * span + steps : (group + 1) * span] for group in range(4)], 0)
    held = facts.astype(F32)
    token = lax.broadcasted_iota(jnp.int32, (128, 64), 0)
    source = lax.broadcasted_iota(jnp.int32, (128, 64), 1)
    spread = one_hot(source == token // 32 * 16 + token % 32 // 4)
    rest = jnp.dot(spread, facts, preferred_element_type=F32)
    step = (lax.broadcasted_iota(jnp.int32, (128, 1), 0) % 4).astype(F32)
    row = jnp.concatenate([held[:, 96:97], rest[:, 98:99]], 0)
    step = jnp.concatenate([held[:, 97:98], step], 0)
    row = (row * 4.0 + step).astype(jnp.int32)
    row = row // steps * span + row % steps
    lane = lax.broadcasted_iota(jnp.int32, (192, rows_ref.shape[0]), 1)
    out_ref[...] = jnp.dot(one_hot(lane == row), rows_ref[...], preferred_element_type=F32).astype(BF16)
    turned = jnp.concatenate([held, held], 0).T
    left = lax.broadcasted_iota(jnp.int32, (48, 128), 1) < 64
    hidden_ref[...] = jnp.where(left, turned[:48], turned[48:96])


def select(rows):
    return pl.pallas_call(
        select_kernel,
        in_specs=[vmem_spec()],
        out_specs=[vmem_spec()] * 2,
        out_shape=[shape((192, 128)), shape((48, 128), F32)],
        cost_estimate=cost(2 * 192 * 1088 * 128, MIB),
        compiler_params=params(),
        name="select",
    )(rows)


def split_out_kernel(where_ref, mine_ref, theirs_ref, after_ref, *out_refs):
    core = where_ref[0]
    row = lax.broadcasted_iota(jnp.int32, (192, 384), 0)
    lane = lax.broadcasted_iota(jnp.int32, (192, 384), 1)
    pick = one_hot(lane == row // 96 * 192 + row % 96 + core * 96)
    for part in range(4):
        for weight_ref, out_ref in zip((mine_ref, theirs_ref), out_refs):
            weight = weight_ref[:, part * 384 : part * 384 + 384]
            out_ref[2 * part : 2 * part + 2] = nt_dot(pick, weight).astype(BF16).reshape(2, 96, 128)


def split_out(where, mine, theirs, after):
    return pl.pallas_call(
        split_out_kernel,
        grid=(4,),
        in_specs=[smem_spec()] + [pl.BlockSpec((128, 1536), lambda i: (0, i))] * 2 + [any_spec()],
        out_specs=[pl.BlockSpec((8, 96, 128), lambda i: (i, 0, 0))] * 2,
        out_shape=[shape((NX * NZ, 96, 128))] * 2,
        cost_estimate=cost(2 * 16 * 384 * 384 * 128, 3 * MIB),
        compiler_params=params(),
        name="split_out",
    )(where, mine, in_hbm(theirs), after)


def split_down_kernel(where_ref, mine_ref, theirs_ref, after_ref, *out_refs):
    core = where_ref[0]
    row = lax.broadcasted_iota(jnp.int32, (384, 256), 0)
    lane = lax.broadcasted_iota(jnp.int32, (384, 256), 1)
    pick = one_hot((row == lane // 128 * 192 + lane % 128 + core * 96) & (lane % 128 < 96))
    for part in range(4):
        for weight_ref, out_ref in zip((mine_ref, theirs_ref), out_refs):
            weight = weight_ref[:, part * 384 : part * 384 + 384]
            total = jnp.dot(weight, pick, preferred_element_type=F32)
            out_ref[:, part * 256 : part * 256 + 256] = total.astype(BF16)


def split_down(where, mine, theirs, after):
    hidden = mine.shape[0]
    return pl.pallas_call(
        split_down_kernel,
        grid=(4,),
        in_specs=[smem_spec()] + [pl.BlockSpec((hidden, 1536), lambda i: (0, i))] * 2 + [any_spec()],
        out_specs=[pl.BlockSpec((hidden, 1024), lambda i: (0, i))] * 2,
        out_shape=[shape((hidden, NX * NZ * 128))] * 2,
        cost_estimate=cost(2 * 16 * 384 * 512 * 144, 4 * MIB),
        compiler_params=params(),
        name="split_down",
    )(where, mine, in_hbm(theirs), after)


def project_kernel(keep_ref, other_ref, mine_ref, theirs_ref, out_ref):
    blocks = keep_ref.shape[0]
    mine, theirs = mine_ref[:64], theirs_ref[:64]
    total = nt_dot(keep_ref[...].reshape(blocks * 96, 128), jnp.concatenate([mine, mine], 0))
    total += nt_dot(other_ref[...].reshape(blocks * 96, 128), jnp.concatenate([theirs, theirs], 0))
    total = total.reshape(blocks, 96, 128)
    left = lax.broadcasted_iota(jnp.int32, (blocks, 48, 128), 2) < 64
    out_ref[...] = jnp.where(left, total[:, :48], total[:, 48:]).astype(BF16)


def project(keep, other, mine, theirs):
    block = 8
    weights = pl.BlockSpec((block, 96, 128), lambda i: (i, 0, 0))
    tokens = pl.BlockSpec((192, 128), lambda i: (0, 0))
    return pl.pallas_call(
        project_kernel,
        grid=(NX * NZ // block,),
        in_specs=[weights, weights, tokens, tokens],
        out_specs=pl.BlockSpec((block, 48, 128), lambda i: (i, 0, 0)),
        out_shape=shape((NX * NZ, 48, 128)),
        cost_estimate=cost(2 * 3072 * 256 * 128, 2 * MIB),
        compiler_params=params(),
        name="project",
    )(keep, other, mine, theirs)


def project_rest_kernel(where_ref, keep_ref, other_ref, mine_ref, theirs_ref, after_ref, *out_refs):
    for far, out_ref in enumerate(out_refs):
        start = lax.rem(where_ref[1] + far, NX) * NZ
        total = nt_dot(keep_ref[pl.ds(start, NZ)].reshape(NZ * 96, 128), mine_ref[64:])
        total += nt_dot(other_ref[pl.ds(start, NZ)].reshape(NZ * 96, 128), theirs_ref[64:])
        out_ref[...] = total.astype(BF16).reshape(NZ, 96, 128)


def project_rest(where, keep, other, mine, theirs, after):
    return pl.pallas_call(
        project_rest_kernel,
        in_specs=[smem_spec()] + [vmem_spec()] * 4 + [any_spec()],
        out_specs=[vmem_spec()] * NX,
        out_shape=[shape((NZ, 96, 128))] * NX,
        cost_estimate=cost(2 * 3072 * 256 * 128, 3 * MIB),
        compiler_params=params(),
        name="project_rest",
    )(where, keep, other, mine, theirs, after)


def add_rest_kernel(*refs):
    in_refs, out_ref = refs[:-1], refs[-1]
    blank = jnp.zeros((32, 128), F32)
    for block in range(NZ):
        total = sum(in_ref[block].astype(F32) for in_ref in in_refs)
        total = jnp.concatenate([total, blank], 0).T
        out_ref[:, block] = total.astype(BF16).reshape(4, 32, 128)


def add_rest(parts):
    return pl.pallas_call(
        add_rest_kernel,
        in_specs=[vmem_spec()] * NX,
        out_specs=vmem_spec(),
        out_shape=shape((4, NZ, 32, 128)),
        cost_estimate=cost(MIB, MIB),
        compiler_params=params(),
        name="add_rest",
    )(*parts)


def residual_kernel(in_ref, hidden_ref, one_ref, two_ref, three_ref, send_ref):
    routed = (jnp.sum(in_ref[...].astype(F32), 0) + hidden_ref[...]).astype(BF16)
    for copy in range(send_ref.shape[0]):
        send_ref[copy] = routed


def routed_residual(parts, hidden, *after):
    return pl.pallas_call(
        residual_kernel,
        in_specs=[vmem_spec()] * 2 + [any_spec()] * 3,
        out_specs=vmem_spec(),
        out_shape=shape((NX * NZ, 48, 128)),
        cost_estimate=cost(MIB, MIB),
        compiler_params=params(),
        name="routed_residual",
    )(parts, hidden, *after)


def up_kernel(where_ref, mine_ref, theirs_ref, weight_ref, out_ref, total_ref, square_ref):
    index = pl.program_id(0)
    even = where_ref[0] == 0
    blocks = mine_ref.shape[0]
    mine, theirs = mine_ref[...], theirs_ref[...]
    first = jnp.where(even, mine, theirs)
    second = jnp.where(even, theirs, mine)
    left = lax.broadcasted_iota(jnp.int32, (48, 128), 1) < 64
    zero = jnp.zeros((48, 128), BF16)
    pieces = []
    for block in range(blocks):
        for part in (first, second):
            pieces += [jnp.where(left, part[block], zero), jnp.where(left, zero, part[block])]
    tokens = jnp.concatenate(pieces, 0)

    @pl.when(index == 0)
    def _():
        total_ref[...] = jnp.zeros_like(total_ref)
        square_ref[...] = jnp.zeros_like(square_ref)

    total_ref[...] += jnp.dot(weight_ref[...], tokens, preferred_element_type=F32)
    wide = tokens.astype(F32)
    square_ref[...] += jnp.sum((wide * wide).reshape(-1, 8, 128), 0)

    @pl.when(index == pl.num_programs(0) - 1)
    def _():
        total, square = total_ref[...], jnp.sum(square_ref[...], 0, keepdims=True)
        total = total[:, :64] + total[:, 64:]
        square = square[:, :64] + square[:, 64:]
        total = total * lax.rsqrt(square / 6144.0 + EPSILON_NORM)
        half = total.shape[0] // 2
        out_ref[...] = (silu(total[:half]) * total[half:]).astype(BF16)


def up_project(where, mine, theirs, weight):
    rows, width = weight.shape
    steps = 4
    tokens = pl.BlockSpec((32 // steps, 48, 128), lambda i: (i, 0, 0))
    return pl.pallas_call(
        up_kernel,
        grid=(steps,),
        in_specs=[smem_spec(), tokens, tokens, pl.BlockSpec((rows, width // steps), lambda i: (0, i))],
        out_specs=pl.BlockSpec((rows // 2, 64), lambda i: (0, 0)),
        out_shape=shape((rows // 2, 64)),
        scratch_shapes=[pltpu.VMEM((rows, 128), F32), pltpu.VMEM((8, 128), F32)],
        cost_estimate=cost(2 * 288 * 6144 * 128, 5 * MIB),
        compiler_params=params(),
        name="up_project",
    )(where, mine, theirs, in_hbm(weight))


def down_kernel(mine_ref, theirs_ref, keep_ref, other_ref, after_ref, out_ref):
    total = tn_dot(mine_ref[...], keep_ref[...]) + tn_dot(theirs_ref[...], other_ref[...])
    total = total.astype(BF16)
    for block in range(NZ):
        out_ref[0, block] = total[:, block * 128 : block * 128 + 128].reshape(4, 16, 128)


def down_project(mine, theirs, keep, other, after):
    hidden = mine.shape[0]
    tokens = pl.BlockSpec((hidden, 64), lambda i: (0, 0))
    weights = pl.BlockSpec((hidden, NZ * 128), lambda i: (0, i))
    return pl.pallas_call(
        down_kernel,
        grid=(NX,),
        in_specs=[tokens, tokens, weights, weights, any_spec()],
        out_specs=pl.BlockSpec((1, NZ, 4, 16, 128), lambda i: (i, 0, 0, 0, 0)),
        out_shape=shape((NX, NZ, 4, 16, 128)),
        cost_estimate=cost(2 * 288 * 4096 * 64, 3 * MIB),
        compiler_params=params(),
        name="down_project",
    )(mine, theirs, keep, other, after)


def merge_kernel(parts_ref, rest_ref, out_ref):
    out_ref[:, :, :32] = rest_ref[...]
    for block in range(NZ):
        out_ref[:, block, 32:] = jnp.sum(parts_ref[:, block].astype(F32), 0).astype(BF16)


def merge(parts, rest):
    return pl.pallas_call(
        merge_kernel,
        in_specs=[vmem_spec()] * 2,
        out_specs=vmem_spec(),
        out_shape=shape((4, NZ, 48, 128)),
        cost_estimate=cost(MIB, MIB),
        compiler_params=params(),
        name="merge",
    )(parts, rest)


def combine_kernel(parts_ref, place_ref, weight_ref, hidden_ref, out_ref):
    parts = jnp.sum(parts_ref[...].astype(F32), 1)
    residual = hidden_ref[...].astype(F32) + parts[:, :32].reshape(128, 128)
    result = parts[:, 32:].astype(BF16).reshape(64, 128)
    fetched = jnp.dot(place_ref[:, :64], result, preferred_element_type=F32)
    out_ref[...] = (residual + weight_ref[...] * fetched)[:, :96].astype(BF16)


def combine(parts, place, weight, hidden):
    return pl.pallas_call(
        combine_kernel,
        in_specs=[vmem_spec()] * 4,
        out_specs=vmem_spec(),
        out_shape=shape((128, 96)),
        cost_estimate=cost(MIB, MIB),
        compiler_params=params(),
        name="combine",
    )(parts, place, weight, hidden)


def swap(value):
    return lax.ppermute(value, "core", [(0, 1), (1, 0)])


def shifted(blocks, axis):
    count = len(blocks)
    return [blocks[0]] + [
        lax.ppermute(blocks[far], axis, [(i, (i + far) % count) for i in range(count)]) for far in range(1, count)
    ]


def per_device(
    unfinished, states, qkv_rows, decay_rate, out_weight, hidden_in, routes, route_weight, expert_up, expert_down
):
    where = jnp.stack([lax.axis_index("core").astype(jnp.int32), lax.axis_index("x").astype(jnp.int32)])

    with jax.named_scope("attention"):
        local = attend(states[0], qkv_rows[0].transpose(0, 2, 1, 3))
        parts = lax.all_to_all(local, HEAD, 0, 0, tiled=True)
    with jax.named_scope("weights"):
        keep_out, other_out = split_out(where, out_weight, swap(out_weight), local)
    with jax.named_scope("routing"):
        hidden = jnp.pad(hidden_in.transpose(1, 2, 0).reshape(128, 96), ((0, 0), (0, 32)))
        slots = jnp.repeat(unfinished, 4)[:, None]
        place, weight, facts = route(routes.reshape(128, 2), route_weight.reshape(128, 2), hidden, slots)
    with jax.named_scope("heads"):
        head_out = decay_heads(decay_rate, parts, facts, keep_out)
        head_rows = lax.all_to_all(head_out, "dp", 0, 0, tiled=True)
        mine, routed_hidden = select(head_rows.reshape(-1, 128))
        theirs = swap(mine)
    with jax.named_scope("projection"):
        partial = project(keep_out, other_out, mine, theirs)
        summed = lax.all_to_all(partial, ("x", "z"), 0, 0, tiled=True)
        keep_down, other_down = split_down(where, expert_down[0], swap(expert_down[0]), partial)
        rest = project_rest(where, keep_out, other_out, mine, theirs, partial)
        rest = shifted(rest, "x")
        routed = routed_residual(summed, routed_hidden, rest[1], rest[3], keep_down)
    with jax.named_scope("expert"):
        features = lax.all_to_all(routed, ("x", "z"), 0, 0, tiled=True)
        up = expert_up[0].transpose(1, 2, 0).reshape(288, 6144)
        expert_hidden = up_project(where, features, swap(features), up)
        results = down_project(expert_hidden, swap(expert_hidden), keep_down, other_down, rest[2])
        rest = add_rest(rest)
        over_x = lax.all_to_all(results, "x", 0, 0, tiled=True)
        merged = merge(over_x, rest).reshape(32, 48, 128)
        returned = lax.all_to_all(merged, ("dp", "z"), 0, 0, tiled=True)
    with jax.named_scope("output"):
        mixed = combine(returned.reshape(4, NZ, 48, 128), place, weight, hidden)
        return mixed.reshape(32, 4, 96).transpose(2, 0, 1)


def solution(mesh):
    grid = Mesh(mesh.devices.reshape(mesh.shape["dp"], NX, NZ, NC), EVERY)
    return jax.shard_map(
        per_device,
        mesh=grid,
        in_specs=(
            P("dp"),
            P(EVERY, None, None, None),
            P(EVERY, None, None, None, None),
            P(HEAD),
            P(HEAD, None),
            P(HEAD, "dp", None),
            P("dp", None, None),
            P("dp", None, None),
            P("dp", None, None, HEAD),
            P("dp", HEAD, None),
        ),
        out_specs=P(HEAD, "dp", None),
        check_vma=False,
    )
```

time: 154 us -> 130 us (0.84)
  blocking collectives: 16.4 us -> 49.8 us
  waiting for transfers between devices: 53.7 us -> 22.3 us
  starting transfers between devices: 42.3 us -> 27.2 us
  local copies, waits for them, and re-layouts: 8.24 us -> 2.98 us
  other arithmetic: 2.67 us -> 0.08 us
  matrix products: 2.09 us -> 0 us
    all_to_all x6 -> x3, waiting for transfers between devices: 49.7 us -> 14.4 us  [the longest x1 8.01 us: per_device(): over_x = lax.all_to_all(results, 'x', 0, 0, tiled=True)]
    all_to_all x1 -> x3, blocking collectives: 16.4 us -> 49.8 us  [the longest x1 20.2 us: per_device(): features = lax.all_to_all(routed, ('x', 'z'), 0, 0, tiled=True)]
    all_to_all x6 -> x3, starting transfers between devices: 41.7 us -> 22.8 us  [the longest x1 12 us: per_device(): parts = lax.all_to_all(local, HEAD, 0, 0, tiled=True)]
    unnamed x21 -> x36, local copies, waits for them, and re-layouts: 6.72 us -> 2.82 us
    ppermute x5 -> x8, waiting for transfers between devices: 4.02 us -> 7.9 us  [the longest x3 6.46 us: shifted(): lax.ppermute(blocks[far], axis, [(i, (i + far) % count) for i in range(co...]
    ppermute x5 -> x8, starting transfers between devices: 0.56 us -> 4.36 us  [the longest x3 3.62 us: shifted(): lax.ppermute(blocks[far], axis, [(i, (i + far) % count) for i in range(co...]
    pallas_call x8 -> x12, Pallas kernels: 22.3 us -> 20 us  [the longest x1 4.14 us: up_project(): pl.pallas_call(up_kernel, grid=(steps,), in_specs=[smem_spec(), tokens, t...]
    dot_general x3 -> x0, matrix products: 2.09 us -> none  [the longest x1 1.62 us: per_device(): lax.dot_general(place, facts, (((0,), (0,)), ((), ())), preferred_element...]
  transfers between devices with their start and end apart: 11 -> 11, of which waited for: 8 -> 8; matrix products, arithmetic and copies ran while one was open for 4% -> 0% of each run, Pallas kernels for 13% -> 16%
where the time goes in v2:
time: 130 us; the launch traced here: 128 us
  blocking collectives  49.8 us (38%)
  starting transfers between devices  27.2 us (21%)
  Pallas kernels  24.7 us (19%)
  waiting for transfers between devices  22.3 us (17%)
  local copies, waits for them, and re-layouts  2.98 us (2%)
    all_to_all x1, blocking collectives, per_device(): features = lax.all_to_all(routed, ('x', 'z'), 0, 0, tiled=True)  20.2 us
    all_to_all x1, blocking collectives, per_device(): returned = lax.all_to_all(merged, ('dp', 'z'), 0, 0, tiled=True)  18.2 us
    all_to_all x1, starting transfers between devices, per_device(): parts = lax.all_to_all(local, HEAD, 0, 0, tiled=True)  12 us
    all_to_all x1, blocking collectives, per_device(): head_rows = lax.all_to_all(head_out, 'dp', 0, 0, tiled=True)  11.5 us
    all_to_all x1, waiting for transfers between devices, per_device(): over_x = lax.all_to_all(results, 'x', 0, 0, tiled=True)  8.01 us
    ppermute x3, waiting for transfers between devices, shifted(): lax.ppermute(blocks[far], axis, [(i, (i + far) % count) for i in range(co...  6.46 us
    all_to_all x1, starting transfers between devices, per_device(): summed = lax.all_to_all(partial, ('x', 'z'), 0, 0, tiled=True)  5.97 us
    all_to_all x1, starting transfers between devices, per_device(): over_x = lax.all_to_all(results, 'x', 0, 0, tiled=True)  4.84 us
  transfers between devices with their start and end apart: 11, of which 8 were waited for; matrix products, arithmetic and copies ran while one was open for 0% of the time, Pallas kernels for 16%

profile of v2, /device:TPU:2, one launch (start us, length us, event | category | flops | bytes accessed | tf_op | source)
XLA Modules:
  0.0 128.0 jit_solution(13497466183177796817)
XLA Ops:
  0.0 0.0 collective-permute-start
  0.0 0.5 collective-permute-start.4
  0.5 0.9 copy-done.4
  1.5 3.9 %attend.1.after_ref = bf16[64,3,4,128]{3,2,1,0:T(4,128)(2,1)} custom-call(bf16[64,128,128]{2,1,0:T(8,128)(2,1)} %bitcast.32, bf16[64,3,4,128]{3,2,1,0:T(4,128)(2,1)S(1)} %bitcast.30), custom_call_target="tpu_custom_call" | custom-call | flops 16777216 | bytes 3145728 | tf_op jit(solution)/shard_map/attention/attend/pallas_call | solution.py:85
  5.4 12.0 %all-to-all-start = ((bf16[64,3,4,128]{3,2,1,0:T(4,128)(2,1)}), bf16[64,3,4,128]{3,2,1,0:T(4,128)(2,1)S(1)}, u32[]{:S(2)}, u32[]{:S(2)}) async-start(bf16[64,3,4,128]{3,2,1,0:T(4,128)(2,1)} %attend.1.after_ref), calls=%async_computation | async-start | bytes 393216 | tf_op jit(solution)/shard_map/attention/all_to_all | solution.py:462
  17.4 0.0 copy-done.16
  17.4 0.1 broadcast_in_dim.3
  17.5 0.1 reshape.36.row_ref
  17.6 0.0 copy-done.14
  17.6 0.1 copy.14
  17.7 0.0 copy-done.15
  17.7 0.1 copy.15
  18.5 0.0 copy-done.13
  18.5 0.6 route.1
  19.1 0.0 copy-start.7
  19.1 0.1 pad_add_fusion.where_ref
  19.2 0.0 collective-permute-done.theirs_ref
  19.2 0.0 copy-done.1
  19.2 3.7 %split_out.1 = (bf16[32,96,128]{2,1,0:T(8,128)(2,1)S(1)}, bf16[32,96,128]{2,1,0:T(8,128)(2,1)S(1)}) custom-call(s32[2]{0:T(128)S(1)} %pad_add_fusion.where_ref, bf16[128,6144]{1,0:T(8,128)(2,1)S(1)} %copy-done.1, bf16[128,6144]{1,0:T(8,128)(2,1)} %collective-permute-done.theirs_ref, bf16[64,3,4,128]{3,2,1,0:T(4,128)(2,1)} %attend.1.after_ref), custom_call_target="tpu_custom_call" | custom-call | flops 603979776 | bytes 3145728 | tf_op jit(solution)/shard_map/weights/split_out/pallas_call | solution.py:209
  22.9 4.8 %all-to-all-done.parts_ref = bf16[64,3,4,128]{3,2,1,0:T(4,128)(2,1)S(1)} async-done(((bf16[64,3,4,128]{3,2,1,0:T(4,128)(2,1)}), bf16[64,3,4,128]{3,2,1,0:T(4,128)(2,1)S(1)}, u32[]{:S(2)}, u32[]{:S(2)}) %all-to-all-start) | async-done | bytes 196640 | tf_op jit(solution)/shard_map/attention/all_to_all | solution.py:462
  27.6 0.5 decay_heads.1
  28.2 0.0 copy-done.7
  28.2 11.5 %all_to_all.30 = bf16[4,68,4,128]{3,2,1,0:T(4,128)(2,1)S(1)} all-to-all(bf16[4,68,4,128]{3,2,1,0:T(4,128)(2,1)S(1)} %decay_heads.1), channel_id=1, replica_groups=mesh['dp'=4,'x'=4,'z'=8,'core'=2] {'dp'}, dimensions={0} | all-to-all | bytes 557056 | tf_op jit(solution)/shard_map/heads/all_to_all | solution.py:471
  39.7 0.5 select.2
  40.2 0.0 copy-start.9
  40.2 0.6 copy-done.9
  40.8 0.0 collective-permute-start.1
  40.8 1.2 collective-permute-done.1.theirs_ref
  42.0 2.1 %project.1.after_ref = bf16[32,48,128]{2,1,0:T(8,128)(2,1)} custom-call(bf16[32,96,128]{2,1,0:T(8,128)(2,1)S(1)} %get-tuple-element.18.after_ref.keep_ref, bf16[32,96,128]{2,1,0:T(8,128)(2,1)S(1)} %get-tuple-element.19.other_ref, bf16[192,128]{1,0:T(8,128)(2,1)S(1)} %get-tuple-element.21.mine_ref, bf16[192,128]{1,0:T(8,128)(2,1)S(1)} %collective-permute-done.1.theirs_ref), custom_call_target="tpu_custom_call" | custom-call | flops 201326592 | bytes 2097152 | tf_op jit(solution)/shard_map/projection/project/pallas_call | solution.py:261
  44.1 6.0 %all-to-all-start.2 = ((bf16[32,48,128]{2,1,0:T(8,128)(2,1)}), bf16[32,48,128]{2,1,0:T(8,128)(2,1)}, u32[]{:S(2)}, u32[]{:S(2)}) async-start(bf16[32,48,128]{2,1,0:T(8,128)(2,1)} %project.1.after_ref), calls=%async_computation.2 | async-start | bytes 786432 | tf_op jit(solution)/shard_map/projection/all_to_all | solution.py:476
  50.1 1.1 project_rest.1
  51.2 0.0 copy-start.5
  51.2 0.0 copy-start.11
  51.2 1.6 %collective-permute-start.2 = (bf16[8,96,128]{2,1,0:T(8,128)(2,1)S(1)}, bf16[8,96,128]{2,1,0:T(8,128)(2,1)S(1)}, u32[]{:S(2)}, u32[]{:S(2)}) collective-permute-start(bf16[8,96,128]{2,1,0:T(8,128)(2,1)S(1)} %get-tuple-element.23), channel_id=1, source_target_pairs={{0,16},{16,32},{32,48},{48,0},{1,17},{17,33},{33,49},{49,1},{2,18}... | collective-permute-start | bytes 589832 | tf_op jit(solution)/shard_map/projection/ppermute | solution.py:451
  52.8 0.6 collective-permute-start.3
  53.3 0.0 collective-permute-done.4.theirs_ref
  53.3 0.0 copy-done
  53.3 3.8 %split_down.1 = (bf16[144,4096]{1,0:T(8,128)(2,1)S(1)}, bf16[144,4096]{1,0:T(8,128)(2,1)S(1)}) custom-call(s32[2]{0:T(128)S(1)} %pad_add_fusion.where_ref, bf16[144,6144]{1,0:T(8,128)(2,1)S(1)} %bitcast.24, bf16[144,6144]{1,0:T(8,128)(2,1)} %collective-permute-done.4.theirs_ref, bf16[32,48,128]{2,1,0:T(8,128)(2,1)} %project.1.after_ref), custom_call_target="tpu_custom_call" | custom-call | flops 905969664 | bytes 4194304 | tf_op jit(solution)/shard_map/projection/split_down/pallas_call | solution.py:235
  57.1 0.0 copy-done.5
  57.1 0.0 copy-done.11
  57.1 0.0 copy-start.2
  57.1 1.0 copy-done.2
  58.2 2.3 %collective-permute-done.2.one_ref.refs_1_ = bf16[8,96,128]{2,1,0:T(8,128)(2,1)S(1)} collective-permute-done((bf16[8,96,128]{2,1,0:T(8,128)(2,1)S(1)}, bf16[8,96,128]{2,1,0:T(8,128)(2,1)S(1)}, u32[]{:S(2)}, u32[]{:S(2)}) %collective-permute-start.2) | collective-permute-done | bytes 196640 | tf_op jit(solution)/shard_map/projection/ppermute | solution.py:451
  60.5 1.4 %collective-permute-done.3.two_ref.refs_3_ = bf16[8,96,128]{2,1,0:T(8,128)(2,1)S(1)} collective-permute-done((bf16[8,96,128]{2,1,0:T(8,128)(2,1)S(1)}, bf16[8,96,128]{2,1,0:T(8,128)(2,1)S(1)}, u32[]{:S(2)}, u32[]{:S(2)}) %collective-permute-start.3) | collective-permute-done | bytes 196640 | tf_op jit(solution)/shard_map/projection/ppermute | solution.py:451
  61.9 1.6 %all-to-all-done.2.in_ref = bf16[32,48,128]{2,1,0:T(8,128)(2,1)} async-done(((bf16[32,48,128]{2,1,0:T(8,128)(2,1)}), bf16[32,48,128]{2,1,0:T(8,128)(2,1)}, u32[]{:S(2)}, u32[]{:S(2)}) %all-to-all-start.2) | async-done | bytes 393248 | tf_op jit(solution)/shard_map/projection/all_to_all | solution.py:476
  63.5 0.0 copy-done.10
  63.5 1.1 routed_residual.1
  64.6 20.2 %all_to_all.31.mine_ref = bf16[32,48,128]{2,1,0:T(8,128)(2,1)S(1)} all-to-all(bf16[32,48,128]{2,1,0:T(8,128)(2,1)S(1)} %routed_residual.1), channel_id=1, replica_groups=mesh['dp'=4,'x'=4,'z'=8,'core'=2] {'x','z'}, dimensions={0} | all-to-all | bytes 786432 | tf_op jit(solution)/shard_map/expert/all_to_all | solution.py:482
  84.8 0.0 collective-permute-start.5
  84.8 1.5 %collective-permute-start.7 = (bf16[8,96,128]{2,1,0:T(8,128)(2,1)S(1)}, bf16[8,96,128]{2,1,0:T(8,128)(2,1)S(1)}, u32[]{:S(2)}, u32[]{:S(2)}) collective-permute-start(bf16[8,96,128]{2,1,0:T(8,128)(2,1)S(1)} %copy-done.12), channel_id=1, source_target_pairs={{0,32},{16,48},{32,0},{48,16},{1,33},{17,49},{33,1},{49,17},{2,34}... | collective-permute-start | bytes 589832 | tf_op jit(solution)/shard_map/projection/ppermute | solution.py:451
  86.3 0.2 collective-permute-done.5.theirs_ref
  86.5 4.1 %up_project.1.mine_ref = bf16[144,64]{1,0:T(8,128)(2,1)S(1)} custom-call(s32[2]{0:T(128)S(1)} %pad_add_fusion.where_ref, bf16[32,48,128]{2,1,0:T(8,128)(2,1)S(1)} %all_to_all.31.mine_ref, bf16[32,48,128]{2,1,0:T(8,128)(2,1)S(1)} %collective-permute-done.5.theirs_ref, bf16[288,6144]{1,0:T(8,128)(2,1)} %bitcast.31), custom_call_target="tpu_custom_call" | custom-call | flops 452984832 | bytes 5242880 | tf_op jit(solution)/shard_map/expert/up_project/pallas_call | solution.py:370
  90.7 0.2 collective-permute-start.6
  90.9 2.7 %collective-permute-done.7.after_ref.refs_2_ = bf16[8,96,128]{2,1,0:T(8,128)(2,1)S(1)} collective-permute-done((bf16[8,96,128]{2,1,0:T(8,128)(2,1)S(1)}, bf16[8,96,128]{2,1,0:T(8,128)(2,1)S(1)}, u32[]{:S(2)}, u32[]{:S(2)}) %collective-permute-start.7) | collective-permute-done | bytes 196640 | tf_op jit(solution)/shard_map/projection/ppermute | solution.py:451
  93.6 0.0 collective-permute-done.6.theirs_ref
  93.6 0.0 copy-done.3
  93.6 2.3 %down_project.1 = bf16[4,8,4,16,128]{4,3,2,1,0:T(8,128)(2,1)} custom-call(bf16[144,64]{1,0:T(8,128)(2,1)S(1)} %up_project.1.mine_ref, bf16[144,64]{1,0:T(8,128)(2,1)S(1)} %collective-permute-done.6.theirs_ref, bf16[144,4096]{1,0:T(8,128)(2,1)S(1)} %get-tuple-element.25.three_ref.keep_ref, bf16[144,4096]{1,0:T(8,128)(2,1)S(1)} %copy-done.3, ...), custom_call_target="tpu_custom_call" | custom-call | flops 150994944 | bytes 3145728 | tf_op jit(solution)/shard_map/expert/down_project/pallas_call | solution.py:394
  95.9 4.8 %all-to-all-start.4 = ((bf16[4,8,4,16,128]{4,3,2,1,0:T(8,128)(2,1)}), bf16[4,8,4,16,128]{4,3,2,1,0:T(8,128)(2,1)S(1)}, u32[]{:S(2)}, u32[]{:S(2)}) async-start(bf16[4,8,4,16,128]{4,3,2,1,0:T(8,128)(2,1)} %down_project.1), calls=%async_computation.4 | async-start | bytes 1048576 | tf_op jit(solution)/shard_map/expert/all_to_all | solution.py:487
  100.8 0.0 copy-done.6
  100.8 0.2 add_rest.1.rest_ref
  100.9 8.0 %all-to-all-done.4.parts_ref = bf16[4,8,4,16,128]{4,3,2,1,0:T(8,128)(2,1)S(1)} async-done(((bf16[4,8,4,16,128]{4,3,2,1,0:T(8,128)(2,1)}), bf16[4,8,4,16,128]{4,3,2,1,0:T(8,128)(2,1)S(1)}, u32[]{:S(2)}, u32[]{:S(2)}) %all-to-all-start.4) | async-done | bytes 524320 | tf_op jit(solution)/shard_map/expert/all_to_all | solution.py:487
  108.9 0.1 merge.1
  109.0 18.2 %all_to_all.32 = bf16[32,48,128]{2,1,0:T(8,128)(2,1)S(1)} all-to-all(bf16[32,48,128]{2,1,0:T(8,128)(2,1)S(1)} %bitcast.26), channel_id=1, replica_groups=mesh['dp'=4,'x'=4,'z'=8,'core'=2] {'dp','z'}, dimensions={0} | all-to-all | bytes 786432 | tf_op jit(solution)/shard_map/expert/all_to_all | solution.py:489
  127.2 0.8 combine.1
  (15 shorter events, 0.0 us)
Async XLA Ops:
  0.0 19.2 %copy-start.1 = (bf16[128,6144]{1,0:T(8,128)(2,1)S(1)}, bf16[128,6144]{1,0:T(8,128)(2,1)}, u32[]{:S(2)}) copy-start(bf16[128,6144]{1,0:T(8,128)(2,1)} %mine_ref.1) | copy-start | bytes 4718596
  0.0 19.2 %collective-permute-start = (bf16[128,6144]{1,0:T(8,128)(2,1)}, bf16[128,6144]{1,0:T(8,128)(2,1)}, u32[]{:S(2)}, u32[]{:S(2)}) collective-permute-start(bf16[128,6144]{1,0:T(8,128)(2,1)} %mine_ref.1), channel_id=1, source_target_pairs={{0,1},{1,0},{2,3},{3,2},{4,5},{5,4},{6,7},{7,6},{8,9},{9,8},{10,11... | collective-permute-start | bytes 4718600 | tf_op jit(solution)/shard_map/weights/ppermute | solution.py:445
  0.0 53.3 %collective-permute-start.4 = (bf16[144,6144]{1,0:T(8,128)(2,1)}, bf16[144,6144]{1,0:T(8,128)(2,1)}, u32[]{:S(2)}, u32[]{:S(2)}) collective-permute-start(bf16[144,6144]{1,0:T(8,128)(2,1)} %bitcast.23), channel_id=1, source_target_pairs={{0,1},{1,0},{2,3},{3,2},{4,5},{5,4},{6,7},{7,6},{8,9},{9,8},{10,11... | collective-permute-start | bytes 5308424 | tf_op jit(solution)/shard_map/projection/ppermute | solution.py:445
  0.5 0.9 copy-start.4
  1.4 16.0 %copy-start.16 = (s32[32]{0:T(128)S(1)}, s32[32]{0:T(128)}, u32[]{:S(2)}) copy-start(s32[32]{0:T(128)} %param.10) | copy-start | bytes 388
  1.4 16.1 %copy-start.14 = (s32[32,4,2]{0,2,1:T(2,128)S(1)}, s32[32,4,2]{0,2,1:T(2,128)}, u32[]{:S(2)}) copy-start(s32[32,4,2]{0,2,1:T(2,128)} %param.16) | copy-start | bytes 3076
  1.4 16.3 %copy-start.15 = (f32[32,4,2]{0,2,1:T(2,128)S(1)}, f32[32,4,2]{0,2,1:T(2,128)}, u32[]{:S(2)}) copy-start(f32[32,4,2]{0,2,1:T(2,128)} %param.17) | copy-start | bytes 3076
  1.4 17.0 %copy-start.13 = (bf16[96,32,4]{0,2,1:T(4,128)(2,1)S(1)}, bf16[96,32,4]{0,2,1:T(4,128)(2,1)}, u32[]{:S(2)}) copy-start(bf16[96,32,4]{0,2,1:T(4,128)(2,1)} %param.15) | copy-start | bytes 73732
  5.4 22.3 %all-to-all-start = ((bf16[64,3,4,128]{3,2,1,0:T(4,128)(2,1)}), bf16[64,3,4,128]{3,2,1,0:T(4,128)(2,1)S(1)}, u32[]{:S(2)}, u32[]{:S(2)}) async-start(bf16[64,3,4,128]{3,2,1,0:T(4,128)(2,1)} %attend.1.after_ref), calls=%async_computation | async-start | bytes 393216 | tf_op jit(solution)/shard_map/attention/all_to_all | solution.py:462
  19.1 9.1 %copy-start.7 = (bf16[128,128]{1,0:T(8,128)(2,1)}, bf16[128,128]{1,0:T(8,128)(2,1)S(1)}, u32[]{:S(2)}) copy-start(bf16[128,128]{1,0:T(8,128)(2,1)S(1)} %get-tuple-element.29.place_ref) | copy-start | bytes 98308
  40.2 0.6 copy-start.9
  40.8 1.2 collective-permute-start.1
  44.1 9.2 %copy-start = (bf16[1,144,6144]{2,1,0:T(8,128)(2,1)S(1)}, bf16[1,144,6144]{2,1,0:T(8,128)(2,1)}, u32[]{:S(2)}) copy-start(bf16[1,144,6144]{2,1,0:T(8,128)(2,1)} %param.19) | copy-start | bytes 5308420
  44.1 19.4 %all-to-all-start.2 = ((bf16[32,48,128]{2,1,0:T(8,128)(2,1)}), bf16[32,48,128]{2,1,0:T(8,128)(2,1)}, u32[]{:S(2)}, u32[]{:S(2)}) async-start(bf16[32,48,128]{2,1,0:T(8,128)(2,1)} %project.1.after_ref), calls=%async_computation.2 | async-start | bytes 786432 | tf_op jit(solution)/shard_map/projection/all_to_all | solution.py:476
  51.2 5.9 %copy-start.5 = (bf16[8,96,128]{2,1,0:T(8,128)(2,1)}, bf16[8,96,128]{2,1,0:T(8,128)(2,1)S(1)}, u32[]{:S(2)}) copy-start(bf16[8,96,128]{2,1,0:T(8,128)(2,1)S(1)} %get-tuple-element.28.refs_0_) | copy-start | bytes 589828
  51.2 5.9 %copy-start.11 = (bf16[8,96,128]{2,1,0:T(8,128)(2,1)}, bf16[8,96,128]{2,1,0:T(8,128)(2,1)S(1)}, u32[]{:S(2)}) copy-start(bf16[8,96,128]{2,1,0:T(8,128)(2,1)S(1)} %get-tuple-element.27) | copy-start | bytes 589828
  51.2 9.3 %collective-permute-start.2 = (bf16[8,96,128]{2,1,0:T(8,128)(2,1)S(1)}, bf16[8,96,128]{2,1,0:T(8,128)(2,1)S(1)}, u32[]{:S(2)}, u32[]{:S(2)}) collective-permute-start(bf16[8,96,128]{2,1,0:T(8,128)(2,1)S(1)} %get-tuple-element.23), channel_id=1, source_target_pairs={{0,16},{16,32},{32,48},{48,0},{1,17},{17,33},{33,49},{49,1},{2,18}... | collective-permute-start | bytes 589832 | tf_op jit(solution)/shard_map/projection/ppermute | solution.py:451
  52.7 10.8 %copy-start.10 = (f32[48,128]{1,0:T(8,128)S(1)}, f32[48,128]{1,0:T(8,128)}, u32[]{:S(2)}) copy-start(f32[48,128]{1,0:T(8,128)} %copy-done.9) | copy-start | bytes 73732
  52.8 9.1 %collective-permute-start.3 = (bf16[8,96,128]{2,1,0:T(8,128)(2,1)S(1)}, bf16[8,96,128]{2,1,0:T(8,128)(2,1)S(1)}, u32[]{:S(2)}, u32[]{:S(2)}) collective-permute-start(bf16[8,96,128]{2,1,0:T(8,128)(2,1)S(1)} %get-tuple-element.24), channel_id=1, source_target_pairs={{0,48},{16,0},{32,16},{48,32},{1,49},{17,1},{33,17},{49,33},{2,50}... | collective-permute-start | bytes 589832 | tf_op jit(solution)/shard_map/projection/ppermute | solution.py:451
  57.1 1.0 copy-start.2
  60.5 24.3 %copy-start.12 = (bf16[8,96,128]{2,1,0:T(8,128)(2,1)S(1)}, bf16[8,96,128]{2,1,0:T(8,128)(2,1)}, u32[]{:S(2)}) copy-start(bf16[8,96,128]{2,1,0:T(8,128)(2,1)} %copy-done.11) | copy-start | bytes 589828
  84.8 1.7 %collective-permute-start.5 = (bf16[32,48,128]{2,1,0:T(8,128)(2,1)S(1)}, bf16[32,48,128]{2,1,0:T(8,128)(2,1)S(1)}, u32[]{:S(2)}, u32[]{:S(2)}) collective-permute-start(bf16[32,48,128]{2,1,0:T(8,128)(2,1)S(1)} %all_to_all.31.mine_ref), channel_id=1, source_target_pairs={{0,1},{1,0},{2,3},{3,2},{4,5},{5,4},{6,7},{7,6},{8,9},{9,8},{10,11... | collective-permute-start | bytes 1179656 | tf_op jit(solution)/shard_map/expert/ppermute | solution.py:445
  84.8 8.8 %collective-permute-start.7 = (bf16[8,96,128]{2,1,0:T(8,128)(2,1)S(1)}, bf16[8,96,128]{2,1,0:T(8,128)(2,1)S(1)}, u32[]{:S(2)}, u32[]{:S(2)}) collective-permute-start(bf16[8,96,128]{2,1,0:T(8,128)(2,1)S(1)} %copy-done.12), channel_id=1, source_target_pairs={{0,32},{16,48},{32,0},{48,16},{1,33},{17,49},{33,1},{49,17},{2,34}... | collective-permute-start | bytes 589832 | tf_op jit(solution)/shard_map/projection/ppermute | solution.py:451
  86.5 7.1 %copy-start.3 = (bf16[144,4096]{1,0:T(8,128)(2,1)S(1)}, bf16[144,4096]{1,0:T(8,128)(2,1)}, u32[]{:S(2)}) copy-start(bf16[144,4096]{1,0:T(8,128)(2,1)} %copy-done.2) | copy-start | bytes 3538948
  90.7 3.0 %collective-permute-start.6 = (bf16[144,64]{1,0:T(8,128)(2,1)S(1)}, bf16[144,64]{1,0:T(8,128)(2,1)S(1)}, u32[]{:S(2)}, u32[]{:S(2)}) collective-permute-start(bf16[144,64]{1,0:T(8,128)(2,1)S(1)} %up_project.1.mine_ref), channel_id=1, source_target_pairs={{0,1},{1,0},{2,3},{3,2},{4,5},{5,4},{6,7},{7,6},{8,9},{9,8},{10,11... | collective-permute-start | bytes 55304 | tf_op jit(solution)/shard_map/expert/ppermute | solution.py:445
  93.6 7.1 %copy-start.6 = (bf16[8,96,128]{2,1,0:T(8,128)(2,1)S(1)}, bf16[8,96,128]{2,1,0:T(8,128)(2,1)}, u32[]{:S(2)}) copy-start(bf16[8,96,128]{2,1,0:T(8,128)(2,1)} %copy-done.5) | copy-start | bytes 589828
  95.9 13.0 %all-to-all-start.4 = ((bf16[4,8,4,16,128]{4,3,2,1,0:T(8,128)(2,1)}), bf16[4,8,4,16,128]{4,3,2,1,0:T(8,128)(2,1)S(1)}, u32[]{:S(2)}, u32[]{:S(2)}) async-start(bf16[4,8,4,16,128]{4,3,2,1,0:T(8,128)(2,1)} %down_project.1), calls=%async_computation.4 | async-start | bytes 1048576 | tf_op jit(solution)/shard_map/expert/all_to_all | solution.py:487
  100.8 26.4 %copy-start.8 = (bf16[128,128]{1,0:T(8,128)(2,1)S(1)}, bf16[128,128]{1,0:T(8,128)(2,1)}, u32[]{:S(2)}) copy-start(bf16[128,128]{1,0:T(8,128)(2,1)} %copy-done.7) | copy-start | bytes 98308

commit v3 on v2

--- a/solution.py
+++ b/solution.py
@@ -81,7 +81,7 @@
 
 
 def attend(states, inputs):
-    heads, block = states.shape[0], 16
+    heads, block = states.shape[0], 32
     return pl.pallas_call(
         attend_kernel,
         grid=(heads // block,),
@@ -94,10 +94,10 @@
         cost_estimate=cost(2 * 8 * 64 * 128 * 128, 3 * MIB),
         compiler_params=params(),
         name="attend",
-    )(in_hbm(states), inputs)
-
-
-def decay_kernel(rate_ref, parts_ref, facts_ref, after_ref, out_ref):
+    )(in_hbm(states), in_hbm(inputs))
+
+
+def decay_kernel(where_ref, rate_ref, parts_ref, facts_ref, after_ref, *out_refs):
     slots = parts_ref.shape[0]
     rate = jnp.full((4, 128), rate_ref[0], F32)
     step = lax.broadcasted_iota(jnp.int32, (4, 128), 0).astype(F32)
@@ -110,22 +110,22 @@
         attn += (factor * cross[:, :, source : source + 1]) * value[:, source : source + 1]
     scaled = attn * lax.rsqrt(jnp.mean(attn * attn, -1, keepdims=True) + EPSILON_HEAD)
     scaled = scaled.astype(BF16)
-    for group in range(out_ref.shape[0]):
-        out_ref[group, :slots] = scaled
-        out_ref[group, slots:] = facts_ref[group]
-
-
-def decay_heads(rate, parts, facts, after):
+    for far, out_ref in enumerate(out_refs):
+        out_ref[:slots] = scaled
+        out_ref[slots:] = facts_ref[lax.rem(where_ref[2] + far, 4)]
+
+
+def decay_heads(where, rate, parts, facts, after):
     slots = parts.shape[0]
     return pl.pallas_call(
         decay_kernel,
-        in_specs=[smem_spec(), vmem_spec(), vmem_spec(), any_spec()],
-        out_specs=vmem_spec(),
-        out_shape=shape((4, slots + 4, 4, 128)),
+        in_specs=[smem_spec(), smem_spec(), vmem_spec(), vmem_spec(), any_spec()],
+        out_specs=[vmem_spec()] * 4,
+        out_shape=[shape((slots + 4, 4, 128))] * 4,
         cost_estimate=cost(4 * MIB, MIB),
         compiler_params=params(),
         name="decay_heads",
-    )(rate, parts, facts, after)
+    )(where, rate, parts, facts, after)
 
 
 def route_kernel(pair_ref, weight_ref, hidden_ref, row_ref, place_ref, factor_ref, out_ref):
@@ -161,10 +161,14 @@
     )(pair, weight, hidden, row)
 
 
-def select_kernel(rows_ref, out_ref, hidden_ref):
-    span = rows_ref.shape[0] // 4
+def select_kernel(where_ref, *refs):
+    in_refs, (out_ref, hidden_ref, held_ref) = refs[:4], refs[4:]
+    span = held_ref.shape[1]
     steps = span - 16
-    facts = jnp.concatenate([rows_ref[group * span + steps : (group + 1) * span] for group in range(4)], 0)
+    for far, in_ref in enumerate(in_refs):
+        held_ref[lax.rem(where_ref[2] + (4 - far), 4)] = in_ref[...]
+    rows = held_ref[...].reshape(4 * span, 128)
+    facts = held_ref[:, steps:].reshape(64, 128)
     held = facts.astype(F32)
     token = lax.broadcasted_iota(jnp.int32, (128, 64), 0)
     source = lax.broadcasted_iota(jnp.int32, (128, 64), 1)
@@ -175,23 +179,24 @@
     step = jnp.concatenate([held[:, 97:98], step], 0)
     row = (row * 4.0 + step).astype(jnp.int32)
     row = row // steps * span + row % steps
-    lane = lax.broadcasted_iota(jnp.int32, (192, rows_ref.shape[0]), 1)
-    out_ref[...] = jnp.dot(one_hot(lane == row), rows_ref[...], preferred_element_type=F32).astype(BF16)
+    lane = lax.broadcasted_iota(jnp.int32, (192, 4 * span), 1)
+    out_ref[...] = jnp.dot(one_hot(lane == row), rows, preferred_element_type=F32).astype(BF16)
     turned = jnp.concatenate([held, held], 0).T
     left = lax.broadcasted_iota(jnp.int32, (48, 128), 1) < 64
     hidden_ref[...] = jnp.where(left, turned[:48], turned[48:96])
 
 
-def select(rows):
+def select(where, parts):
     return pl.pallas_call(
         select_kernel,
-        in_specs=[vmem_spec()],
+        in_specs=[smem_spec()] + [vmem_spec()] * 4,
         out_specs=[vmem_spec()] * 2,
         out_shape=[shape((192, 128)), shape((48, 128), F32)],
+        scratch_shapes=[pltpu.VMEM((4,) + parts[0].shape, BF16)],
         cost_estimate=cost(2 * 192 * 1088 * 128, MIB),
         compiler_params=params(),
         name="select",
-    )(rows)
+    )(where, *parts)
 
 
 def split_out_kernel(where_ref, mine_ref, theirs_ref, after_ref, *out_refs):
@@ -199,7 +204,7 @@
     row = lax.broadcasted_iota(jnp.int32, (192, 384), 0)
     lane = lax.broadcasted_iota(jnp.int32, (192, 384), 1)
     pick = one_hot(lane == row // 96 * 192 + row % 96 + core * 96)
-    for part in range(4):
+    for part in range(8):
         for weight_ref, out_ref in zip((mine_ref, theirs_ref), out_refs):
             weight = weight_ref[:, part * 384 : part * 384 + 384]
             out_ref[2 * part : 2 * part + 2] = nt_dot(pick, weight).astype(BF16).reshape(2, 96, 128)
@@ -208,9 +213,9 @@
 def split_out(where, mine, theirs, after):
     return pl.pallas_call(
         split_out_kernel,
-        grid=(4,),
-        in_specs=[smem_spec()] + [pl.BlockSpec((128, 1536), lambda i: (0, i))] * 2 + [any_spec()],
-        out_specs=[pl.BlockSpec((8, 96, 128), lambda i: (i, 0, 0))] * 2,
+        grid=(2,),
+        in_specs=[smem_spec()] + [pl.BlockSpec((128, 3072), lambda i: (0, i))] * 2 + [any_spec()],
+        out_specs=[pl.BlockSpec((16, 96, 128), lambda i: (i, 0, 0))] * 2,
         out_shape=[shape((NX * NZ, 96, 128))] * 2,
         cost_estimate=cost(2 * 16 * 384 * 384 * 128, 3 * MIB),
         compiler_params=params(),
@@ -232,11 +237,15 @@
 
 def split_down(where, mine, theirs, after):
     hidden = mine.shape[0]
+    weights = pl.BlockSpec((hidden, 1536), lambda i, where: (0, lax.rem(where[1] + i, NX)))
     return pl.pallas_call(
         split_down_kernel,
-        grid=(4,),
-        in_specs=[smem_spec()] + [pl.BlockSpec((hidden, 1536), lambda i: (0, i))] * 2 + [any_spec()],
-        out_specs=[pl.BlockSpec((hidden, 1024), lambda i: (0, i))] * 2,
+        grid_spec=pltpu.PrefetchScalarGridSpec(
+            num_scalar_prefetch=1,
+            grid=(NX,),
+            in_specs=[weights, weights, any_spec()],
+            out_specs=[pl.BlockSpec((hidden, NZ * 128), lambda i, where: (0, i))] * 2,
+        ),
         out_shape=[shape((hidden, NX * NZ * 128))] * 2,
         cost_estimate=cost(2 * 16 * 384 * 512 * 144, 4 * MIB),
         compiler_params=params(),
@@ -251,19 +260,21 @@
     total += nt_dot(other_ref[...].reshape(blocks * 96, 128), jnp.concatenate([theirs, theirs], 0))
     total = total.reshape(blocks, 96, 128)
     left = lax.broadcasted_iota(jnp.int32, (blocks, 48, 128), 2) < 64
-    out_ref[...] = jnp.where(left, total[:, :48], total[:, 48:]).astype(BF16)
+    total = jnp.where(left, total[:, :48], total[:, 48:]).astype(BF16)
+    for column in range(blocks // NZ):
+        out_ref[:, column] = total[column * NZ : (column + 1) * NZ]
 
 
 def project(keep, other, mine, theirs):
-    block = 8
+    block = 16
     weights = pl.BlockSpec((block, 96, 128), lambda i: (i, 0, 0))
     tokens = pl.BlockSpec((192, 128), lambda i: (0, 0))
     return pl.pallas_call(
         project_kernel,
         grid=(NX * NZ // block,),
         in_specs=[weights, weights, tokens, tokens],
-        out_specs=pl.BlockSpec((block, 48, 128), lambda i: (i, 0, 0)),
-        out_shape=shape((NX * NZ, 48, 128)),
+        out_specs=pl.BlockSpec((NZ, block // NZ, 48, 128), lambda i: (0, i, 0, 0)),
+        out_shape=shape((NZ, NX, 48, 128)),
         cost_estimate=cost(2 * 3072 * 256 * 128, 2 * MIB),
         compiler_params=params(),
         name="project",
@@ -329,96 +340,106 @@
     )(parts, hidden, *after)
 
 
-def up_kernel(where_ref, mine_ref, theirs_ref, weight_ref, out_ref, total_ref, square_ref):
-    index = pl.program_id(0)
+def start_copies(pairs, sems):
+    copies = [pltpu.make_async_copy(source, target, sems.at[i]) for i, (source, target) in enumerate(pairs)]
+    for copy in copies:
+        copy.start()
+    return copies
+
+
+def up_kernel(where_ref, mine_ref, theirs_ref, weight_ref, out_ref, held_ref, sems):
+    step = 4
+    parts = range(0, mine_ref.shape[0], step)
+    span = step * 192
+    copies = start_copies(
+        [(weight_ref.at[:, pl.ds(start * 192, span)], held_ref.at[index]) for index, start in enumerate(parts)], sems
+    )
     even = where_ref[0] == 0
-    blocks = mine_ref.shape[0]
-    mine, theirs = mine_ref[...], theirs_ref[...]
-    first = jnp.where(even, mine, theirs)
-    second = jnp.where(even, theirs, mine)
     left = lax.broadcasted_iota(jnp.int32, (48, 128), 1) < 64
     zero = jnp.zeros((48, 128), BF16)
-    pieces = []
-    for block in range(blocks):
-        for part in (first, second):
-            pieces += [jnp.where(left, part[block], zero), jnp.where(left, zero, part[block])]
-    tokens = jnp.concatenate(pieces, 0)
-
-    @pl.when(index == 0)
-    def _():
-        total_ref[...] = jnp.zeros_like(total_ref)
-        square_ref[...] = jnp.zeros_like(square_ref)
-
-    total_ref[...] += jnp.dot(weight_ref[...], tokens, preferred_element_type=F32)
-    wide = tokens.astype(F32)
-    square_ref[...] += jnp.sum((wide * wide).reshape(-1, 8, 128), 0)
-
-    @pl.when(index == pl.num_programs(0) - 1)
-    def _():
-        total, square = total_ref[...], jnp.sum(square_ref[...], 0, keepdims=True)
-        total = total[:, :64] + total[:, 64:]
-        square = square[:, :64] + square[:, 64:]
-        total = total * lax.rsqrt(square / 6144.0 + EPSILON_NORM)
-        half = total.shape[0] // 2
-        out_ref[...] = (silu(total[:half]) * total[half:]).astype(BF16)
+    total = jnp.zeros((weight_ref.shape[0], 128), F32)
+    square = jnp.zeros((8, 128), F32)
+    for index, start in enumerate(parts):
+        pieces = []
+        for block in range(start, start + step):
+            place = block % NZ * NX + block // NZ
+            mine, theirs = mine_ref[place], theirs_ref[place]
+            for part in (jnp.where(even, mine, theirs), jnp.where(even, theirs, mine)):
+                pieces += [jnp.where(left, part, zero), jnp.where(left, zero, part)]
+                wide = part.astype(F32)
+                square += jnp.sum((wide * wide).reshape(6, 8, 128), 0)
+        tokens = jnp.concatenate(pieces, 0)
+        copies[index].wait()
+        total += jnp.dot(held_ref[index], tokens, preferred_element_type=F32)
+    square = jnp.sum(square, 0, keepdims=True)
+    total = total[:, :64] + total[:, 64:]
+    square = square[:, :64] + square[:, 64:]
+    total = total * lax.rsqrt(square / 6144.0 + EPSILON_NORM)
+    half = total.shape[0] // 2
+    out_ref[...] = (silu(total[:half]) * total[half:]).astype(BF16)
 
 
 def up_project(where, mine, theirs, weight):
     rows, width = weight.shape
-    steps = 4
-    tokens = pl.BlockSpec((32 // steps, 48, 128), lambda i: (i, 0, 0))
     return pl.pallas_call(
         up_kernel,
-        grid=(steps,),
-        in_specs=[smem_spec(), tokens, tokens, pl.BlockSpec((rows, width // steps), lambda i: (0, i))],
-        out_specs=pl.BlockSpec((rows // 2, 64), lambda i: (0, 0)),
+        in_specs=[smem_spec(), vmem_spec(), vmem_spec(), any_spec()],
+        out_specs=vmem_spec(),
         out_shape=shape((rows // 2, 64)),
-        scratch_shapes=[pltpu.VMEM((rows, 128), F32), pltpu.VMEM((8, 128), F32)],
+        scratch_shapes=[pltpu.VMEM((8, rows, width // 8), BF16), pltpu.SemaphoreType.DMA((8,))],
         cost_estimate=cost(2 * 288 * 6144 * 128, 5 * MIB),
         compiler_params=params(),
         name="up_project",
     )(where, mine, theirs, in_hbm(weight))
 
 
-def down_kernel(mine_ref, theirs_ref, keep_ref, other_ref, after_ref, out_ref):
+def down_kernel(mine_ref, theirs_ref, keep_ref, other_ref, *out_refs):
     total = tn_dot(mine_ref[...], keep_ref[...]) + tn_dot(theirs_ref[...], other_ref[...])
     total = total.astype(BF16)
-    for block in range(NZ):
-        out_ref[0, block] = total[:, block * 128 : block * 128 + 128].reshape(4, 16, 128)
-
-
-def down_project(mine, theirs, keep, other, after):
+    half = NX // 2
+    for step in range(2):
+
+        @pl.when(pl.program_id(0) == step)
+        def _():
+            for column in range(half):
+                for block in range(NZ):
+                    start = (column * NZ + block) * 128
+                    out_refs[step * half + column][block] = total[:, start : start + 128].reshape(4, 16, 128)
+
+
+def down_project(mine, theirs, keep, other):
     hidden = mine.shape[0]
     tokens = pl.BlockSpec((hidden, 64), lambda i: (0, 0))
-    weights = pl.BlockSpec((hidden, NZ * 128), lambda i: (0, i))
+    weights = pl.BlockSpec((hidden, NX * NZ * 64), lambda i: (0, i))
     return pl.pallas_call(
         down_kernel,
-        grid=(NX,),
-        in_specs=[tokens, tokens, weights, weights, any_spec()],
-        out_specs=pl.BlockSpec((1, NZ, 4, 16, 128), lambda i: (i, 0, 0, 0, 0)),
-        out_shape=shape((NX, NZ, 4, 16, 128)),
+        grid=(2,),
+        in_specs=[tokens, tokens, weights, weights],
+        out_specs=[pl.BlockSpec((NZ, 4, 16, 128), lambda i: (0, 0, 0, 0))] * NX,
+        out_shape=[shape((NZ, 4, 16, 128))] * NX,
         cost_estimate=cost(2 * 288 * 4096 * 64, 3 * MIB),
-        compiler_params=params(),
+        compiler_params=params(16),
         name="down_project",
-    )(mine, theirs, keep, other, after)
-
-
-def merge_kernel(parts_ref, rest_ref, out_ref):
+    )(mine, theirs, keep, other)
+
+
+def merge_kernel(rest_ref, *refs):
+    in_refs, out_ref = refs[:-1], refs[-1]
     out_ref[:, :, :32] = rest_ref[...]
     for block in range(NZ):
-        out_ref[:, block, 32:] = jnp.sum(parts_ref[:, block].astype(F32), 0).astype(BF16)
-
-
-def merge(parts, rest):
+        out_ref[:, block, 32:] = sum(in_ref[block].astype(F32) for in_ref in in_refs).astype(BF16)
+
+
+def merge(rest, parts):
     return pl.pallas_call(
         merge_kernel,
-        in_specs=[vmem_spec()] * 2,
+        in_specs=[vmem_spec()] * (1 + NX),
         out_specs=vmem_spec(),
         out_shape=shape((4, NZ, 48, 128)),
         cost_estimate=cost(MIB, MIB),
         compiler_params=params(),
         name="merge",
-    )(parts, rest)
+    )(rest, *parts)
 
 
 def combine_kernel(parts_ref, place_ref, weight_ref, hidden_ref, out_ref):
@@ -441,6 +462,22 @@
     )(parts, place, weight, hidden)
 
 
+def gate_kernel(value_ref, after_ref, out_ref):
+    pass
+
+
+def gate(value, after):
+    return pl.pallas_call(
+        gate_kernel,
+        in_specs=[pl.BlockSpec(memory_space=pltpu.VMEM), any_spec()],
+        out_specs=pl.BlockSpec(memory_space=pltpu.VMEM),
+        out_shape=jax.ShapeDtypeStruct(value.shape, value.dtype),
+        input_output_aliases={0: 0},
+        compiler_params=params(1),
+        name="gate",
+    )(value, after)
+
+
 def swap(value):
     return lax.ppermute(value, "core", [(0, 1), (1, 0)])
 
@@ -455,7 +492,7 @@
 def per_device(
     unfinished, states, qkv_rows, decay_rate, out_weight, hidden_in, routes, route_weight, expert_up, expert_down
 ):
-    where = jnp.stack([lax.axis_index("core").astype(jnp.int32), lax.axis_index("x").astype(jnp.int32)])
+    where = jnp.stack([lax.axis_index(axis).astype(jnp.int32) for axis in ("core", "x", "dp")])
 
     with jax.named_scope("attention"):
         local = attend(states[0], qkv_rows[0].transpose(0, 2, 1, 3))
@@ -467,25 +504,24 @@
         slots = jnp.repeat(unfinished, 4)[:, None]
         place, weight, facts = route(routes.reshape(128, 2), route_weight.reshape(128, 2), hidden, slots)
     with jax.named_scope("heads"):
-        head_out = decay_heads(decay_rate, parts, facts, keep_out)
-        head_rows = lax.all_to_all(head_out, "dp", 0, 0, tiled=True)
-        mine, routed_hidden = select(head_rows.reshape(-1, 128))
+        head_out = decay_heads(where, decay_rate, parts, facts, keep_out)
+        head_rows = [rows.reshape(-1, 128) for rows in shifted(head_out, "dp")]
+        mine, routed_hidden = select(where, head_rows)
         theirs = swap(mine)
     with jax.named_scope("projection"):
         partial = project(keep_out, other_out, mine, theirs)
-        summed = lax.all_to_all(partial, ("x", "z"), 0, 0, tiled=True)
+        summed = lax.all_to_all(partial.reshape(NZ * NX, 48, 128), ("z", "x"), 0, 0, tiled=True)
         keep_down, other_down = split_down(where, expert_down[0], swap(expert_down[0]), partial)
         rest = project_rest(where, keep_out, other_out, mine, theirs, partial)
         rest = shifted(rest, "x")
         routed = routed_residual(summed, routed_hidden, rest[1], rest[3], keep_down)
     with jax.named_scope("expert"):
-        features = lax.all_to_all(routed, ("x", "z"), 0, 0, tiled=True)
+        features = gate(lax.all_to_all(routed, ("z", "x"), 0, 0, tiled=True), rest[2])
         up = expert_up[0].transpose(1, 2, 0).reshape(288, 6144)
         expert_hidden = up_project(where, features, swap(features), up)
-        results = down_project(expert_hidden, swap(expert_hidden), keep_down, other_down, rest[2])
+        results = down_project(expert_hidden, swap(expert_hidden), keep_down, other_down)
         rest = add_rest(rest)
-        over_x = lax.all_to_all(results, "x", 0, 0, tiled=True)
-        merged = merge(over_x, rest).reshape(32, 48, 128)
+        merged = merge(rest, shifted(results, "x")).reshape(32, 48, 128)
         returned = lax.all_to_all(merged, ("dp", "z"), 0, 0, tiled=True)
     with jax.named_scope("output"):
         mixed = combine(returned.reshape(4, NZ, 48, 128), place, weight, hidden)

time: 130 us -> 124 us (0.954)
  blocking collectives: 49.8 us -> 19.6 us
  starting transfers between devices: 27.2 us -> 40.2 us
  waiting for transfers between devices: 22.3 us -> 34.4 us
  Pallas kernels: 24.7 us -> 23.3 us
    all_to_all x2 -> x0, blocking collectives: 31.7 us -> none  [the longest x1 20.2 us: per_device(): features = lax.all_to_all(routed, ('x', 'z'), 0, 0, tiled=True)]
    ppermute x3 -> x9, waiting for transfers between devices: 6.46 us -> 21.1 us  [shifted(): lax.ppermute(blocks[far], axis, [(i, (i + far) % count) for i in range(co...]
    ppermute x3 -> x9, starting transfers between devices: 3.62 us -> 14.9 us  [shifted(): lax.ppermute(blocks[far], axis, [(i, (i + far) % count) for i in range(co...]
    all_to_all x2, waiting for transfers between devices: 9.63 us -> 5.02 us  [the longest x1 2.84 us: per_device(): lax.all_to_all(routed, ('z', 'x'), 0, 0, tiled=True)]
    ppermute x5, waiting for transfers between devices: 1.43 us -> 4.03 us  [swap(): return lax.ppermute(value, 'core', [(0, 1), (1, 0)])]
    all_to_all x2, starting transfers between devices: 10.8 us -> 12.4 us  [the longest x1 6.25 us: per_device(): lax.all_to_all(routed, ('z', 'x'), 0, 0, tiled=True)]
    all_to_all x1, blocking collectives: 18.2 us -> 19.6 us  [per_device(): returned = lax.all_to_all(merged, ('dp', 'z'), 0, 0, tiled=True)]
    pallas_call x7 -> x8, Pallas kernels: 15 us -> 14.7 us  [the longest x1 4.37 us: split_down(): pl.pallas_call(split_down_kernel, grid_spec=pltpu.PrefetchScalarGridSpec(...]
  transfers between devices with their start and end apart: 11 -> 17, of which waited for: 8 -> 14; matrix products, arithmetic and copies ran while one was open for 0% -> 0% of each run, Pallas kernels for 16% -> 13%
where the time goes in v3:
time: 124 us; the launch traced here: 122 us
  starting transfers between devices  40.2 us (32%)
  waiting for transfers between devices  34.4 us (28%)
  Pallas kernels  23.3 us (19%)
  blocking collectives  19.6 us (16%)
  local copies, waits for them, and re-layouts  3.31 us (3%)
    ppermute x9, waiting for transfers between devices, shifted(): lax.ppermute(blocks[far], axis, [(i, (i + far) % count) for i in range(co...  21.1 us
    all_to_all x1, blocking collectives, per_device(): returned = lax.all_to_all(merged, ('dp', 'z'), 0, 0, tiled=True)  19.6 us
    ppermute x9, starting transfers between devices, shifted(): lax.ppermute(blocks[far], axis, [(i, (i + far) % count) for i in range(co...  14.9 us
    all_to_all x1, starting transfers between devices, per_device(): parts = lax.all_to_all(local, HEAD, 0, 0, tiled=True)  12 us
    all_to_all x1, starting transfers between devices, per_device(): lax.all_to_all(routed, ('z', 'x'), 0, 0, tiled=True)  6.25 us
    all_to_all x1, starting transfers between devices, per_device(): lax.all_to_all(partial.reshape(NZ * NX, 48, 128), ('z', 'x'), 0, 0, tiled...  6.17 us
    pallas_call x1, Pallas kernels, split_down(): pl.pallas_call(split_down_kernel, grid_spec=pltpu.PrefetchScalarGridSpec(...  4.37 us
    all_to_all x1, waiting for transfers between devices, per_device(): parts = lax.all_to_all(local, HEAD, 0, 0, tiled=True)  4.27 us
  transfers between devices with their start and end apart: 17, of which 14 were waited for; matrix products, arithmetic and copies ran while one was open for 0% of the time, Pallas kernels for 13%

profile of v3, /device:TPU:2, one launch (start us, length us, event | category | flops | bytes accessed | tf_op | source)
XLA Modules:
  0.0 121.8 jit_solution(830331053178371570)
XLA Ops:
  0.0 0.1 collective-permute-start
  0.1 0.5 collective-permute-start.8
  0.6 2.7 %attend.1.after_ref = bf16[64,3,4,128]{3,2,1,0:T(4,128)(2,1)} custom-call(bf16[64,128,128]{2,1,0:T(8,128)(2,1)} %bitcast.39, bf16[64,3,4,128]{3,2,1,0:T(4,128)(2,1)} %bitcast.40), custom_call_target="tpu_custom_call" | custom-call | flops 16777216 | bytes 3145728 | tf_op jit(solution)/shard_map/attention/attend/pallas_call | solution.py:85
  3.3 12.0 %all-to-all-start = ((bf16[64,3,4,128]{3,2,1,0:T(4,128)(2,1)}), bf16[64,3,4,128]{3,2,1,0:T(4,128)(2,1)S(1)}, u32[]{:S(2)}, u32[]{:S(2)}) async-start(bf16[64,3,4,128]{3,2,1,0:T(4,128)(2,1)} %attend.1.after_ref), calls=%async_computation | async-start | bytes 393216 | tf_op jit(solution)/shard_map/attention/all_to_all | solution.py:499
  16.0 0.1 broadcast_in_dim.3
  16.1 0.1 reshape.52.row_ref
  16.1 0.0 copy-done.19
  16.1 0.1 copy.15
  16.3 0.0 copy-done.20
  16.3 0.1 copy.16
  16.4 0.0 copy-start.6
  16.4 0.6 route.1
  17.0 0.6 copy-done.10
  17.6 0.6 copy-done.12
  18.3 0.1 pad_add_fusion.where_ref
  18.3 0.0 collective-permute-done.theirs_ref
  18.3 0.0 copy-done.1
  18.3 2.9 %split_out.1 = (bf16[32,96,128]{2,1,0:T(8,128)(2,1)S(1)}, bf16[32,96,128]{2,1,0:T(8,128)(2,1)S(1)}) custom-call(s32[3]{0:T(128)S(1)} %pad_add_fusion.where_ref, bf16[128,6144]{1,0:T(8,128)(2,1)S(1)} %copy-done.1, bf16[128,6144]{1,0:T(8,128)(2,1)} %collective-permute-done.theirs_ref, bf16[64,3,4,128]{3,2,1,0:T(4,128)(2,1)} %attend.1.after_ref), custom_call_target="tpu_custom_call" | custom-call | flops 603979776 | bytes 3145728 | tf_op jit(solution)/shard_map/weights/split_out/pallas_call | solution.py:214
  21.3 4.3 %all-to-all-done.parts_ref = bf16[64,3,4,128]{3,2,1,0:T(4,128)(2,1)S(1)} async-done(((bf16[64,3,4,128]{3,2,1,0:T(4,128)(2,1)}), bf16[64,3,4,128]{3,2,1,0:T(4,128)(2,1)S(1)}, u32[]{:S(2)}, u32[]{:S(2)}) %all-to-all-start) | async-done | bytes 196640 | tf_op jit(solution)/shard_map/attention/all_to_all | solution.py:499
  25.6 1.1 decay_heads.1
  26.6 1.7 %collective-permute-start.1 = (bf16[68,4,128]{2,1,0:T(4,128)(2,1)S(1)}, bf16[68,4,128]{2,1,0:T(4,128)(2,1)S(1)}, u32[]{:S(2)}, u32[]{:S(2)}) collective-permute-start(bf16[68,4,128]{2,1,0:T(4,128)(2,1)S(1)} %get-tuple-element.30), channel_id=1, source_target_pairs={{0,64},{64,128},{128,192},{192,0},{1,65},{65,129},{129,193},{193,1... | collective-permute-start | bytes 208904 | tf_op jit(solution)/shard_map/heads/ppermute | solution.py:488
  28.3 2.9 %collective-permute-start.2 = (bf16[68,4,128]{2,1,0:T(4,128)(2,1)S(1)}, bf16[68,4,128]{2,1,0:T(4,128)(2,1)S(1)}, u32[]{:S(2)}, u32[]{:S(2)}) collective-permute-start(bf16[68,4,128]{2,1,0:T(4,128)(2,1)S(1)} %get-tuple-element.31), channel_id=1, source_target_pairs={{0,128},{64,192},{128,0},{192,64},{1,129},{65,193},{129,1},{193,65... | collective-permute-start | bytes 208904 | tf_op jit(solution)/shard_map/heads/ppermute | solution.py:488
  31.2 1.3 %collective-permute-start.3 = (bf16[68,4,128]{2,1,0:T(4,128)(2,1)S(1)}, bf16[68,4,128]{2,1,0:T(4,128)(2,1)S(1)}, u32[]{:S(2)}, u32[]{:S(2)}) collective-permute-start(bf16[68,4,128]{2,1,0:T(4,128)(2,1)S(1)} %get-tuple-element.32), channel_id=1, source_target_pairs={{0,192},{64,0},{128,64},{192,128},{1,193},{65,1},{129,65},{193,129... | collective-permute-start | bytes 208904 | tf_op jit(solution)/shard_map/heads/ppermute | solution.py:488
  32.5 0.0 collective-permute-done.1
  32.5 2.4 %collective-permute-done.2 = bf16[68,4,128]{2,1,0:T(4,128)(2,1)S(1)} collective-permute-done((bf16[68,4,128]{2,1,0:T(4,128)(2,1)S(1)}, bf16[68,4,128]{2,1,0:T(4,128)(2,1)S(1)}, u32[]{:S(2)}, u32[]{:S(2)}) %collective-permute-start.2) | collective-permute-done | bytes 69664 | tf_op jit(solution)/shard_map/heads/ppermute | solution.py:488
  34.9 0.6 collective-permute-done.3
  35.5 1.1 select.2
  36.6 0.0 copy-start.14
  36.6 0.6 copy-done.14
  37.2 0.0 collective-permute-start.4
  37.2 1.2 %collective-permute-done.4.theirs_ref = bf16[192,128]{1,0:T(8,128)(2,1)S(1)} collective-permute-done((bf16[192,128]{1,0:T(8,128)(2,1)S(1)}, bf16[192,128]{1,0:T(8,128)(2,1)S(1)}, u32[]{:S(2)}, u32[]{:S(2)}) %collective-permute-start.4) | collective-permute-done | bytes 49184 | tf_op jit(solution)/shard_map/heads/ppermute | solution.py:482
  38.5 1.5 %project.1.after_ref = bf16[8,4,48,128]{3,2,1,0:T(8,128)(2,1)} custom-call(bf16[32,96,128]{2,1,0:T(8,128)(2,1)S(1)} %get-tuple-element.26.after_ref.keep_ref, bf16[32,96,128]{2,1,0:T(8,128)(2,1)S(1)} %get-tuple-element.27.other_ref, bf16[192,128]{1,0:T(8,128)(2,1)S(1)} %get-tuple-element.33.mine_ref, bf16[192,128]{1,0:T(8,128)(2,1)S(1)} %collective-permute-done.4.theirs_ref), custom_call_target="tpu_custom_call" | custom-call | flops 201326592 | bytes 2097152 | tf_op jit(solution)/shard_map/projection/project/pallas_call | solution.py:272
  39.9 6.2 %all-to-all-start.1 = ((bf16[32,48,128]{2,1,0:T(8,128)(2,1)}), bf16[32,48,128]{2,1,0:T(8,128)(2,1)}, u32[]{:S(2)}, u32[]{:S(2)}) async-start(bf16[32,48,128]{2,1,0:T(8,128)(2,1)} %bitcast.14), calls=%async_computation.1 | async-start | bytes 786432 | tf_op jit(solution)/shard_map/projection/all_to_all | solution.py:513
  46.1 1.1 project_rest.1
  47.3 1.5 %collective-permute-start.5 = (bf16[8,96,128]{2,1,0:T(8,128)(2,1)S(1)}, bf16[8,96,128]{2,1,0:T(8,128)(2,1)S(1)}, u32[]{:S(2)}, u32[]{:S(2)}) collective-permute-start(bf16[8,96,128]{2,1,0:T(8,128)(2,1)S(1)} %get-tuple-element.35), channel_id=1, source_target_pairs={{0,16},{16,32},{32,48},{48,0},{1,17},{17,33},{33,49},{49,1},{2,18}... | collective-permute-start | bytes 589832 | tf_op jit(solution)/shard_map/projection/ppermute | solution.py:488
  48.8 0.6 collective-permute-start.7
  49.4 0.0 collective-permute-done.8.theirs_ref
  49.4 4.4 %split_down.1 = (bf16[144,4096]{1,0:T(8,128)(2,1)S(1)}, bf16[144,4096]{1,0:T(8,128)(2,1)S(1)}) custom-call(s32[3]{0:T(128)S(1)} %pad_add_fusion.where_ref, bf16[144,6144]{1,0:T(8,128)(2,1)S(1)} %bitcast.29, bf16[144,6144]{1,0:T(8,128)(2,1)} %collective-permute-done.8.theirs_ref, bf16[8,4,48,128]{3,2,1,0:T(8,128)(2,1)} %project.1.after_ref), custom_call_target="tpu_custom_call" | custom-call | flops 905969664 | bytes 4194304 | tf_op jit(solution)/shard_map/projection/split_down/pallas_call | solution.py:241
  53.8 1.0 copy-done.2
  54.8 1.8 %collective-permute-done.5.refs_1_.one_ref = bf16[8,96,128]{2,1,0:T(8,128)(2,1)S(1)} collective-permute-done((bf16[8,96,128]{2,1,0:T(8,128)(2,1)S(1)}, bf16[8,96,128]{2,1,0:T(8,128)(2,1)S(1)}, u32[]{:S(2)}, u32[]{:S(2)}) %collective-permute-start.5) | collective-permute-done | bytes 196640 | tf_op jit(solution)/shard_map/projection/ppermute | solution.py:488
  56.7 1.7 %collective-permute-done.7.refs_3_.two_ref = bf16[8,96,128]{2,1,0:T(8,128)(2,1)S(1)} collective-permute-done((bf16[8,96,128]{2,1,0:T(8,128)(2,1)S(1)}, bf16[8,96,128]{2,1,0:T(8,128)(2,1)S(1)}, u32[]{:S(2)}, u32[]{:S(2)}) %collective-permute-start.7) | collective-permute-done | bytes 196640 | tf_op jit(solution)/shard_map/projection/ppermute | solution.py:488
  58.3 2.2 %all-to-all-done.1.in_ref = bf16[32,48,128]{2,1,0:T(8,128)(2,1)} async-done(((bf16[32,48,128]{2,1,0:T(8,128)(2,1)}), bf16[32,48,128]{2,1,0:T(8,128)(2,1)}, u32[]{:S(2)}, u32[]{:S(2)}) %all-to-all-start.1) | async-done | bytes 393248 | tf_op jit(solution)/shard_map/projection/all_to_all | solution.py:513
  60.5 1.9 %routed_residual.1 = bf16[32,48,128]{2,1,0:T(8,128)(2,1)} custom-call(bf16[32,48,128]{2,1,0:T(8,128)(2,1)} %all-to-all-done.1.in_ref, f32[48,128]{1,0:T(8,128)S(1)} %copy-done.15, bf16[8,96,128]{2,1,0:T(8,128)(2,1)S(1)} %collective-permute-done.5.refs_1_.one_ref, bf16[8,96,128]{2,1,0:T(8,128)(2,1)S(1)} %collective-permute-done.7.refs_3_.two_ref, ...), custom_call_target="tpu_custom_call" | custom-call | flops 1048576 | bytes 1048576 | tf_op jit(solution)/shard_map/projection/routed_residual/pallas_call | solution.py:332
  62.4 6.2 %all-to-all-start.2 = ((bf16[32,48,128]{2,1,0:T(8,128)(2,1)}), bf16[32,48,128]{2,1,0:T(8,128)(2,1)S(1)}, u32[]{:S(2)}, u32[]{:S(2)}) async-start(bf16[32,48,128]{2,1,0:T(8,128)(2,1)} %routed_residual.1), calls=%async_computation.2 | async-start | bytes 786432 | tf_op jit(solution)/shard_map/expert/all_to_all | solution.py:519
  68.6 2.2 %collective-permute-start.6 = (bf16[8,96,128]{2,1,0:T(8,128)(2,1)S(1)}, bf16[8,96,128]{2,1,0:T(8,128)(2,1)S(1)}, u32[]{:S(2)}, u32[]{:S(2)}) collective-permute-start(bf16[8,96,128]{2,1,0:T(8,128)(2,1)S(1)} %copy-done.17), channel_id=1, source_target_pairs={{0,32},{16,48},{32,0},{48,16},{1,33},{17,49},{33,1},{49,17},{2,34}... | collective-permute-start | bytes 589832 | tf_op jit(solution)/shard_map/projection/ppermute | solution.py:488
  70.8 8.4 %collective-permute-done.6.refs_2_.after_ref = bf16[8,96,128]{2,1,0:T(8,128)(2,1)S(1)} collective-permute-done((bf16[8,96,128]{2,1,0:T(8,128)(2,1)S(1)}, bf16[8,96,128]{2,1,0:T(8,128)(2,1)S(1)}, u32[]{:S(2)}, u32[]{:S(2)}) %collective-permute-start.6) | collective-permute-done | bytes 196640 | tf_op jit(solution)/shard_map/projection/ppermute | solution.py:488
  79.2 2.8 %all-to-all-done.2.value_ref = bf16[32,48,128]{2,1,0:T(8,128)(2,1)S(1)} async-done(((bf16[32,48,128]{2,1,0:T(8,128)(2,1)}), bf16[32,48,128]{2,1,0:T(8,128)(2,1)S(1)}, u32[]{:S(2)}, u32[]{:S(2)}) %all-to-all-start.2) | async-done | bytes 393248 | tf_op jit(solution)/shard_map/expert/all_to_all | solution.py:519
  82.1 0.0 collective-permute-start.9
  82.1 1.7 %collective-permute-done.9.theirs_ref = bf16[32,48,128]{2,1,0:T(8,128)(2,1)S(1)} collective-permute-done((bf16[32,48,128]{2,1,0:T(8,128)(2,1)S(1)}, bf16[32,48,128]{2,1,0:T(8,128)(2,1)S(1)}, u32[]{:S(2)}, u32[]{:S(2)}) %collective-permute-start.9) | collective-permute-done | bytes 393248 | tf_op jit(solution)/shard_map/expert/ppermute | solution.py:482
  83.8 4.1 %up_project.1.mine_ref = bf16[144,64]{1,0:T(8,128)(2,1)S(1)} custom-call(s32[3]{0:T(128)S(1)} %pad_add_fusion.where_ref, bf16[32,48,128]{2,1,0:T(8,128)(2,1)S(1)} %gate.1.mine_ref, bf16[32,48,128]{2,1,0:T(8,128)(2,1)S(1)} %collective-permute-done.9.theirs_ref, bf16[288,6144]{1,0:T(8,128)(2,1)} %bitcast.38), custom_call_target="tpu_custom_call" | custom-call | flops 452984832 | bytes 5242880 | tf_op jit(solution)/shard_map/expert/up_project/pallas_call | solution.py:384
  88.0 0.2 collective-permute-start.10
  88.2 1.1 collective-permute-done.10.theirs_ref
  89.3 0.9 down_project.1
  90.2 0.0 copy-start.13
  90.2 1.5 %collective-permute-start.11 = (bf16[8,4,16,128]{3,2,1,0:T(8,128)(2,1)S(1)}, bf16[8,4,16,128]{3,2,1,0:T(8,128)(2,1)S(1)}, u32[]{:S(2)}, u32[]{:S(2)}) collective-permute-start(bf16[8,4,16,128]{3,2,1,0:T(8,128)(2,1)S(1)} %get-tuple-element.42), channel_id=1, source_target_pairs={{0,16},{16,32},{32,48},{48,0},{1,17},{17,33},{33,49},{49,1},{2,18}... | collective-permute-start | bytes 393224 | tf_op jit(solution)/shard_map/expert/ppermute | solution.py:488
  91.8 2.2 %collective-permute-start.12 = (bf16[8,4,16,128]{3,2,1,0:T(8,128)(2,1)S(1)}, bf16[8,4,16,128]{3,2,1,0:T(8,128)(2,1)S(1)}, u32[]{:S(2)}, u32[]{:S(2)}) collective-permute-start(bf16[8,4,16,128]{3,2,1,0:T(8,128)(2,1)S(1)} %get-tuple-element.43), channel_id=1, source_target_pairs={{0,32},{16,48},{32,0},{48,16},{1,33},{17,49},{33,1},{49,17},{2,34}... | collective-permute-start | bytes 393224 | tf_op jit(solution)/shard_map/expert/ppermute | solution.py:488
  94.0 1.0 collective-permute-start.13
  95.0 0.2 add_rest.1.rest_ref
  95.2 1.0 collective-permute-done.11.refs_1_
  96.2 3.4 %collective-permute-done.12.refs_2_ = bf16[8,4,16,128]{3,2,1,0:T(8,128)(2,1)S(1)} collective-permute-done((bf16[8,4,16,128]{3,2,1,0:T(8,128)(2,1)S(1)}, bf16[8,4,16,128]{3,2,1,0:T(8,128)(2,1)S(1)}, u32[]{:S(2)}, u32[]{:S(2)}) %collective-permute-start.12) | collective-permute-done | bytes 131104 | tf_op jit(solution)/shard_map/expert/ppermute | solution.py:488
  99.7 1.7 %collective-permute-done.13.refs_3_ = bf16[8,4,16,128]{3,2,1,0:T(8,128)(2,1)S(1)} collective-permute-done((bf16[8,4,16,128]{3,2,1,0:T(8,128)(2,1)S(1)}, bf16[8,4,16,128]{3,2,1,0:T(8,128)(2,1)S(1)}, u32[]{:S(2)}, u32[]{:S(2)}) %collective-permute-start.13) | collective-permute-done | bytes 131104 | tf_op jit(solution)/shard_map/expert/ppermute | solution.py:488
  101.4 0.1 merge.1
  101.5 19.6 %all_to_all.20 = bf16[32,48,128]{2,1,0:T(8,128)(2,1)S(1)} all-to-all(bf16[32,48,128]{2,1,0:T(8,128)(2,1)S(1)} %bitcast.31), channel_id=1, replica_groups=mesh['dp'=4,'x'=4,'z'=8,'core'=2] {'dp','z'}, dimensions={0} | all-to-all | bytes 786432 | tf_op jit(solution)/shard_map/expert/all_to_all | solution.py:525
  121.0 0.8 combine.1
  (36 shorter events, 0.1 us)
Async XLA Ops:
  0.0 18.3 %copy-start.1 = (bf16[128,6144]{1,0:T(8,128)(2,1)S(1)}, bf16[128,6144]{1,0:T(8,128)(2,1)}, u32[]{:S(2)}) copy-start(bf16[128,6144]{1,0:T(8,128)(2,1)} %mine_ref.1) | copy-start | bytes 4718596
  0.0 16.0 %copy-start.21 = (s32[32]{0:T(128)S(1)}, s32[32]{0:T(128)}, u32[]{:S(2)}) copy-start(s32[32]{0:T(128)} %param.10) | copy-start | bytes 388
  0.0 16.1 %copy-start.19 = (s32[32,4,2]{0,2,1:T(2,128)S(1)}, s32[32,4,2]{0,2,1:T(2,128)}, u32[]{:S(2)}) copy-start(s32[32,4,2]{0,2,1:T(2,128)} %param.16) | copy-start | bytes 3076
  0.0 16.3 %copy-start.20 = (f32[32,4,2]{0,2,1:T(2,128)S(1)}, f32[32,4,2]{0,2,1:T(2,128)}, u32[]{:S(2)}) copy-start(f32[32,4,2]{0,2,1:T(2,128)} %param.17) | copy-start | bytes 3076
  0.0 16.4 %copy-start.18 = (bf16[96,32,4]{0,2,1:T(4,128)(2,1)S(1)}, bf16[96,32,4]{0,2,1:T(4,128)(2,1)}, u32[]{:S(2)}) copy-start(bf16[96,32,4]{0,2,1:T(4,128)(2,1)} %param.15) | copy-start | bytes 73732
  0.0 18.3 %collective-permute-start = (bf16[128,6144]{1,0:T(8,128)(2,1)}, bf16[128,6144]{1,0:T(8,128)(2,1)}, u32[]{:S(2)}, u32[]{:S(2)}) collective-permute-start(bf16[128,6144]{1,0:T(8,128)(2,1)} %mine_ref.1), channel_id=1, source_target_pairs={{0,1},{1,0},{2,3},{3,2},{4,5},{5,4},{6,7},{7,6},{8,9},{9,8},{10,11... | collective-permute-start | bytes 4718600 | tf_op jit(solution)/shard_map/weights/ppermute | solution.py:482
  0.1 49.2 %collective-permute-start.8 = (bf16[144,6144]{1,0:T(8,128)(2,1)}, bf16[144,6144]{1,0:T(8,128)(2,1)}, u32[]{:S(2)}, u32[]{:S(2)}) collective-permute-start(bf16[144,6144]{1,0:T(8,128)(2,1)} %bitcast.28), channel_id=1, source_target_pairs={{0,1},{1,0},{2,3},{3,2},{4,5},{5,4},{6,7},{7,6},{8,9},{9,8},{10,11... | collective-permute-start | bytes 5308424 | tf_op jit(solution)/shard_map/projection/ppermute | solution.py:482
  3.3 22.3 %all-to-all-start = ((bf16[64,3,4,128]{3,2,1,0:T(4,128)(2,1)}), bf16[64,3,4,128]{3,2,1,0:T(4,128)(2,1)S(1)}, u32[]{:S(2)}, u32[]{:S(2)}) async-start(bf16[64,3,4,128]{3,2,1,0:T(4,128)(2,1)} %attend.1.after_ref), calls=%async_computation | async-start | bytes 393216 | tf_op jit(solution)/shard_map/attention/all_to_all | solution.py:499
  16.4 1.9 %copy-start.6 = (bf16[128,128]{1,0:T(8,128)(2,1)}, bf16[128,128]{1,0:T(8,128)(2,1)S(1)}, u32[]{:S(2)}) copy-start(bf16[128,128]{1,0:T(8,128)(2,1)S(1)} %pad.4.hidden_ref) | copy-start | bytes 98308
  17.0 0.6 copy-start.10
  17.6 0.6 copy-start.12
  26.6 5.9 %collective-permute-start.1 = (bf16[68,4,128]{2,1,0:T(4,128)(2,1)S(1)}, bf16[68,4,128]{2,1,0:T(4,128)(2,1)S(1)}, u32[]{:S(2)}, u32[]{:S(2)}) collective-permute-start(bf16[68,4,128]{2,1,0:T(4,128)(2,1)S(1)} %get-tuple-element.30), channel_id=1, source_target_pairs={{0,64},{64,128},{128,192},{192,0},{1,65},{65,129},{129,193},{193,1... | collective-permute-start | bytes 208904 | tf_op jit(solution)/shard_map/heads/ppermute | solution.py:488
  28.3 6.6 %collective-permute-start.2 = (bf16[68,4,128]{2,1,0:T(4,128)(2,1)S(1)}, bf16[68,4,128]{2,1,0:T(4,128)(2,1)S(1)}, u32[]{:S(2)}, u32[]{:S(2)}) collective-permute-start(bf16[68,4,128]{2,1,0:T(4,128)(2,1)S(1)} %get-tuple-element.31), channel_id=1, source_target_pairs={{0,128},{64,192},{128,0},{192,64},{1,129},{65,193},{129,1},{193,65... | collective-permute-start | bytes 208904 | tf_op jit(solution)/shard_map/heads/ppermute | solution.py:488
  31.2 4.3 %collective-permute-start.3 = (bf16[68,4,128]{2,1,0:T(4,128)(2,1)S(1)}, bf16[68,4,128]{2,1,0:T(4,128)(2,1)S(1)}, u32[]{:S(2)}, u32[]{:S(2)}) collective-permute-start(bf16[68,4,128]{2,1,0:T(4,128)(2,1)S(1)} %get-tuple-element.32), channel_id=1, source_target_pairs={{0,192},{64,0},{128,64},{192,128},{1,193},{65,1},{129,65},{193,129... | collective-permute-start | bytes 208904 | tf_op jit(solution)/shard_map/heads/ppermute | solution.py:488
  36.6 0.6 copy-start.14
  37.2 1.2 %collective-permute-start.4 = (bf16[192,128]{1,0:T(8,128)(2,1)S(1)}, bf16[192,128]{1,0:T(8,128)(2,1)S(1)}, u32[]{:S(2)}, u32[]{:S(2)}) collective-permute-start(bf16[192,128]{1,0:T(8,128)(2,1)S(1)} %get-tuple-element.33.mine_ref), channel_id=1, source_target_pairs={{0,1},{1,0},{2,3},{3,2},{4,5},{5,4},{6,7},{7,6},{8,9},{9,8},{10,11... | collective-permute-start | bytes 147464 | tf_op jit(solution)/shard_map/heads/ppermute | solution.py:482
  39.9 9.4 %copy-start = (bf16[1,144,6144]{2,1,0:T(8,128)(2,1)S(1)}, bf16[1,144,6144]{2,1,0:T(8,128)(2,1)}, u32[]{:S(2)}) copy-start(bf16[1,144,6144]{2,1,0:T(8,128)(2,1)} %param.19) | copy-start | bytes 5308420
  39.9 20.6 %all-to-all-start.1 = ((bf16[32,48,128]{2,1,0:T(8,128)(2,1)}), bf16[32,48,128]{2,1,0:T(8,128)(2,1)}, u32[]{:S(2)}, u32[]{:S(2)}) async-start(bf16[32,48,128]{2,1,0:T(8,128)(2,1)} %bitcast.14), calls=%async_computation.1 | async-start | bytes 786432 | tf_op jit(solution)/shard_map/projection/all_to_all | solution.py:513
  47.2 6.5 %copy-start.8 = (bf16[8,96,128]{2,1,0:T(8,128)(2,1)}, bf16[8,96,128]{2,1,0:T(8,128)(2,1)S(1)}, u32[]{:S(2)}) copy-start(bf16[8,96,128]{2,1,0:T(8,128)(2,1)S(1)} %get-tuple-element.34.refs_0_) | copy-start | bytes 589828
  47.2 6.5 %copy-start.16 = (bf16[8,96,128]{2,1,0:T(8,128)(2,1)}, bf16[8,96,128]{2,1,0:T(8,128)(2,1)S(1)}, u32[]{:S(2)}) copy-start(bf16[8,96,128]{2,1,0:T(8,128)(2,1)S(1)} %get-tuple-element.36) | copy-start | bytes 589828
  47.3 9.4 %collective-permute-start.5 = (bf16[8,96,128]{2,1,0:T(8,128)(2,1)S(1)}, bf16[8,96,128]{2,1,0:T(8,128)(2,1)S(1)}, u32[]{:S(2)}, u32[]{:S(2)}) collective-permute-start(bf16[8,96,128]{2,1,0:T(8,128)(2,1)S(1)} %get-tuple-element.35), channel_id=1, source_target_pairs={{0,16},{16,32},{32,48},{48,0},{1,17},{17,33},{33,49},{49,1},{2,18}... | collective-permute-start | bytes 589832 | tf_op jit(solution)/shard_map/projection/ppermute | solution.py:488
  48.8 11.7 %copy-start.15 = (f32[48,128]{1,0:T(8,128)S(1)}, f32[48,128]{1,0:T(8,128)}, u32[]{:S(2)}) copy-start(f32[48,128]{1,0:T(8,128)} %copy-done.14) | copy-start | bytes 73732
  48.8 9.5 %collective-permute-start.7 = (bf16[8,96,128]{2,1,0:T(8,128)(2,1)S(1)}, bf16[8,96,128]{2,1,0:T(8,128)(2,1)S(1)}, u32[]{:S(2)}, u32[]{:S(2)}) collective-permute-start(bf16[8,96,128]{2,1,0:T(8,128)(2,1)S(1)} %get-tuple-element.37), channel_id=1, source_target_pairs={{0,48},{16,0},{32,16},{48,32},{1,49},{17,1},{33,17},{49,33},{2,50}... | collective-permute-start | bytes 589832 | tf_op jit(solution)/shard_map/projection/ppermute | solution.py:488
  53.8 1.0 copy-start.2
  56.7 12.0 %copy-start.17 = (bf16[8,96,128]{2,1,0:T(8,128)(2,1)S(1)}, bf16[8,96,128]{2,1,0:T(8,128)(2,1)}, u32[]{:S(2)}) copy-start(bf16[8,96,128]{2,1,0:T(8,128)(2,1)} %copy-done.16) | copy-start | bytes 589828
  58.3 4.0 %copy-start.4 = (bf16[8,96,128]{2,1,0:T(8,128)(2,1)}, bf16[8,96,128]{2,1,0:T(8,128)(2,1)S(1)}, u32[]{:S(2)}) copy-start(bf16[8,96,128]{2,1,0:T(8,128)(2,1)S(1)} %collective-permute-done.7.refs_3_.two_ref) | copy-start | bytes 589828
  62.4 19.7 %all-to-all-start.2 = ((bf16[32,48,128]{2,1,0:T(8,128)(2,1)}), bf16[32,48,128]{2,1,0:T(8,128)(2,1)S(1)}, u32[]{:S(2)}, u32[]{:S(2)}) async-start(bf16[32,48,128]{2,1,0:T(8,128)(2,1)} %routed_residual.1), calls=%async_computation.2 | async-start | bytes 786432 | tf_op jit(solution)/shard_map/expert/all_to_all | solution.py:519
  68.6 10.6 %collective-permute-start.6 = (bf16[8,96,128]{2,1,0:T(8,128)(2,1)S(1)}, bf16[8,96,128]{2,1,0:T(8,128)(2,1)S(1)}, u32[]{:S(2)}, u32[]{:S(2)}) collective-permute-start(bf16[8,96,128]{2,1,0:T(8,128)(2,1)S(1)} %copy-done.17), channel_id=1, source_target_pairs={{0,32},{16,48},{32,0},{48,16},{1,33},{17,49},{33,1},{49,17},{2,34}... | collective-permute-start | bytes 589832 | tf_op jit(solution)/shard_map/projection/ppermute | solution.py:488
  82.1 1.7 %collective-permute-start.9 = (bf16[32,48,128]{2,1,0:T(8,128)(2,1)S(1)}, bf16[32,48,128]{2,1,0:T(8,128)(2,1)S(1)}, u32[]{:S(2)}, u32[]{:S(2)}) collective-permute-start(bf16[32,48,128]{2,1,0:T(8,128)(2,1)S(1)} %gate.1.mine_ref), channel_id=1, source_target_pairs={{0,1},{1,0},{2,3},{3,2},{4,5},{5,4},{6,7},{7,6},{8,9},{9,8},{10,11... | collective-permute-start | bytes 1179656 | tf_op jit(solution)/shard_map/expert/ppermute | solution.py:482
  83.8 5.4 %copy-start.3 = (bf16[144,4096]{1,0:T(8,128)(2,1)S(1)}, bf16[144,4096]{1,0:T(8,128)(2,1)}, u32[]{:S(2)}) copy-start(bf16[144,4096]{1,0:T(8,128)(2,1)} %copy-done.2) | copy-start | bytes 3538948
  87.9 7.1 %copy-start.5 = (bf16[8,96,128]{2,1,0:T(8,128)(2,1)S(1)}, bf16[8,96,128]{2,1,0:T(8,128)(2,1)}, u32[]{:S(2)}) copy-start(bf16[8,96,128]{2,1,0:T(8,128)(2,1)} %copy-done.4) | copy-start | bytes 589828
  87.9 7.1 %copy-start.9 = (bf16[8,96,128]{2,1,0:T(8,128)(2,1)S(1)}, bf16[8,96,128]{2,1,0:T(8,128)(2,1)}, u32[]{:S(2)}) copy-start(bf16[8,96,128]{2,1,0:T(8,128)(2,1)} %copy-done.8) | copy-start | bytes 589828
  88.0 1.3 %collective-permute-start.10 = (bf16[144,64]{1,0:T(8,128)(2,1)S(1)}, bf16[144,64]{1,0:T(8,128)(2,1)S(1)}, u32[]{:S(2)}, u32[]{:S(2)}) collective-permute-start(bf16[144,64]{1,0:T(8,128)(2,1)S(1)} %up_project.1.mine_ref), channel_id=1, source_target_pairs={{0,1},{1,0},{2,3},{3,2},{4,5},{5,4},{6,7},{7,6},{8,9},{9,8},{10,11... | collective-permute-start | bytes 55304 | tf_op jit(solution)/shard_map/expert/ppermute | solution.py:482
  90.2 30.8 %copy-start.7 = (bf16[128,128]{1,0:T(8,128)(2,1)S(1)}, bf16[128,128]{1,0:T(8,128)(2,1)}, u32[]{:S(2)}) copy-start(bf16[128,128]{1,0:T(8,128)(2,1)} %copy-done.6) | copy-start | bytes 98308
  90.2 30.8 %copy-start.11 = (f32[128,1]{1,0:T(8,128)S(1)}, f32[128,1]{1,0:T(8,128)}, u32[]{:S(2)}) copy-start(f32[128,1]{1,0:T(8,128)} %copy-done.10) | copy-start | bytes 1540
  90.2 30.8 %copy-start.13 = (bf16[128,128]{1,0:T(8,128)(2,1)S(1)}, bf16[128,128]{1,0:T(8,128)(2,1)}, u32[]{:S(2)}) copy-start(bf16[128,128]{1,0:T(8,128)(2,1)} %copy-done.12) | copy-start | bytes 98308
  90.2 6.0 %collective-permute-start.11 = (bf16[8,4,16,128]{3,2,1,0:T(8,128)(2,1)S(1)}, bf16[8,4,16,128]{3,2,1,0:T(8,128)(2,1)S(1)}, u32[]{:S(2)}, u32[]{:S(2)}) collective-permute-start(bf16[8,4,16,128]{3,2,1,0:T(8,128)(2,1)S(1)} %get-tuple-element.42), channel_id=1, source_target_pairs={{0,16},{16,32},{32,48},{48,0},{1,17},{17,33},{33,49},{49,1},{2,18}... | collective-permute-start | bytes 393224 | tf_op jit(solution)/shard_map/expert/ppermute | solution.py:488
  91.8 7.9 %collective-permute-start.12 = (bf16[8,4,16,128]{3,2,1,0:T(8,128)(2,1)S(1)}, bf16[8,4,16,128]{3,2,1,0:T(8,128)(2,1)S(1)}, u32[]{:S(2)}, u32[]{:S(2)}) collective-permute-start(bf16[8,4,16,128]{3,2,1,0:T(8,128)(2,1)S(1)} %get-tuple-element.43), channel_id=1, source_target_pairs={{0,32},{16,48},{32,0},{48,16},{1,33},{17,49},{33,1},{49,17},{2,34}... | collective-permute-start | bytes 393224 | tf_op jit(solution)/shard_map/expert/ppermute | solution.py:488
  94.0 7.4 %collective-permute-start.13 = (bf16[8,4,16,128]{3,2,1,0:T(8,128)(2,1)S(1)}, bf16[8,4,16,128]{3,2,1,0:T(8,128)(2,1)S(1)}, u32[]{:S(2)}, u32[]{:S(2)}) collective-permute-start(bf16[8,4,16,128]{3,2,1,0:T(8,128)(2,1)S(1)} %get-tuple-element.44), channel_id=1, source_target_pairs={{0,48},{16,0},{32,16},{48,32},{1,49},{17,1},{33,17},{49,33},{2,50}... | collective-permute-start | bytes 393224 | tf_op jit(solution)/shard_map/expert/ppermute | solution.py:488

commit v4 on v3

--- a/solution.py
+++ b/solution.py
@@ -223,16 +223,18 @@
     )(where, mine, in_hbm(theirs), after)
 
 
+def own_blocks(core):
+    row = lax.broadcasted_iota(jnp.int32, (768, 384), 0)
+    lane = lax.broadcasted_iota(jnp.int32, (768, 384), 1)
+    return one_hot(row == lane // 96 * 192 + lane % 96 + core * 96)
+
+
 def split_down_kernel(where_ref, mine_ref, theirs_ref, after_ref, *out_refs):
-    core = where_ref[0]
-    row = lax.broadcasted_iota(jnp.int32, (384, 256), 0)
-    lane = lax.broadcasted_iota(jnp.int32, (384, 256), 1)
-    pick = one_hot((row == lane // 128 * 192 + lane % 128 + core * 96) & (lane % 128 < 96))
-    for part in range(4):
+    pick = own_blocks(where_ref[0])
+    for part in range(2):
         for weight_ref, out_ref in zip((mine_ref, theirs_ref), out_refs):
-            weight = weight_ref[:, part * 384 : part * 384 + 384]
-            total = jnp.dot(weight, pick, preferred_element_type=F32)
-            out_ref[:, part * 256 : part * 256 + 256] = total.astype(BF16)
+            weight = weight_ref[:, part * 768 : part * 768 + 768]
+            out_ref[:, part * 384 : part * 384 + 384] = jnp.dot(weight, pick, preferred_element_type=F32).astype(BF16)
 
 
 def split_down(where, mine, theirs, after):
@@ -244,13 +246,40 @@
             num_scalar_prefetch=1,
             grid=(NX,),
             in_specs=[weights, weights, any_spec()],
-            out_specs=[pl.BlockSpec((hidden, NZ * 128), lambda i, where: (0, i))] * 2,
+            out_specs=[pl.BlockSpec((hidden, NZ * 96), lambda i, where: (0, i))] * 2,
         ),
-        out_shape=[shape((hidden, NX * NZ * 128))] * 2,
+        out_shape=[shape((hidden, NX * NZ * 96))] * 2,
         cost_estimate=cost(2 * 16 * 384 * 512 * 144, 4 * MIB),
         compiler_params=params(),
         name="split_down",
     )(where, mine, in_hbm(theirs), after)
+
+
+def split_up_kernel(where_ref, mine_ref, theirs_ref, after_ref, out_ref, done_ref):
+    done_ref[...] = jnp.zeros_like(done_ref)
+    pick = own_blocks(where_ref[0])
+    rows = mine_ref.shape[0]
+    for part in range(2):
+        for side, weight_ref in enumerate((mine_ref, theirs_ref)):
+            weight = weight_ref[:, part * 768 : part * 768 + 768]
+            out_ref[side * rows : (side + 1) * rows, part * 384 : part * 384 + 384] = jnp.dot(
+                weight, pick, preferred_element_type=F32
+            ).astype(BF16)
+
+
+def split_up(where, mine, theirs, after):
+    rows, width = mine.shape
+    weights = pl.BlockSpec((rows, 1536), lambda i: (0, i))
+    return pl.pallas_call(
+        split_up_kernel,
+        grid=(width // 1536,),
+        in_specs=[smem_spec(), weights, weights, any_spec()],
+        out_specs=[pl.BlockSpec((2 * rows, 768), lambda i: (0, i)), pl.BlockSpec((8, 128), lambda i: (0, 0))],
+        out_shape=[shape((2 * rows, width // 2)), shape((8, 128), F32)],
+        cost_estimate=cost(2 * 576 * 6144 * 768, 11 * MIB),
+        compiler_params=params(16),
+        name="split_up",
+    )(where, in_hbm(mine), in_hbm(theirs), after)
 
 
 def project_kernel(keep_ref, other_ref, mine_ref, theirs_ref, out_ref):
@@ -340,84 +369,70 @@
     )(parts, hidden, *after)
 
 
-def start_copies(pairs, sems):
-    copies = [pltpu.make_async_copy(source, target, sems.at[i]) for i, (source, target) in enumerate(pairs)]
-    for copy in copies:
-        copy.start()
-    return copies
-
-
-def up_kernel(where_ref, mine_ref, theirs_ref, weight_ref, out_ref, held_ref, sems):
-    step = 4
-    parts = range(0, mine_ref.shape[0], step)
-    span = step * 192
-    copies = start_copies(
-        [(weight_ref.at[:, pl.ds(start * 192, span)], held_ref.at[index]) for index, start in enumerate(parts)], sems
-    )
-    even = where_ref[0] == 0
+def up_kernel(features_ref, weight_ref, after_ref, out_ref):
+    rows, blocks = weight_ref.shape[0], features_ref.shape[0]
+    step = blocks // 2
     left = lax.broadcasted_iota(jnp.int32, (48, 128), 1) < 64
     zero = jnp.zeros((48, 128), BF16)
-    total = jnp.zeros((weight_ref.shape[0], 128), F32)
+    total = jnp.zeros((rows, 128), F32)
     square = jnp.zeros((8, 128), F32)
-    for index, start in enumerate(parts):
+    for start in range(0, blocks, step):
         pieces = []
         for block in range(start, start + step):
-            place = block % NZ * NX + block // NZ
-            mine, theirs = mine_ref[place], theirs_ref[place]
-            for part in (jnp.where(even, mine, theirs), jnp.where(even, theirs, mine)):
-                pieces += [jnp.where(left, part, zero), jnp.where(left, zero, part)]
-                wide = part.astype(F32)
-                square += jnp.sum((wide * wide).reshape(6, 8, 128), 0)
-        tokens = jnp.concatenate(pieces, 0)
-        copies[index].wait()
-        total += jnp.dot(held_ref[index], tokens, preferred_element_type=F32)
-    square = jnp.sum(square, 0, keepdims=True)
-    total = total[:, :64] + total[:, 64:]
-    square = square[:, :64] + square[:, 64:]
-    total = total * lax.rsqrt(square / 6144.0 + EPSILON_NORM)
-    half = total.shape[0] // 2
-    out_ref[...] = (silu(total[:half]) * total[half:]).astype(BF16)
-
-
-def up_project(where, mine, theirs, weight):
-    rows, width = weight.shape
+            part = features_ref[block % NZ * NX + block // NZ]
+            pieces += [jnp.where(left, part, zero), jnp.where(left, zero, part)]
+            wide = part.astype(F32)
+            square += jnp.sum((wide * wide).reshape(6, 8, 128), 0)
+        weight = weight_ref[:, start * 96 : (start + step) * 96]
+        total += jnp.dot(weight, jnp.concatenate(pieces, 0), preferred_element_type=F32)
+    square = jnp.broadcast_to(jnp.sum(square, 0, keepdims=True), (8, 128))
+    out_ref[:rows] = total[:, :64] + total[:, 64:]
+    out_ref[rows:] = square[:, :64] + square[:, 64:]
+
+
+def up_project(features, weight, after):
+    rows = weight.shape[0]
     return pl.pallas_call(
         up_kernel,
-        in_specs=[smem_spec(), vmem_spec(), vmem_spec(), any_spec()],
+        in_specs=[vmem_spec(), vmem_spec(), any_spec()],
         out_specs=vmem_spec(),
-        out_shape=shape((rows // 2, 64)),
-        scratch_shapes=[pltpu.VMEM((8, rows, width // 8), BF16), pltpu.SemaphoreType.DMA((8,))],
-        cost_estimate=cost(2 * 288 * 6144 * 128, 5 * MIB),
-        compiler_params=params(),
+        out_shape=shape((rows + 8, 64), F32),
+        cost_estimate=cost(2 * 576 * 3072 * 128, 5 * MIB),
+        compiler_params=params(16),
         name="up_project",
-    )(where, mine, theirs, in_hbm(weight))
+    )(features, weight, after)
 
 
 def down_kernel(mine_ref, theirs_ref, keep_ref, other_ref, *out_refs):
-    total = tn_dot(mine_ref[...], keep_ref[...]) + tn_dot(theirs_ref[...], other_ref[...])
+    rows = (mine_ref.shape[0] - 8) // 2
+    square = mine_ref[2 * rows : 2 * rows + 1] + theirs_ref[2 * rows : 2 * rows + 1]
+    scale = lax.rsqrt(square / 6144.0 + EPSILON_NORM)
+    total = jnp.zeros((64, keep_ref.shape[1]), F32)
+    for one, two, weight_ref in ((0, rows, keep_ref), (rows, 0, other_ref)):
+        product = (mine_ref[one : one + rows] + theirs_ref[two : two + rows]) * scale
+        hidden = (silu(product[: rows // 2]) * product[rows // 2 :]).astype(BF16)
+        total += tn_dot(hidden, weight_ref[...])
     total = total.astype(BF16)
-    half = NX // 2
+    width = NZ * 96
     for step in range(2):
 
         @pl.when(pl.program_id(0) == step)
         def _():
-            for column in range(half):
-                for block in range(NZ):
-                    start = (column * NZ + block) * 128
-                    out_refs[step * half + column][block] = total[:, start : start + 128].reshape(4, 16, 128)
+            for column in range(2):
+                out_refs[2 * step + column][...] = total[:, column * width : (column + 1) * width]
 
 
 def down_project(mine, theirs, keep, other):
-    hidden = mine.shape[0]
-    tokens = pl.BlockSpec((hidden, 64), lambda i: (0, 0))
-    weights = pl.BlockSpec((hidden, NX * NZ * 64), lambda i: (0, i))
+    hidden, width = keep.shape
+    products = pl.BlockSpec(mine.shape, lambda i: (0, 0))
+    weights = pl.BlockSpec((hidden, width // 2), lambda i: (0, i))
     return pl.pallas_call(
         down_kernel,
         grid=(2,),
-        in_specs=[tokens, tokens, weights, weights],
-        out_specs=[pl.BlockSpec((NZ, 4, 16, 128), lambda i: (0, 0, 0, 0))] * NX,
-        out_shape=[shape((NZ, 4, 16, 128))] * NX,
-        cost_estimate=cost(2 * 288 * 4096 * 64, 3 * MIB),
+        in_specs=[products, products, weights, weights],
+        out_specs=[pl.BlockSpec((64, NZ * 96), lambda i: (0, 0))] * NX,
+        out_shape=[shape((64, NZ * 96))] * NX,
+        cost_estimate=cost(2 * 288 * 3072 * 64, 3 * MIB),
         compiler_params=params(16),
         name="down_project",
     )(mine, theirs, keep, other)
@@ -426,8 +441,15 @@
 def merge_kernel(rest_ref, *refs):
     in_refs, out_ref = refs[:-1], refs[-1]
     out_ref[:, :, :32] = rest_ref[...]
-    for block in range(NZ):
-        out_ref[:, block, 32:] = sum(in_ref[block].astype(F32) for in_ref in in_refs).astype(BF16)
+    row = lax.broadcasted_iota(jnp.int32, (384, 512), 0)
+    lane = lax.broadcasted_iota(jnp.int32, (384, 512), 1)
+    spread = one_hot((row == lane // 128 * 96 + lane % 128) & (lane % 128 < 96))
+    for half in range(2):
+        total = sum(in_ref[:, half * 384 : half * 384 + 384].astype(F32) for in_ref in in_refs).astype(BF16)
+        total = jnp.dot(total, spread, preferred_element_type=F32).astype(BF16)
+        for block in range(4):
+            part = total[:, block * 128 : block * 128 + 128]
+            out_ref[:, half * 4 + block, 32:] = part.reshape(4, 16, 128)
 
 
 def merge(rest, parts):
@@ -463,17 +485,16 @@
 
 
 def gate_kernel(value_ref, after_ref, out_ref):
-    pass
+    out_ref[...] = value_ref[...]
 
 
 def gate(value, after):
     return pl.pallas_call(
         gate_kernel,
-        in_specs=[pl.BlockSpec(memory_space=pltpu.VMEM), any_spec()],
-        out_specs=pl.BlockSpec(memory_space=pltpu.VMEM),
+        in_specs=[vmem_spec(), any_spec()],
+        out_specs=vmem_spec(),
         out_shape=jax.ShapeDtypeStruct(value.shape, value.dtype),
-        input_output_aliases={0: 0},
-        compiler_params=params(1),
+        compiler_params=params(4),
         name="gate",
     )(value, after)
 
@@ -516,10 +537,11 @@
         rest = shifted(rest, "x")
         routed = routed_residual(summed, routed_hidden, rest[1], rest[3], keep_down)
     with jax.named_scope("expert"):
+        up = expert_up[0].transpose(1, 2, 0).reshape(288, 6144)
+        up, split = split_up(where, up, swap(up), routed)
         features = gate(lax.all_to_all(routed, ("z", "x"), 0, 0, tiled=True), rest[2])
-        up = expert_up[0].transpose(1, 2, 0).reshape(288, 6144)
-        expert_hidden = up_project(where, features, swap(features), up)
-        results = down_project(expert_hidden, swap(expert_hidden), keep_down, other_down)
+        products = up_project(features, up, swap(split))
+        results = down_project(products, swap(products), keep_down, other_down)
         rest = add_rest(rest)
         merged = merge(rest, shifted(results, "x")).reshape(32, 48, 128)
         returned = lax.all_to_all(merged, ("dp", "z"), 0, 0, tiled=True)

time: 124 us -> 121 us (0.976)
  waiting for transfers between devices: 34.4 us -> 23.1 us
  Pallas kernels: 23.3 us -> 27.4 us
  local copies, waits for them, and re-layouts: 3.31 us -> 6.95 us
    ppermute x9, waiting for transfers between devices: 21.1 us -> 11.3 us  [shifted(): lax.ppermute(blocks[far], axis, [(i, (i + far) % count) for i in range(co...]
    unnamed x46, local copies, waits for them, and re-layouts: 3.15 us -> 6.79 us
    pallas_call x3 -> x4, Pallas kernels: 5.06 us -> 8.51 us  [the longest x1 6.43 us: split_up(): pl.pallas_call(split_up_kernel, grid=(width // 1536,), in_specs=[smem_spe...]
    ppermute x5 -> x6, waiting for transfers between devices: 4.03 us -> 2.81 us  [swap(): return lax.ppermute(value, 'core', [(0, 1), (1, 0)])]
  transfers between devices with their start and end apart: 17 -> 18, of which waited for: 14 -> 12; matrix products, arithmetic and copies ran while one was open for 0% -> 0% of each run, Pallas kernels for 13% -> 20%
where the time goes in v4:
time: 121 us; the launch traced here: 119 us
  starting transfers between devices  40.2 us (33%)
  Pallas kernels  27.4 us (23%)
  waiting for transfers between devices  23.1 us (19%)
  blocking collectives  20 us (17%)
  local copies, waits for them, and re-layouts  6.95 us (6%)
    all_to_all x1, blocking collectives, per_device(): returned = lax.all_to_all(merged, ('dp', 'z'), 0, 0, tiled=True)  20 us
    ppermute x9, starting transfers between devices, shifted(): lax.ppermute(blocks[far], axis, [(i, (i + far) % count) for i in range(co...  15.1 us
    all_to_all x1, starting transfers between devices, per_device(): parts = lax.all_to_all(local, HEAD, 0, 0, tiled=True)  12.1 us
    ppermute x9, waiting for transfers between devices, shifted(): lax.ppermute(blocks[far], axis, [(i, (i + far) % count) for i in range(co...  11.3 us
    unnamed x46, local copies, waits for them, and re-layouts  6.79 us
    pallas_call x1, Pallas kernels, split_up(): pl.pallas_call(split_up_kernel, grid=(width // 1536,), in_specs=[smem_spe...  6.43 us
    all_to_all x1, starting transfers between devices, per_device(): lax.all_to_all(routed, ('z', 'x'), 0, 0, tiled=True)  6.22 us
    all_to_all x1, starting transfers between devices, per_device(): lax.all_to_all(partial.reshape(NZ * NX, 48, 128), ('z', 'x'), 0, 0, tiled...  6.04 us
  transfers between devices with their start and end apart: 18, of which 12 were waited for; matrix products, arithmetic and copies ran while one was open for 0% of the time, Pallas kernels for 20%

profile of v4, /device:TPU:2, one launch (start us, length us, event | category | flops | bytes accessed | tf_op | source)
XLA Modules:
  0.0 118.7 jit_solution(11595721522786677008)
XLA Ops:
  0.0 0.1 collective-permute-start.9
  0.1 0.5 collective-permute-start
  0.6 0.1 collective-permute-start.8
  0.7 2.7 %attend.1.after_ref = bf16[64,3,4,128]{3,2,1,0:T(4,128)(2,1)} custom-call(bf16[64,128,128]{2,1,0:T(8,128)(2,1)} %bitcast.38, bf16[64,3,4,128]{3,2,1,0:T(4,128)(2,1)} %bitcast.39), custom_call_target="tpu_custom_call" | custom-call | flops 16777216 | bytes 3145728 | tf_op jit(solution)/shard_map/attention/attend/pallas_call | solution.py:85
  3.4 12.1 %all-to-all-start = ((bf16[64,3,4,128]{3,2,1,0:T(4,128)(2,1)}), bf16[64,3,4,128]{3,2,1,0:T(4,128)(2,1)S(1)}, u32[]{:S(2)}, u32[]{:S(2)}) async-start(bf16[64,3,4,128]{3,2,1,0:T(4,128)(2,1)} %attend.1.after_ref), calls=%async_computation | async-start | bytes 393216 | tf_op jit(solution)/shard_map/attention/all_to_all | solution.py:520
  16.1 0.0 copy-done.21
  16.1 0.1 broadcast_in_dim.3
  16.2 0.1 reshape.52.row_ref
  16.3 0.1 copy.14
  16.4 0.1 copy.15
  16.6 0.6 route.1
  17.2 0.6 copy-done.10
  17.8 0.6 copy-done.12
  18.4 0.1 pad_add_fusion.where_ref
  18.5 0.0 collective-permute-done.theirs_ref
  18.5 2.9 %split_out.1 = (bf16[32,96,128]{2,1,0:T(8,128)(2,1)S(1)}, bf16[32,96,128]{2,1,0:T(8,128)(2,1)S(1)}) custom-call(s32[3]{0:T(128)S(1)} %pad_add_fusion.where_ref, bf16[128,6144]{1,0:T(8,128)(2,1)S(1)} %copy-done.3, bf16[128,6144]{1,0:T(8,128)(2,1)} %collective-permute-done.theirs_ref, bf16[64,3,4,128]{3,2,1,0:T(4,128)(2,1)} %attend.1.after_ref), custom_call_target="tpu_custom_call" | custom-call | flops 603979776 | bytes 3145728 | tf_op jit(solution)/shard_map/weights/split_out/pallas_call | solution.py:214
  21.4 4.3 %all-to-all-done.parts_ref = bf16[64,3,4,128]{3,2,1,0:T(4,128)(2,1)S(1)} async-done(((bf16[64,3,4,128]{3,2,1,0:T(4,128)(2,1)}), bf16[64,3,4,128]{3,2,1,0:T(4,128)(2,1)S(1)}, u32[]{:S(2)}, u32[]{:S(2)}) %all-to-all-start) | async-done | bytes 196640 | tf_op jit(solution)/shard_map/attention/all_to_all | solution.py:520
  25.7 1.1 decay_heads.1
  26.8 1.7 %collective-permute-start.1 = (bf16[68,4,128]{2,1,0:T(4,128)(2,1)S(1)}, bf16[68,4,128]{2,1,0:T(4,128)(2,1)S(1)}, u32[]{:S(2)}, u32[]{:S(2)}) collective-permute-start(bf16[68,4,128]{2,1,0:T(4,128)(2,1)S(1)} %get-tuple-element.32), channel_id=1, source_target_pairs={{0,64},{64,128},{128,192},{192,0},{1,65},{65,129},{129,193},{193,1... | collective-permute-start | bytes 208904 | tf_op jit(solution)/shard_map/heads/ppermute | solution.py:509
  28.4 2.9 %collective-permute-start.2 = (bf16[68,4,128]{2,1,0:T(4,128)(2,1)S(1)}, bf16[68,4,128]{2,1,0:T(4,128)(2,1)S(1)}, u32[]{:S(2)}, u32[]{:S(2)}) collective-permute-start(bf16[68,4,128]{2,1,0:T(4,128)(2,1)S(1)} %get-tuple-element.33), channel_id=1, source_target_pairs={{0,128},{64,192},{128,0},{192,64},{1,129},{65,193},{129,1},{193,65... | collective-permute-start | bytes 208904 | tf_op jit(solution)/shard_map/heads/ppermute | solution.py:509
  31.3 1.3 %collective-permute-start.3 = (bf16[68,4,128]{2,1,0:T(4,128)(2,1)S(1)}, bf16[68,4,128]{2,1,0:T(4,128)(2,1)S(1)}, u32[]{:S(2)}, u32[]{:S(2)}) collective-permute-start(bf16[68,4,128]{2,1,0:T(4,128)(2,1)S(1)} %get-tuple-element.34), channel_id=1, source_target_pairs={{0,192},{64,0},{128,64},{192,128},{1,193},{65,1},{129,65},{193,129... | collective-permute-start | bytes 208904 | tf_op jit(solution)/shard_map/heads/ppermute | solution.py:509
  32.7 0.0 collective-permute-done.1
  32.7 2.4 %collective-permute-done.2 = bf16[68,4,128]{2,1,0:T(4,128)(2,1)S(1)} collective-permute-done((bf16[68,4,128]{2,1,0:T(4,128)(2,1)S(1)}, bf16[68,4,128]{2,1,0:T(4,128)(2,1)S(1)}, u32[]{:S(2)}, u32[]{:S(2)}) %collective-permute-start.2) | collective-permute-done | bytes 69664 | tf_op jit(solution)/shard_map/heads/ppermute | solution.py:509
  35.1 0.6 collective-permute-done.3
  35.6 1.1 select.2
  36.8 0.6 copy-done.14
  37.4 0.0 collective-permute-start.4
  37.4 1.2 %collective-permute-done.4.theirs_ref = bf16[192,128]{1,0:T(8,128)(2,1)S(1)} collective-permute-done((bf16[192,128]{1,0:T(8,128)(2,1)S(1)}, bf16[192,128]{1,0:T(8,128)(2,1)S(1)}, u32[]{:S(2)}, u32[]{:S(2)}) %collective-permute-start.4) | collective-permute-done | bytes 49184 | tf_op jit(solution)/shard_map/heads/ppermute | solution.py:503
  38.6 1.4 %project.1.after_ref = bf16[8,4,48,128]{3,2,1,0:T(8,128)(2,1)} custom-call(bf16[32,96,128]{2,1,0:T(8,128)(2,1)S(1)} %get-tuple-element.28.after_ref.keep_ref, bf16[32,96,128]{2,1,0:T(8,128)(2,1)S(1)} %get-tuple-element.29.other_ref, bf16[192,128]{1,0:T(8,128)(2,1)S(1)} %get-tuple-element.35.mine_ref, bf16[192,128]{1,0:T(8,128)(2,1)S(1)} %collective-permute-done.4.theirs_ref), custom_call_target="tpu_custom_call" | custom-call | flops 201326592 | bytes 2097152 | tf_op jit(solution)/shard_map/projection/project/pallas_call | solution.py:301
  40.1 6.0 %all-to-all-start.1 = ((bf16[32,48,128]{2,1,0:T(8,128)(2,1)}), bf16[32,48,128]{2,1,0:T(8,128)(2,1)}, u32[]{:S(2)}, u32[]{:S(2)}) async-start(bf16[32,48,128]{2,1,0:T(8,128)(2,1)} %bitcast.14), calls=%async_computation.1 | async-start | bytes 786432 | tf_op jit(solution)/shard_map/projection/all_to_all | solution.py:534
  46.1 1.1 project_rest.1
  47.3 1.5 %collective-permute-start.5 = (bf16[8,96,128]{2,1,0:T(8,128)(2,1)S(1)}, bf16[8,96,128]{2,1,0:T(8,128)(2,1)S(1)}, u32[]{:S(2)}, u32[]{:S(2)}) collective-permute-start(bf16[8,96,128]{2,1,0:T(8,128)(2,1)S(1)} %get-tuple-element.37), channel_id=1, source_target_pairs={{0,16},{16,32},{32,48},{48,0},{1,17},{17,33},{33,49},{49,1},{2,18}... | collective-permute-start | bytes 589832 | tf_op jit(solution)/shard_map/projection/ppermute | solution.py:509
  48.8 0.6 collective-permute-start.7
  49.4 0.0 collective-permute-done.8.theirs_ref
  49.4 4.8 %split_down.1 = (bf16[144,3072]{1,0:T(8,128)(2,1)S(1)}, bf16[144,3072]{1,0:T(8,128)(2,1)S(1)}) custom-call(s32[3]{0:T(128)S(1)} %pad_add_fusion.where_ref, bf16[144,6144]{1,0:T(8,128)(2,1)S(1)} %bitcast.29, bf16[144,6144]{1,0:T(8,128)(2,1)} %collective-permute-done.8.theirs_ref, bf16[8,4,48,128]{3,2,1,0:T(8,128)(2,1)} %project.1.after_ref), custom_call_target="tpu_custom_call" | custom-call | flops 905969664 | bytes 4194304 | tf_op jit(solution)/shard_map/projection/split_down/pallas_call | solution.py:243
  54.2 0.9 copy-done.4
  55.1 1.6 %collective-permute-done.5.refs_1_.one_ref = bf16[8,96,128]{2,1,0:T(8,128)(2,1)S(1)} collective-permute-done((bf16[8,96,128]{2,1,0:T(8,128)(2,1)S(1)}, bf16[8,96,128]{2,1,0:T(8,128)(2,1)S(1)}, u32[]{:S(2)}, u32[]{:S(2)}) %collective-permute-start.5) | collective-permute-done | bytes 196640 | tf_op jit(solution)/shard_map/projection/ppermute | solution.py:509
  56.7 1.7 %collective-permute-done.7.refs_3_.two_ref = bf16[8,96,128]{2,1,0:T(8,128)(2,1)S(1)} collective-permute-done((bf16[8,96,128]{2,1,0:T(8,128)(2,1)S(1)}, bf16[8,96,128]{2,1,0:T(8,128)(2,1)S(1)}, u32[]{:S(2)}, u32[]{:S(2)}) %collective-permute-start.7) | collective-permute-done | bytes 196640 | tf_op jit(solution)/shard_map/projection/ppermute | solution.py:509
  58.4 2.2 %all-to-all-done.1.in_ref = bf16[32,48,128]{2,1,0:T(8,128)(2,1)} async-done(((bf16[32,48,128]{2,1,0:T(8,128)(2,1)}), bf16[32,48,128]{2,1,0:T(8,128)(2,1)}, u32[]{:S(2)}, u32[]{:S(2)}) %all-to-all-start.1) | async-done | bytes 393248 | tf_op jit(solution)/shard_map/projection/all_to_all | solution.py:534
  60.5 1.8 %routed_residual.1.after_ref = bf16[32,48,128]{2,1,0:T(8,128)(2,1)} custom-call(bf16[32,48,128]{2,1,0:T(8,128)(2,1)} %all-to-all-done.1.in_ref, f32[48,128]{1,0:T(8,128)S(1)} %copy-done.15, bf16[8,96,128]{2,1,0:T(8,128)(2,1)S(1)} %collective-permute-done.5.refs_1_.one_ref, bf16[8,96,128]{2,1,0:T(8,128)(2,1)S(1)} %collective-permute-done.7.refs_3_.two_ref, ...), custom_call_target="tpu_custom_call" | custom-call | flops 1048576 | bytes 1048576 | tf_op jit(solution)/shard_map/projection/routed_residual/pallas_call | solution.py:361
  62.4 6.2 %all-to-all-start.2 = ((bf16[32,48,128]{2,1,0:T(8,128)(2,1)}), bf16[32,48,128]{2,1,0:T(8,128)(2,1)S(1)}, u32[]{:S(2)}, u32[]{:S(2)}) async-start(bf16[32,48,128]{2,1,0:T(8,128)(2,1)} %routed_residual.1.after_ref), calls=%async_computation.2 | async-start | bytes 786432 | tf_op jit(solution)/shard_map/expert/all_to_all | solution.py:542
  68.6 2.3 %collective-permute-start.6 = (bf16[8,96,128]{2,1,0:T(8,128)(2,1)S(1)}, bf16[8,96,128]{2,1,0:T(8,128)(2,1)S(1)}, u32[]{:S(2)}, u32[]{:S(2)}) collective-permute-start(bf16[8,96,128]{2,1,0:T(8,128)(2,1)S(1)} %copy-done.17), channel_id=1, source_target_pairs={{0,32},{16,48},{32,0},{48,16},{1,33},{17,49},{33,1},{49,17},{2,34}... | collective-permute-start | bytes 589832 | tf_op jit(solution)/shard_map/projection/ppermute | solution.py:509
  70.9 0.0 collective-permute-done.9.theirs_ref
  70.9 6.4 %split_up.1 = (bf16[576,3072]{1,0:T(8,128)(2,1)S(1)}, f32[8,128]{1,0:T(8,128)S(1)}) custom-call(s32[3]{0:T(128)S(1)} %pad_add_fusion.where_ref, bf16[288,6144]{1,0:T(8,128)(2,1)} %bitcast.42, bf16[288,6144]{1,0:T(8,128)(2,1)} %collective-permute-done.9.theirs_ref, bf16[32,48,128]{2,1,0:T(8,128)(2,1)} %routed_residual.1.after_ref), custom_call_target="tpu_custom_call" | custom-call | flops 5435817984 | bytes 11534336 | tf_op jit(solution)/shard_map/expert/split_up/pallas_call | solution.py:273
  77.4 1.7 %copy-done = bf16[576,3072]{1,0:T(8,128)(2,1)} copy-done((bf16[576,3072]{1,0:T(8,128)(2,1)}, bf16[576,3072]{1,0:T(8,128)(2,1)S(1)}, u32[]{:S(2)}) %copy-start) | copy-done | bytes 3538968
  79.1 0.0 collective-permute-start.10
  79.1 0.4 collective-permute-done.6.refs_2_.after_ref
  79.5 2.5 %all-to-all-done.2.value_ref = bf16[32,48,128]{2,1,0:T(8,128)(2,1)S(1)} async-done(((bf16[32,48,128]{2,1,0:T(8,128)(2,1)}), bf16[32,48,128]{2,1,0:T(8,128)(2,1)S(1)}, u32[]{:S(2)}, u32[]{:S(2)}) %all-to-all-start.2) | async-done | bytes 393248 | tf_op jit(solution)/shard_map/expert/all_to_all | solution.py:542
  82.1 0.0 collective-permute-done.10.after_ref
  82.1 2.0 %copy-done.1 = bf16[576,3072]{1,0:T(8,128)(2,1)S(1)} copy-done((bf16[576,3072]{1,0:T(8,128)(2,1)S(1)}, bf16[576,3072]{1,0:T(8,128)(2,1)}, u32[]{:S(2)}) %copy-start.1) | copy-done | bytes 3538968
  84.1 1.1 up_project.1.mine_ref
  85.3 0.1 collective-permute-start.11
  85.4 1.6 %collective-permute-done.11.theirs_ref = f32[584,64]{1,0:T(8,128)S(1)} collective-permute-done((f32[584,64]{1,0:T(8,128)S(1)}, f32[584,64]{1,0:T(8,128)S(1)}, u32[]{:S(2)}, u32[]{:S(2)}) %collective-permute-start.11) | collective-permute-done | bytes 149536 | tf_op jit(solution)/shard_map/expert/ppermute | solution.py:503
  86.9 0.9 down_project.1
  87.9 1.5 %collective-permute-start.12 = (bf16[64,768]{1,0:T(8,128)(2,1)S(1)}, bf16[64,768]{1,0:T(8,128)(2,1)S(1)}, u32[]{:S(2)}, u32[]{:S(2)}) collective-permute-start(bf16[64,768]{1,0:T(8,128)(2,1)S(1)} %get-tuple-element.46), channel_id=1, source_target_pairs={{0,16},{16,32},{32,48},{48,0},{1,17},{17,33},{33,49},{49,1},{2,18}... | collective-permute-start | bytes 294920 | tf_op jit(solution)/shard_map/expert/ppermute | solution.py:509
  89.4 2.2 %collective-permute-start.13 = (bf16[64,768]{1,0:T(8,128)(2,1)S(1)}, bf16[64,768]{1,0:T(8,128)(2,1)S(1)}, u32[]{:S(2)}, u32[]{:S(2)}) collective-permute-start(bf16[64,768]{1,0:T(8,128)(2,1)S(1)} %get-tuple-element.47), channel_id=1, source_target_pairs={{0,32},{16,48},{32,0},{48,16},{1,33},{17,49},{33,1},{49,17},{2,34}... | collective-permute-start | bytes 294920 | tf_op jit(solution)/shard_map/expert/ppermute | solution.py:509
  91.6 1.1 collective-permute-start.14
  92.6 0.2 add_rest.1.rest_ref
  92.8 0.0 collective-permute-done.12.refs_1_
  92.8 3.7 %collective-permute-done.13.refs_2_ = bf16[64,768]{1,0:T(8,128)(2,1)S(1)} collective-permute-done((bf16[64,768]{1,0:T(8,128)(2,1)S(1)}, bf16[64,768]{1,0:T(8,128)(2,1)S(1)}, u32[]{:S(2)}, u32[]{:S(2)}) %collective-permute-start.13) | collective-permute-done | bytes 98336 | tf_op jit(solution)/shard_map/expert/ppermute | solution.py:509
  96.5 1.0 collective-permute-done.14.refs_3_
  97.6 0.3 merge.1
  97.9 20.0 %all_to_all.20 = bf16[32,48,128]{2,1,0:T(8,128)(2,1)S(1)} all-to-all(bf16[32,48,128]{2,1,0:T(8,128)(2,1)S(1)} %bitcast.31), channel_id=1, replica_groups=mesh['dp'=4,'x'=4,'z'=8,'core'=2] {'dp','z'}, dimensions={0} | all-to-all | bytes 786432 | tf_op jit(solution)/shard_map/expert/all_to_all | solution.py:547
  117.9 0.8 combine.1
  (39 shorter events, 0.1 us)
Async XLA Ops:
  0.0 18.5 %copy-start.3 = (bf16[128,6144]{1,0:T(8,128)(2,1)S(1)}, bf16[128,6144]{1,0:T(8,128)(2,1)}, u32[]{:S(2)}) copy-start(bf16[128,6144]{1,0:T(8,128)(2,1)} %mine_ref.1) | copy-start | bytes 4718596
  0.0 16.1 %copy-start.21 = (s32[32]{0:T(128)S(1)}, s32[32]{0:T(128)}, u32[]{:S(2)}) copy-start(s32[32]{0:T(128)} %param.10) | copy-start | bytes 388
  0.0 16.3 %copy-start.19 = (s32[32,4,2]{0,2,1:T(2,128)S(1)}, s32[32,4,2]{0,2,1:T(2,128)}, u32[]{:S(2)}) copy-start(s32[32,4,2]{0,2,1:T(2,128)} %param.16) | copy-start | bytes 3076
  0.0 16.4 %copy-start.20 = (f32[32,4,2]{0,2,1:T(2,128)S(1)}, f32[32,4,2]{0,2,1:T(2,128)}, u32[]{:S(2)}) copy-start(f32[32,4,2]{0,2,1:T(2,128)} %param.17) | copy-start | bytes 3076
  0.0 16.5 %copy-start.18 = (bf16[96,32,4]{0,2,1:T(4,128)(2,1)S(1)}, bf16[96,32,4]{0,2,1:T(4,128)(2,1)}, u32[]{:S(2)}) copy-start(bf16[96,32,4]{0,2,1:T(4,128)(2,1)} %param.15) | copy-start | bytes 73732
  0.0 70.9 %collective-permute-start.9 = (bf16[288,6144]{1,0:T(8,128)(2,1)}, bf16[288,6144]{1,0:T(8,128)(2,1)}, u32[]{:S(2)}, u32[]{:S(2)}) collective-permute-start(bf16[288,6144]{1,0:T(8,128)(2,1)} %bitcast.41), channel_id=1, source_target_pairs={{0,1},{1,0},{2,3},{3,2},{4,5},{5,4},{6,7},{7,6},{8,9},{9,8},{10,11... | collective-permute-start | bytes 10616840 | tf_op jit(solution)/shard_map/expert/ppermute | solution.py:503
  0.1 18.4 %collective-permute-start = (bf16[128,6144]{1,0:T(8,128)(2,1)}, bf16[128,6144]{1,0:T(8,128)(2,1)}, u32[]{:S(2)}, u32[]{:S(2)}) collective-permute-start(bf16[128,6144]{1,0:T(8,128)(2,1)} %mine_ref.1), channel_id=1, source_target_pairs={{0,1},{1,0},{2,3},{3,2},{4,5},{5,4},{6,7},{7,6},{8,9},{9,8},{10,11... | collective-permute-start | bytes 4718600 | tf_op jit(solution)/shard_map/weights/ppermute | solution.py:503
  0.6 48.7 %collective-permute-start.8 = (bf16[144,6144]{1,0:T(8,128)(2,1)}, bf16[144,6144]{1,0:T(8,128)(2,1)}, u32[]{:S(2)}, u32[]{:S(2)}) collective-permute-start(bf16[144,6144]{1,0:T(8,128)(2,1)} %bitcast.28), channel_id=1, source_target_pairs={{0,1},{1,0},{2,3},{3,2},{4,5},{5,4},{6,7},{7,6},{8,9},{9,8},{10,11... | collective-permute-start | bytes 5308424 | tf_op jit(solution)/shard_map/projection/ppermute | solution.py:503
  3.4 22.3 %all-to-all-start = ((bf16[64,3,4,128]{3,2,1,0:T(4,128)(2,1)}), bf16[64,3,4,128]{3,2,1,0:T(4,128)(2,1)S(1)}, u32[]{:S(2)}, u32[]{:S(2)}) async-start(bf16[64,3,4,128]{3,2,1,0:T(4,128)(2,1)} %attend.1.after_ref), calls=%async_computation | async-start | bytes 393216 | tf_op jit(solution)/shard_map/attention/all_to_all | solution.py:520
  16.6 1.9 %copy-start.6 = (bf16[128,128]{1,0:T(8,128)(2,1)}, bf16[128,128]{1,0:T(8,128)(2,1)S(1)}, u32[]{:S(2)}) copy-start(bf16[128,128]{1,0:T(8,128)(2,1)S(1)} %pad.4.hidden_ref) | copy-start | bytes 98308
  17.2 0.6 copy-start.10
  17.8 0.6 copy-start.12
  26.8 5.9 %collective-permute-start.1 = (bf16[68,4,128]{2,1,0:T(4,128)(2,1)S(1)}, bf16[68,4,128]{2,1,0:T(4,128)(2,1)S(1)}, u32[]{:S(2)}, u32[]{:S(2)}) collective-permute-start(bf16[68,4,128]{2,1,0:T(4,128)(2,1)S(1)} %get-tuple-element.32), channel_id=1, source_target_pairs={{0,64},{64,128},{128,192},{192,0},{1,65},{65,129},{129,193},{193,1... | collective-permute-start | bytes 208904 | tf_op jit(solution)/shard_map/heads/ppermute | solution.py:509
  28.4 6.6 %collective-permute-start.2 = (bf16[68,4,128]{2,1,0:T(4,128)(2,1)S(1)}, bf16[68,4,128]{2,1,0:T(4,128)(2,1)S(1)}, u32[]{:S(2)}, u32[]{:S(2)}) collective-permute-start(bf16[68,4,128]{2,1,0:T(4,128)(2,1)S(1)} %get-tuple-element.33), channel_id=1, source_target_pairs={{0,128},{64,192},{128,0},{192,64},{1,129},{65,193},{129,1},{193,65... | collective-permute-start | bytes 208904 | tf_op jit(solution)/shard_map/heads/ppermute | solution.py:509
  31.3 4.3 %collective-permute-start.3 = (bf16[68,4,128]{2,1,0:T(4,128)(2,1)S(1)}, bf16[68,4,128]{2,1,0:T(4,128)(2,1)S(1)}, u32[]{:S(2)}, u32[]{:S(2)}) collective-permute-start(bf16[68,4,128]{2,1,0:T(4,128)(2,1)S(1)} %get-tuple-element.34), channel_id=1, source_target_pairs={{0,192},{64,0},{128,64},{192,128},{1,193},{65,1},{129,65},{193,129... | collective-permute-start | bytes 208904 | tf_op jit(solution)/shard_map/heads/ppermute | solution.py:509
  36.8 0.6 copy-start.14
  37.4 1.2 %collective-permute-start.4 = (bf16[192,128]{1,0:T(8,128)(2,1)S(1)}, bf16[192,128]{1,0:T(8,128)(2,1)S(1)}, u32[]{:S(2)}, u32[]{:S(2)}) collective-permute-start(bf16[192,128]{1,0:T(8,128)(2,1)S(1)} %get-tuple-element.35.mine_ref), channel_id=1, source_target_pairs={{0,1},{1,0},{2,3},{3,2},{4,5},{5,4},{6,7},{7,6},{8,9},{9,8},{10,11... | collective-permute-start | bytes 147464 | tf_op jit(solution)/shard_map/heads/ppermute | solution.py:503
  38.6 10.7 %copy-start.2 = (bf16[1,144,6144]{2,1,0:T(8,128)(2,1)S(1)}, bf16[1,144,6144]{2,1,0:T(8,128)(2,1)}, u32[]{:S(2)}) copy-start(bf16[1,144,6144]{2,1,0:T(8,128)(2,1)} %param.19) | copy-start | bytes 5308420
  40.1 20.4 %all-to-all-start.1 = ((bf16[32,48,128]{2,1,0:T(8,128)(2,1)}), bf16[32,48,128]{2,1,0:T(8,128)(2,1)}, u32[]{:S(2)}, u32[]{:S(2)}) async-start(bf16[32,48,128]{2,1,0:T(8,128)(2,1)} %bitcast.14), calls=%async_computation.1 | async-start | bytes 786432 | tf_op jit(solution)/shard_map/projection/all_to_all | solution.py:534
  47.2 9.4 %copy-start.8 = (bf16[8,96,128]{2,1,0:T(8,128)(2,1)}, bf16[8,96,128]{2,1,0:T(8,128)(2,1)S(1)}, u32[]{:S(2)}) copy-start(bf16[8,96,128]{2,1,0:T(8,128)(2,1)S(1)} %get-tuple-element.36.refs_0_) | copy-start | bytes 589828
  47.2 9.4 %copy-start.16 = (bf16[8,96,128]{2,1,0:T(8,128)(2,1)}, bf16[8,96,128]{2,1,0:T(8,128)(2,1)S(1)}, u32[]{:S(2)}) copy-start(bf16[8,96,128]{2,1,0:T(8,128)(2,1)S(1)} %get-tuple-element.38) | copy-start | bytes 589828
  47.3 13.3 %copy-start.15 = (f32[48,128]{1,0:T(8,128)S(1)}, f32[48,128]{1,0:T(8,128)}, u32[]{:S(2)}) copy-start(f32[48,128]{1,0:T(8,128)} %copy-done.14) | copy-start | bytes 73732
  47.3 9.4 %collective-permute-start.5 = (bf16[8,96,128]{2,1,0:T(8,128)(2,1)S(1)}, bf16[8,96,128]{2,1,0:T(8,128)(2,1)S(1)}, u32[]{:S(2)}, u32[]{:S(2)}) collective-permute-start(bf16[8,96,128]{2,1,0:T(8,128)(2,1)S(1)} %get-tuple-element.37), channel_id=1, source_target_pairs={{0,16},{16,32},{32,48},{48,0},{1,17},{17,33},{33,49},{49,1},{2,18}... | collective-permute-start | bytes 589832 | tf_op jit(solution)/shard_map/projection/ppermute | solution.py:509
  48.8 9.6 %collective-permute-start.7 = (bf16[8,96,128]{2,1,0:T(8,128)(2,1)S(1)}, bf16[8,96,128]{2,1,0:T(8,128)(2,1)S(1)}, u32[]{:S(2)}, u32[]{:S(2)}) collective-permute-start(bf16[8,96,128]{2,1,0:T(8,128)(2,1)S(1)} %get-tuple-element.39), channel_id=1, source_target_pairs={{0,48},{16,0},{32,16},{48,32},{1,49},{17,1},{33,17},{49,33},{2,50}... | collective-permute-start | bytes 589832 | tf_op jit(solution)/shard_map/projection/ppermute | solution.py:509
  54.2 0.9 copy-start.4
  58.4 10.2 %copy-start.17 = (bf16[8,96,128]{2,1,0:T(8,128)(2,1)S(1)}, bf16[8,96,128]{2,1,0:T(8,128)(2,1)}, u32[]{:S(2)}) copy-start(bf16[8,96,128]{2,1,0:T(8,128)(2,1)} %copy-done.16) | copy-start | bytes 589828
  62.4 19.7 %all-to-all-start.2 = ((bf16[32,48,128]{2,1,0:T(8,128)(2,1)}), bf16[32,48,128]{2,1,0:T(8,128)(2,1)S(1)}, u32[]{:S(2)}, u32[]{:S(2)}) async-start(bf16[32,48,128]{2,1,0:T(8,128)(2,1)} %routed_residual.1.after_ref), calls=%async_computation.2 | async-start | bytes 786432 | tf_op jit(solution)/shard_map/expert/all_to_all | solution.py:542
  68.6 10.9 %collective-permute-start.6 = (bf16[8,96,128]{2,1,0:T(8,128)(2,1)S(1)}, bf16[8,96,128]{2,1,0:T(8,128)(2,1)S(1)}, u32[]{:S(2)}, u32[]{:S(2)}) collective-permute-start(bf16[8,96,128]{2,1,0:T(8,128)(2,1)S(1)} %copy-done.17), channel_id=1, source_target_pairs={{0,32},{16,48},{32,0},{48,16},{1,33},{17,49},{33,1},{49,17},{2,34}... | collective-permute-start | bytes 589832 | tf_op jit(solution)/shard_map/projection/ppermute | solution.py:509
  77.4 1.8 %copy-start = (bf16[576,3072]{1,0:T(8,128)(2,1)}, bf16[576,3072]{1,0:T(8,128)(2,1)S(1)}, u32[]{:S(2)}) copy-start(bf16[576,3072]{1,0:T(8,128)(2,1)S(1)} %get-tuple-element.42.weight_ref) | copy-start | bytes 10616836
  79.1 2.9 %collective-permute-start.10 = (f32[8,128]{1,0:T(8,128)S(1)}, f32[8,128]{1,0:T(8,128)S(1)}, u32[]{:S(2)}, u32[]{:S(2)}) collective-permute-start(f32[8,128]{1,0:T(8,128)S(1)} %get-tuple-element.43), channel_id=1, source_target_pairs={{0,1},{1,0},{2,3},{3,2},{4,5},{5,4},{6,7},{7,6},{8,9},{9,8},{10,11... | collective-permute-start | bytes 12296 | tf_op jit(solution)/shard_map/expert/ppermute | solution.py:503
  82.1 2.0 %copy-start.1 = (bf16[576,3072]{1,0:T(8,128)(2,1)S(1)}, bf16[576,3072]{1,0:T(8,128)(2,1)}, u32[]{:S(2)}) copy-start(bf16[576,3072]{1,0:T(8,128)(2,1)} %copy-done) | copy-start | bytes 10616836
  84.1 2.8 %copy-start.5 = (bf16[144,3072]{1,0:T(8,128)(2,1)S(1)}, bf16[144,3072]{1,0:T(8,128)(2,1)}, u32[]{:S(2)}) copy-start(bf16[144,3072]{1,0:T(8,128)(2,1)} %copy-done.4) | copy-start | bytes 2654212
  85.2 7.4 %copy-start.9 = (bf16[8,96,128]{2,1,0:T(8,128)(2,1)S(1)}, bf16[8,96,128]{2,1,0:T(8,128)(2,1)}, u32[]{:S(2)}) copy-start(bf16[8,96,128]{2,1,0:T(8,128)(2,1)} %copy-done.8) | copy-start | bytes 589828
  85.3 1.7 %collective-permute-start.11 = (f32[584,64]{1,0:T(8,128)S(1)}, f32[584,64]{1,0:T(8,128)S(1)}, u32[]{:S(2)}, u32[]{:S(2)}) collective-permute-start(f32[584,64]{1,0:T(8,128)S(1)} %up_project.1.mine_ref), channel_id=1, source_target_pairs={{0,1},{1,0},{2,3},{3,2},{4,5},{5,4},{6,7},{7,6},{8,9},{9,8},{10,11... | collective-permute-start | bytes 448520 | tf_op jit(solution)/shard_map/expert/ppermute | solution.py:503
  86.9 31.0 %copy-start.7 = (bf16[128,128]{1,0:T(8,128)(2,1)S(1)}, bf16[128,128]{1,0:T(8,128)(2,1)}, u32[]{:S(2)}) copy-start(bf16[128,128]{1,0:T(8,128)(2,1)} %copy-done.6) | copy-start | bytes 98308
  86.9 31.0 %copy-start.11 = (f32[128,1]{1,0:T(8,128)S(1)}, f32[128,1]{1,0:T(8,128)}, u32[]{:S(2)}) copy-start(f32[128,1]{1,0:T(8,128)} %copy-done.10) | copy-start | bytes 1540
  86.9 31.0 %copy-start.13 = (bf16[128,128]{1,0:T(8,128)(2,1)S(1)}, bf16[128,128]{1,0:T(8,128)(2,1)}, u32[]{:S(2)}) copy-start(bf16[128,128]{1,0:T(8,128)(2,1)} %copy-done.12) | copy-start | bytes 98308
  87.9 5.0 %collective-permute-start.12 = (bf16[64,768]{1,0:T(8,128)(2,1)S(1)}, bf16[64,768]{1,0:T(8,128)(2,1)S(1)}, u32[]{:S(2)}, u32[]{:S(2)}) collective-permute-start(bf16[64,768]{1,0:T(8,128)(2,1)S(1)} %get-tuple-element.46), channel_id=1, source_target_pairs={{0,16},{16,32},{32,48},{48,0},{1,17},{17,33},{33,49},{49,1},{2,18}... | collective-permute-start | bytes 294920 | tf_op jit(solution)/shard_map/expert/ppermute | solution.py:509
  89.4 7.1 %collective-permute-start.13 = (bf16[64,768]{1,0:T(8,128)(2,1)S(1)}, bf16[64,768]{1,0:T(8,128)(2,1)S(1)}, u32[]{:S(2)}, u32[]{:S(2)}) collective-permute-start(bf16[64,768]{1,0:T(8,128)(2,1)S(1)} %get-tuple-element.47), channel_id=1, source_target_pairs={{0,32},{16,48},{32,0},{48,16},{1,33},{17,49},{33,1},{49,17},{2,34}... | collective-permute-start | bytes 294920 | tf_op jit(solution)/shard_map/expert/ppermute | solution.py:509
  91.6 6.0 %collective-permute-start.14 = (bf16[64,768]{1,0:T(8,128)(2,1)S(1)}, bf16[64,768]{1,0:T(8,128)(2,1)S(1)}, u32[]{:S(2)}, u32[]{:S(2)}) collective-permute-start(bf16[64,768]{1,0:T(8,128)(2,1)S(1)} %get-tuple-element.48), channel_id=1, source_target_pairs={{0,48},{16,0},{32,16},{48,32},{1,49},{17,1},{33,17},{49,33},{2,50}... | collective-permute-start | bytes 294920 | tf_op jit(solution)/shard_map/expert/ppermute | solution.py:509

commit v5 on v4

--- a/solution.py
+++ b/solution.py
@@ -351,18 +351,28 @@
     )(*parts)
 
 
-def residual_kernel(in_ref, hidden_ref, one_ref, two_ref, three_ref, send_ref):
+def residual_kernel(in_ref, hidden_ref, one_ref, two_ref, three_ref, send_ref, held_ref, sems):
     routed = (jnp.sum(in_ref[...].astype(F32), 0) + hidden_ref[...]).astype(BF16)
-    for copy in range(send_ref.shape[0]):
-        send_ref[copy] = routed
+    span = held_ref.shape[0]
+    for copy in range(span):
+        held_ref[copy] = routed
+    copies = [
+        pltpu.make_async_copy(held_ref, send_ref.at[pl.ds(index * span, span)], sems.at[index])
+        for index in range(NX * NZ // span)
+    ]
+    for copy in copies:
+        copy.start()
+    for copy in copies:
+        copy.wait()
 
 
 def routed_residual(parts, hidden, *after):
     return pl.pallas_call(
         residual_kernel,
         in_specs=[vmem_spec()] * 2 + [any_spec()] * 3,
-        out_specs=vmem_spec(),
+        out_specs=any_spec(),
         out_shape=shape((NX * NZ, 48, 128)),
+        scratch_shapes=[pltpu.VMEM((4, 48, 128), BF16), pltpu.SemaphoreType.DMA((8,))],
         cost_estimate=cost(MIB, MIB),
         compiler_params=params(),
         name="routed_residual",

time: 121 us -> 121 us (level)
  no operation moved by 1% of the time
where the time goes in v5:
time: 121 us; the launch traced here: 119 us
  starting transfers between devices  40.2 us (33%)
  Pallas kernels  27.5 us (23%)
  waiting for transfers between devices  23.1 us (19%)
  blocking collectives  20 us (17%)
  local copies, waits for them, and re-layouts  6.95 us (6%)
    all_to_all x1, blocking collectives, per_device(): returned = lax.all_to_all(merged, ('dp', 'z'), 0, 0, tiled=True)  20 us
    ppermute x9, starting transfers between devices, shifted(): lax.ppermute(blocks[far], axis, [(i, (i + far) % count) for i in range(co...  15.1 us
    all_to_all x1, starting transfers between devices, per_device(): parts = lax.all_to_all(local, HEAD, 0, 0, tiled=True)  12.1 us
    ppermute x9, waiting for transfers between devices, shifted(): lax.ppermute(blocks[far], axis, [(i, (i + far) % count) for i in range(co...  11.3 us
    unnamed x46, local copies, waits for them, and re-layouts  6.79 us
    pallas_call x1, Pallas kernels, split_up(): pl.pallas_call(split_up_kernel, grid=(width // 1536,), in_specs=[smem_spe...  6.43 us
    all_to_all x1, starting transfers between devices, per_device(): lax.all_to_all(routed, ('z', 'x'), 0, 0, tiled=True)  6.23 us
    all_to_all x1, starting transfers between devices, per_device(): lax.all_to_all(partial.reshape(NZ * NX, 48, 128), ('z', 'x'), 0, 0, tiled...  6.04 us
  transfers between devices with their start and end apart: 18, of which 12 were waited for; matrix products, arithmetic and copies ran while one was open for 0% of the time, Pallas kernels for 20%

profile of v5, /device:TPU:2, one launch (start us, length us, event | category | flops | bytes accessed | tf_op | source)
XLA Modules:
  0.0 118.8 jit_solution(12094611409606697996)
XLA Ops:
  0.0 0.1 collective-permute-start.9
  0.1 0.5 collective-permute-start
  0.6 0.1 collective-permute-start.8
  0.7 2.7 %attend.1.after_ref = bf16[64,3,4,128]{3,2,1,0:T(4,128)(2,1)} custom-call(bf16[64,128,128]{2,1,0:T(8,128)(2,1)} %bitcast.38, bf16[64,3,4,128]{3,2,1,0:T(4,128)(2,1)} %bitcast.39), custom_call_target="tpu_custom_call" | custom-call | flops 16777216 | bytes 3145728 | tf_op jit(solution)/shard_map/attention/attend/pallas_call | solution.py:85
  3.4 12.1 %all-to-all-start = ((bf16[64,3,4,128]{3,2,1,0:T(4,128)(2,1)}), bf16[64,3,4,128]{3,2,1,0:T(4,128)(2,1)S(1)}, u32[]{:S(2)}, u32[]{:S(2)}) async-start(bf16[64,3,4,128]{3,2,1,0:T(4,128)(2,1)} %attend.1.after_ref), calls=%async_computation | async-start | bytes 393216 | tf_op jit(solution)/shard_map/attention/all_to_all | solution.py:530
  16.1 0.1 broadcast_in_dim.3
  16.2 0.1 reshape.52.row_ref
  16.3 0.0 copy-done.19
  16.3 0.1 copy.14
  16.4 0.1 copy.15
  16.6 0.6 route.1
  17.2 0.6 copy-done.10
  17.8 0.6 copy-done.12
  18.4 0.1 pad_add_fusion.where_ref
  18.5 0.0 collective-permute-done.theirs_ref
  18.5 2.9 %split_out.1 = (bf16[32,96,128]{2,1,0:T(8,128)(2,1)S(1)}, bf16[32,96,128]{2,1,0:T(8,128)(2,1)S(1)}) custom-call(s32[3]{0:T(128)S(1)} %pad_add_fusion.where_ref, bf16[128,6144]{1,0:T(8,128)(2,1)S(1)} %copy-done.3, bf16[128,6144]{1,0:T(8,128)(2,1)} %collective-permute-done.theirs_ref, bf16[64,3,4,128]{3,2,1,0:T(4,128)(2,1)} %attend.1.after_ref), custom_call_target="tpu_custom_call" | custom-call | flops 603979776 | bytes 3145728 | tf_op jit(solution)/shard_map/weights/split_out/pallas_call | solution.py:214
  21.4 4.3 %all-to-all-done.parts_ref = bf16[64,3,4,128]{3,2,1,0:T(4,128)(2,1)S(1)} async-done(((bf16[64,3,4,128]{3,2,1,0:T(4,128)(2,1)}), bf16[64,3,4,128]{3,2,1,0:T(4,128)(2,1)S(1)}, u32[]{:S(2)}, u32[]{:S(2)}) %all-to-all-start) | async-done | bytes 196640 | tf_op jit(solution)/shard_map/attention/all_to_all | solution.py:530
  25.7 1.1 decay_heads.1
  26.8 1.7 %collective-permute-start.1 = (bf16[68,4,128]{2,1,0:T(4,128)(2,1)S(1)}, bf16[68,4,128]{2,1,0:T(4,128)(2,1)S(1)}, u32[]{:S(2)}, u32[]{:S(2)}) collective-permute-start(bf16[68,4,128]{2,1,0:T(4,128)(2,1)S(1)} %get-tuple-element.32), channel_id=1, source_target_pairs={{0,64},{64,128},{128,192},{192,0},{1,65},{65,129},{129,193},{193,1... | collective-permute-start | bytes 208904 | tf_op jit(solution)/shard_map/heads/ppermute | solution.py:519
  28.4 2.9 %collective-permute-start.2 = (bf16[68,4,128]{2,1,0:T(4,128)(2,1)S(1)}, bf16[68,4,128]{2,1,0:T(4,128)(2,1)S(1)}, u32[]{:S(2)}, u32[]{:S(2)}) collective-permute-start(bf16[68,4,128]{2,1,0:T(4,128)(2,1)S(1)} %get-tuple-element.33), channel_id=1, source_target_pairs={{0,128},{64,192},{128,0},{192,64},{1,129},{65,193},{129,1},{193,65... | collective-permute-start | bytes 208904 | tf_op jit(solution)/shard_map/heads/ppermute | solution.py:519
  31.3 1.3 %collective-permute-start.3 = (bf16[68,4,128]{2,1,0:T(4,128)(2,1)S(1)}, bf16[68,4,128]{2,1,0:T(4,128)(2,1)S(1)}, u32[]{:S(2)}, u32[]{:S(2)}) collective-permute-start(bf16[68,4,128]{2,1,0:T(4,128)(2,1)S(1)} %get-tuple-element.34), channel_id=1, source_target_pairs={{0,192},{64,0},{128,64},{192,128},{1,193},{65,1},{129,65},{193,129... | collective-permute-start | bytes 208904 | tf_op jit(solution)/shard_map/heads/ppermute | solution.py:519
  32.7 0.0 collective-permute-done.1
  32.7 2.4 %collective-permute-done.2 = bf16[68,4,128]{2,1,0:T(4,128)(2,1)S(1)} collective-permute-done((bf16[68,4,128]{2,1,0:T(4,128)(2,1)S(1)}, bf16[68,4,128]{2,1,0:T(4,128)(2,1)S(1)}, u32[]{:S(2)}, u32[]{:S(2)}) %collective-permute-start.2) | collective-permute-done | bytes 69664 | tf_op jit(solution)/shard_map/heads/ppermute | solution.py:519
  35.1 0.6 collective-permute-done.3
  35.6 1.1 select.2
  36.8 0.6 copy-done.14
  37.4 0.0 collective-permute-start.4
  37.4 1.2 %collective-permute-done.4.theirs_ref = bf16[192,128]{1,0:T(8,128)(2,1)S(1)} collective-permute-done((bf16[192,128]{1,0:T(8,128)(2,1)S(1)}, bf16[192,128]{1,0:T(8,128)(2,1)S(1)}, u32[]{:S(2)}, u32[]{:S(2)}) %collective-permute-start.4) | collective-permute-done | bytes 49184 | tf_op jit(solution)/shard_map/heads/ppermute | solution.py:513
  38.6 1.4 %project.1.after_ref = bf16[8,4,48,128]{3,2,1,0:T(8,128)(2,1)} custom-call(bf16[32,96,128]{2,1,0:T(8,128)(2,1)S(1)} %get-tuple-element.28.after_ref.keep_ref, bf16[32,96,128]{2,1,0:T(8,128)(2,1)S(1)} %get-tuple-element.29.other_ref, bf16[192,128]{1,0:T(8,128)(2,1)S(1)} %get-tuple-element.35.mine_ref, bf16[192,128]{1,0:T(8,128)(2,1)S(1)} %collective-permute-done.4.theirs_ref), custom_call_target="tpu_custom_call" | custom-call | flops 201326592 | bytes 2097152 | tf_op jit(solution)/shard_map/projection/project/pallas_call | solution.py:301
  40.1 6.0 %all-to-all-start.1 = ((bf16[32,48,128]{2,1,0:T(8,128)(2,1)}), bf16[32,48,128]{2,1,0:T(8,128)(2,1)}, u32[]{:S(2)}, u32[]{:S(2)}) async-start(bf16[32,48,128]{2,1,0:T(8,128)(2,1)} %bitcast.14), calls=%async_computation.1 | async-start | bytes 786432 | tf_op jit(solution)/shard_map/projection/all_to_all | solution.py:544
  46.1 1.1 project_rest.1
  47.3 1.5 %collective-permute-start.5 = (bf16[8,96,128]{2,1,0:T(8,128)(2,1)S(1)}, bf16[8,96,128]{2,1,0:T(8,128)(2,1)S(1)}, u32[]{:S(2)}, u32[]{:S(2)}) collective-permute-start(bf16[8,96,128]{2,1,0:T(8,128)(2,1)S(1)} %get-tuple-element.37), channel_id=1, source_target_pairs={{0,16},{16,32},{32,48},{48,0},{1,17},{17,33},{33,49},{49,1},{2,18}... | collective-permute-start | bytes 589832 | tf_op jit(solution)/shard_map/projection/ppermute | solution.py:519
  48.8 0.6 collective-permute-start.7
  49.4 0.0 collective-permute-done.8.theirs_ref
  49.4 4.8 %split_down.1 = (bf16[144,3072]{1,0:T(8,128)(2,1)S(1)}, bf16[144,3072]{1,0:T(8,128)(2,1)S(1)}) custom-call(s32[3]{0:T(128)S(1)} %pad_add_fusion.where_ref, bf16[144,6144]{1,0:T(8,128)(2,1)S(1)} %bitcast.29, bf16[144,6144]{1,0:T(8,128)(2,1)} %collective-permute-done.8.theirs_ref, bf16[8,4,48,128]{3,2,1,0:T(8,128)(2,1)} %project.1.after_ref), custom_call_target="tpu_custom_call" | custom-call | flops 905969664 | bytes 4194304 | tf_op jit(solution)/shard_map/projection/split_down/pallas_call | solution.py:243
  54.2 0.9 copy-done.4
  55.1 1.6 %collective-permute-done.5.refs_1_.one_ref = bf16[8,96,128]{2,1,0:T(8,128)(2,1)S(1)} collective-permute-done((bf16[8,96,128]{2,1,0:T(8,128)(2,1)S(1)}, bf16[8,96,128]{2,1,0:T(8,128)(2,1)S(1)}, u32[]{:S(2)}, u32[]{:S(2)}) %collective-permute-start.5) | collective-permute-done | bytes 196640 | tf_op jit(solution)/shard_map/projection/ppermute | solution.py:519
  56.7 1.7 %collective-permute-done.7.refs_3_.two_ref = bf16[8,96,128]{2,1,0:T(8,128)(2,1)S(1)} collective-permute-done((bf16[8,96,128]{2,1,0:T(8,128)(2,1)S(1)}, bf16[8,96,128]{2,1,0:T(8,128)(2,1)S(1)}, u32[]{:S(2)}, u32[]{:S(2)}) %collective-permute-start.7) | collective-permute-done | bytes 196640 | tf_op jit(solution)/shard_map/projection/ppermute | solution.py:519
  58.4 2.2 %all-to-all-done.1.in_ref = bf16[32,48,128]{2,1,0:T(8,128)(2,1)} async-done(((bf16[32,48,128]{2,1,0:T(8,128)(2,1)}), bf16[32,48,128]{2,1,0:T(8,128)(2,1)}, u32[]{:S(2)}, u32[]{:S(2)}) %all-to-all-start.1) | async-done | bytes 393248 | tf_op jit(solution)/shard_map/projection/all_to_all | solution.py:544
  60.5 1.9 %routed_residual.1.after_ref = bf16[32,48,128]{2,1,0:T(8,128)(2,1)} custom-call(bf16[32,48,128]{2,1,0:T(8,128)(2,1)} %all-to-all-done.1.in_ref, f32[48,128]{1,0:T(8,128)S(1)} %copy-done.15, bf16[8,96,128]{2,1,0:T(8,128)(2,1)S(1)} %collective-permute-done.5.refs_1_.one_ref, bf16[8,96,128]{2,1,0:T(8,128)(2,1)S(1)} %collective-permute-done.7.refs_3_.two_ref, ...), custom_call_target="tpu_custom_call" | custom-call | flops 1048576 | bytes 1048576 | tf_op jit(solution)/shard_map/projection/routed_residual/pallas_call | solution.py:370
  62.4 6.2 %all-to-all-start.2 = ((bf16[32,48,128]{2,1,0:T(8,128)(2,1)}), bf16[32,48,128]{2,1,0:T(8,128)(2,1)S(1)}, u32[]{:S(2)}, u32[]{:S(2)}) async-start(bf16[32,48,128]{2,1,0:T(8,128)(2,1)} %routed_residual.1.after_ref), calls=%async_computation.2 | async-start | bytes 786432 | tf_op jit(solution)/shard_map/expert/all_to_all | solution.py:552
  68.7 2.3 %collective-permute-start.6 = (bf16[8,96,128]{2,1,0:T(8,128)(2,1)S(1)}, bf16[8,96,128]{2,1,0:T(8,128)(2,1)S(1)}, u32[]{:S(2)}, u32[]{:S(2)}) collective-permute-start(bf16[8,96,128]{2,1,0:T(8,128)(2,1)S(1)} %copy-done.17), channel_id=1, source_target_pairs={{0,32},{16,48},{32,0},{48,16},{1,33},{17,49},{33,1},{49,17},{2,34}... | collective-permute-start | bytes 589832 | tf_op jit(solution)/shard_map/projection/ppermute | solution.py:519
  71.0 0.0 collective-permute-done.9.theirs_ref
  71.0 6.4 %split_up.1 = (bf16[576,3072]{1,0:T(8,128)(2,1)S(1)}, f32[8,128]{1,0:T(8,128)S(1)}) custom-call(s32[3]{0:T(128)S(1)} %pad_add_fusion.where_ref, bf16[288,6144]{1,0:T(8,128)(2,1)} %bitcast.42, bf16[288,6144]{1,0:T(8,128)(2,1)} %collective-permute-done.9.theirs_ref, bf16[32,48,128]{2,1,0:T(8,128)(2,1)} %routed_residual.1.after_ref), custom_call_target="tpu_custom_call" | custom-call | flops 5435817984 | bytes 11534336 | tf_op jit(solution)/shard_map/expert/split_up/pallas_call | solution.py:273
  77.5 1.7 %copy-done = bf16[576,3072]{1,0:T(8,128)(2,1)} copy-done((bf16[576,3072]{1,0:T(8,128)(2,1)}, bf16[576,3072]{1,0:T(8,128)(2,1)S(1)}, u32[]{:S(2)}) %copy-start) | copy-done | bytes 3538968
  79.2 0.0 collective-permute-start.10
  79.2 0.4 collective-permute-done.6.refs_2_.after_ref
  79.6 2.5 %all-to-all-done.2.value_ref = bf16[32,48,128]{2,1,0:T(8,128)(2,1)S(1)} async-done(((bf16[32,48,128]{2,1,0:T(8,128)(2,1)}), bf16[32,48,128]{2,1,0:T(8,128)(2,1)S(1)}, u32[]{:S(2)}, u32[]{:S(2)}) %all-to-all-start.2) | async-done | bytes 393248 | tf_op jit(solution)/shard_map/expert/all_to_all | solution.py:552
  82.2 0.0 collective-permute-done.10.after_ref
  82.2 2.0 %copy-done.1 = bf16[576,3072]{1,0:T(8,128)(2,1)S(1)} copy-done((bf16[576,3072]{1,0:T(8,128)(2,1)S(1)}, bf16[576,3072]{1,0:T(8,128)(2,1)}, u32[]{:S(2)}) %copy-start.1) | copy-done | bytes 3538968
  84.2 1.1 up_project.1.mine_ref
  85.3 0.1 collective-permute-start.11
  85.4 1.6 %collective-permute-done.11.theirs_ref = f32[584,64]{1,0:T(8,128)S(1)} collective-permute-done((f32[584,64]{1,0:T(8,128)S(1)}, f32[584,64]{1,0:T(8,128)S(1)}, u32[]{:S(2)}, u32[]{:S(2)}) %collective-permute-start.11) | collective-permute-done | bytes 149536 | tf_op jit(solution)/shard_map/expert/ppermute | solution.py:513
  87.0 0.9 down_project.1
  87.9 1.5 %collective-permute-start.12 = (bf16[64,768]{1,0:T(8,128)(2,1)S(1)}, bf16[64,768]{1,0:T(8,128)(2,1)S(1)}, u32[]{:S(2)}, u32[]{:S(2)}) collective-permute-start(bf16[64,768]{1,0:T(8,128)(2,1)S(1)} %get-tuple-element.46), channel_id=1, source_target_pairs={{0,16},{16,32},{32,48},{48,0},{1,17},{17,33},{33,49},{49,1},{2,18}... | collective-permute-start | bytes 294920 | tf_op jit(solution)/shard_map/expert/ppermute | solution.py:519
  89.5 2.2 %collective-permute-start.13 = (bf16[64,768]{1,0:T(8,128)(2,1)S(1)}, bf16[64,768]{1,0:T(8,128)(2,1)S(1)}, u32[]{:S(2)}, u32[]{:S(2)}) collective-permute-start(bf16[64,768]{1,0:T(8,128)(2,1)S(1)} %get-tuple-element.47), channel_id=1, source_target_pairs={{0,32},{16,48},{32,0},{48,16},{1,33},{17,49},{33,1},{49,17},{2,34}... | collective-permute-start | bytes 294920 | tf_op jit(solution)/shard_map/expert/ppermute | solution.py:519
  91.7 1.1 collective-permute-start.14
  92.7 0.2 add_rest.1.rest_ref
  92.9 0.0 collective-permute-done.12.refs_1_
  92.9 3.7 %collective-permute-done.13.refs_2_ = bf16[64,768]{1,0:T(8,128)(2,1)S(1)} collective-permute-done((bf16[64,768]{1,0:T(8,128)(2,1)S(1)}, bf16[64,768]{1,0:T(8,128)(2,1)S(1)}, u32[]{:S(2)}, u32[]{:S(2)}) %collective-permute-start.13) | collective-permute-done | bytes 98336 | tf_op jit(solution)/shard_map/expert/ppermute | solution.py:519
  96.6 1.0 collective-permute-done.14.refs_3_
  97.6 0.3 merge.1
  98.0 20.0 %all_to_all.20 = bf16[32,48,128]{2,1,0:T(8,128)(2,1)S(1)} all-to-all(bf16[32,48,128]{2,1,0:T(8,128)(2,1)S(1)} %bitcast.31), channel_id=1, replica_groups=mesh['dp'=4,'x'=4,'z'=8,'core'=2] {'dp','z'}, dimensions={0} | all-to-all | bytes 786432 | tf_op jit(solution)/shard_map/expert/all_to_all | solution.py:557
  118.0 0.8 combine.1
  (39 shorter events, 0.1 us)
Async XLA Ops:
  0.0 18.5 %copy-start.3 = (bf16[128,6144]{1,0:T(8,128)(2,1)S(1)}, bf16[128,6144]{1,0:T(8,128)(2,1)}, u32[]{:S(2)}) copy-start(bf16[128,6144]{1,0:T(8,128)(2,1)} %mine_ref.1) | copy-start | bytes 4718596
  0.0 16.1 %copy-start.21 = (s32[32]{0:T(128)S(1)}, s32[32]{0:T(128)}, u32[]{:S(2)}) copy-start(s32[32]{0:T(128)} %param.10) | copy-start | bytes 388
  0.0 16.3 %copy-start.19 = (s32[32,4,2]{0,2,1:T(2,128)S(1)}, s32[32,4,2]{0,2,1:T(2,128)}, u32[]{:S(2)}) copy-start(s32[32,4,2]{0,2,1:T(2,128)} %param.16) | copy-start | bytes 3076
  0.0 16.4 %copy-start.20 = (f32[32,4,2]{0,2,1:T(2,128)S(1)}, f32[32,4,2]{0,2,1:T(2,128)}, u32[]{:S(2)}) copy-start(f32[32,4,2]{0,2,1:T(2,128)} %param.17) | copy-start | bytes 3076
  0.0 16.5 %copy-start.18 = (bf16[96,32,4]{0,2,1:T(4,128)(2,1)S(1)}, bf16[96,32,4]{0,2,1:T(4,128)(2,1)}, u32[]{:S(2)}) copy-start(bf16[96,32,4]{0,2,1:T(4,128)(2,1)} %param.15) | copy-start | bytes 73732
  0.0 71.0 %collective-permute-start.9 = (bf16[288,6144]{1,0:T(8,128)(2,1)}, bf16[288,6144]{1,0:T(8,128)(2,1)}, u32[]{:S(2)}, u32[]{:S(2)}) collective-permute-start(bf16[288,6144]{1,0:T(8,128)(2,1)} %bitcast.41), channel_id=1, source_target_pairs={{0,1},{1,0},{2,3},{3,2},{4,5},{5,4},{6,7},{7,6},{8,9},{9,8},{10,11... | collective-permute-start | bytes 10616840 | tf_op jit(solution)/shard_map/expert/ppermute | solution.py:513
  0.1 18.4 %collective-permute-start = (bf16[128,6144]{1,0:T(8,128)(2,1)}, bf16[128,6144]{1,0:T(8,128)(2,1)}, u32[]{:S(2)}, u32[]{:S(2)}) collective-permute-start(bf16[128,6144]{1,0:T(8,128)(2,1)} %mine_ref.1), channel_id=1, source_target_pairs={{0,1},{1,0},{2,3},{3,2},{4,5},{5,4},{6,7},{7,6},{8,9},{9,8},{10,11... | collective-permute-start | bytes 4718600 | tf_op jit(solution)/shard_map/weights/ppermute | solution.py:513
  0.6 48.7 %collective-permute-start.8 = (bf16[144,6144]{1,0:T(8,128)(2,1)}, bf16[144,6144]{1,0:T(8,128)(2,1)}, u32[]{:S(2)}, u32[]{:S(2)}) collective-permute-start(bf16[144,6144]{1,0:T(8,128)(2,1)} %bitcast.28), channel_id=1, source_target_pairs={{0,1},{1,0},{2,3},{3,2},{4,5},{5,4},{6,7},{7,6},{8,9},{9,8},{10,11... | collective-permute-start | bytes 5308424 | tf_op jit(solution)/shard_map/projection/ppermute | solution.py:513
  3.4 22.3 %all-to-all-start = ((bf16[64,3,4,128]{3,2,1,0:T(4,128)(2,1)}), bf16[64,3,4,128]{3,2,1,0:T(4,128)(2,1)S(1)}, u32[]{:S(2)}, u32[]{:S(2)}) async-start(bf16[64,3,4,128]{3,2,1,0:T(4,128)(2,1)} %attend.1.after_ref), calls=%async_computation | async-start | bytes 393216 | tf_op jit(solution)/shard_map/attention/all_to_all | solution.py:530
  16.6 1.9 %copy-start.6 = (bf16[128,128]{1,0:T(8,128)(2,1)}, bf16[128,128]{1,0:T(8,128)(2,1)S(1)}, u32[]{:S(2)}) copy-start(bf16[128,128]{1,0:T(8,128)(2,1)S(1)} %pad.4.hidden_ref) | copy-start | bytes 98308
  17.2 0.6 copy-start.10
  17.8 0.6 copy-start.12
  26.8 5.9 %collective-permute-start.1 = (bf16[68,4,128]{2,1,0:T(4,128)(2,1)S(1)}, bf16[68,4,128]{2,1,0:T(4,128)(2,1)S(1)}, u32[]{:S(2)}, u32[]{:S(2)}) collective-permute-start(bf16[68,4,128]{2,1,0:T(4,128)(2,1)S(1)} %get-tuple-element.32), channel_id=1, source_target_pairs={{0,64},{64,128},{128,192},{192,0},{1,65},{65,129},{129,193},{193,1... | collective-permute-start | bytes 208904 | tf_op jit(solution)/shard_map/heads/ppermute | solution.py:519
  28.4 6.6 %collective-permute-start.2 = (bf16[68,4,128]{2,1,0:T(4,128)(2,1)S(1)}, bf16[68,4,128]{2,1,0:T(4,128)(2,1)S(1)}, u32[]{:S(2)}, u32[]{:S(2)}) collective-permute-start(bf16[68,4,128]{2,1,0:T(4,128)(2,1)S(1)} %get-tuple-element.33), channel_id=1, source_target_pairs={{0,128},{64,192},{128,0},{192,64},{1,129},{65,193},{129,1},{193,65... | collective-permute-start | bytes 208904 | tf_op jit(solution)/shard_map/heads/ppermute | solution.py:519
  31.3 4.3 %collective-permute-start.3 = (bf16[68,4,128]{2,1,0:T(4,128)(2,1)S(1)}, bf16[68,4,128]{2,1,0:T(4,128)(2,1)S(1)}, u32[]{:S(2)}, u32[]{:S(2)}) collective-permute-start(bf16[68,4,128]{2,1,0:T(4,128)(2,1)S(1)} %get-tuple-element.34), channel_id=1, source_target_pairs={{0,192},{64,0},{128,64},{192,128},{1,193},{65,1},{129,65},{193,129... | collective-permute-start | bytes 208904 | tf_op jit(solution)/shard_map/heads/ppermute | solution.py:519
  36.8 0.6 copy-start.14
  37.4 1.2 %collective-permute-start.4 = (bf16[192,128]{1,0:T(8,128)(2,1)S(1)}, bf16[192,128]{1,0:T(8,128)(2,1)S(1)}, u32[]{:S(2)}, u32[]{:S(2)}) collective-permute-start(bf16[192,128]{1,0:T(8,128)(2,1)S(1)} %get-tuple-element.35.mine_ref), channel_id=1, source_target_pairs={{0,1},{1,0},{2,3},{3,2},{4,5},{5,4},{6,7},{7,6},{8,9},{9,8},{10,11... | collective-permute-start | bytes 147464 | tf_op jit(solution)/shard_map/heads/ppermute | solution.py:513
  38.6 10.7 %copy-start.2 = (bf16[1,144,6144]{2,1,0:T(8,128)(2,1)S(1)}, bf16[1,144,6144]{2,1,0:T(8,128)(2,1)}, u32[]{:S(2)}) copy-start(bf16[1,144,6144]{2,1,0:T(8,128)(2,1)} %param.19) | copy-start | bytes 5308420
  40.1 20.4 %all-to-all-start.1 = ((bf16[32,48,128]{2,1,0:T(8,128)(2,1)}), bf16[32,48,128]{2,1,0:T(8,128)(2,1)}, u32[]{:S(2)}, u32[]{:S(2)}) async-start(bf16[32,48,128]{2,1,0:T(8,128)(2,1)} %bitcast.14), calls=%async_computation.1 | async-start | bytes 786432 | tf_op jit(solution)/shard_map/projection/all_to_all | solution.py:544
  47.2 9.4 %copy-start.8 = (bf16[8,96,128]{2,1,0:T(8,128)(2,1)}, bf16[8,96,128]{2,1,0:T(8,128)(2,1)S(1)}, u32[]{:S(2)}) copy-start(bf16[8,96,128]{2,1,0:T(8,128)(2,1)S(1)} %get-tuple-element.36.refs_0_) | copy-start | bytes 589828
  47.2 9.4 %copy-start.16 = (bf16[8,96,128]{2,1,0:T(8,128)(2,1)}, bf16[8,96,128]{2,1,0:T(8,128)(2,1)S(1)}, u32[]{:S(2)}) copy-start(bf16[8,96,128]{2,1,0:T(8,128)(2,1)S(1)} %get-tuple-element.38) | copy-start | bytes 589828
  47.3 13.3 %copy-start.15 = (f32[48,128]{1,0:T(8,128)S(1)}, f32[48,128]{1,0:T(8,128)}, u32[]{:S(2)}) copy-start(f32[48,128]{1,0:T(8,128)} %copy-done.14) | copy-start | bytes 73732
  47.3 9.4 %collective-permute-start.5 = (bf16[8,96,128]{2,1,0:T(8,128)(2,1)S(1)}, bf16[8,96,128]{2,1,0:T(8,128)(2,1)S(1)}, u32[]{:S(2)}, u32[]{:S(2)}) collective-permute-start(bf16[8,96,128]{2,1,0:T(8,128)(2,1)S(1)} %get-tuple-element.37), channel_id=1, source_target_pairs={{0,16},{16,32},{32,48},{48,0},{1,17},{17,33},{33,49},{49,1},{2,18}... | collective-permute-start | bytes 589832 | tf_op jit(solution)/shard_map/projection/ppermute | solution.py:519
  48.8 9.6 %collective-permute-start.7 = (bf16[8,96,128]{2,1,0:T(8,128)(2,1)S(1)}, bf16[8,96,128]{2,1,0:T(8,128)(2,1)S(1)}, u32[]{:S(2)}, u32[]{:S(2)}) collective-permute-start(bf16[8,96,128]{2,1,0:T(8,128)(2,1)S(1)} %get-tuple-element.39), channel_id=1, source_target_pairs={{0,48},{16,0},{32,16},{48,32},{1,49},{17,1},{33,17},{49,33},{2,50}... | collective-permute-start | bytes 589832 | tf_op jit(solution)/shard_map/projection/ppermute | solution.py:519
  54.2 0.9 copy-start.4
  58.4 10.3 %copy-start.17 = (bf16[8,96,128]{2,1,0:T(8,128)(2,1)S(1)}, bf16[8,96,128]{2,1,0:T(8,128)(2,1)}, u32[]{:S(2)}) copy-start(bf16[8,96,128]{2,1,0:T(8,128)(2,1)} %copy-done.16) | copy-start | bytes 589828
  62.4 19.7 %all-to-all-start.2 = ((bf16[32,48,128]{2,1,0:T(8,128)(2,1)}), bf16[32,48,128]{2,1,0:T(8,128)(2,1)S(1)}, u32[]{:S(2)}, u32[]{:S(2)}) async-start(bf16[32,48,128]{2,1,0:T(8,128)(2,1)} %routed_residual.1.after_ref), calls=%async_computation.2 | async-start | bytes 786432 | tf_op jit(solution)/shard_map/expert/all_to_all | solution.py:552
  68.7 10.9 %collective-permute-start.6 = (bf16[8,96,128]{2,1,0:T(8,128)(2,1)S(1)}, bf16[8,96,128]{2,1,0:T(8,128)(2,1)S(1)}, u32[]{:S(2)}, u32[]{:S(2)}) collective-permute-start(bf16[8,96,128]{2,1,0:T(8,128)(2,1)S(1)} %copy-done.17), channel_id=1, source_target_pairs={{0,32},{16,48},{32,0},{48,16},{1,33},{17,49},{33,1},{49,17},{2,34}... | collective-permute-start | bytes 589832 | tf_op jit(solution)/shard_map/projection/ppermute | solution.py:519
  77.5 1.8 %copy-start = (bf16[576,3072]{1,0:T(8,128)(2,1)}, bf16[576,3072]{1,0:T(8,128)(2,1)S(1)}, u32[]{:S(2)}) copy-start(bf16[576,3072]{1,0:T(8,128)(2,1)S(1)} %get-tuple-element.42.weight_ref) | copy-start | bytes 10616836
  79.2 2.9 %collective-permute-start.10 = (f32[8,128]{1,0:T(8,128)S(1)}, f32[8,128]{1,0:T(8,128)S(1)}, u32[]{:S(2)}, u32[]{:S(2)}) collective-permute-start(f32[8,128]{1,0:T(8,128)S(1)} %get-tuple-element.43), channel_id=1, source_target_pairs={{0,1},{1,0},{2,3},{3,2},{4,5},{5,4},{6,7},{7,6},{8,9},{9,8},{10,11... | collective-permute-start | bytes 12296 | tf_op jit(solution)/shard_map/expert/ppermute | solution.py:513
  82.2 2.0 %copy-start.1 = (bf16[576,3072]{1,0:T(8,128)(2,1)S(1)}, bf16[576,3072]{1,0:T(8,128)(2,1)}, u32[]{:S(2)}) copy-start(bf16[576,3072]{1,0:T(8,128)(2,1)} %copy-done) | copy-start | bytes 10616836
  84.2 2.8 %copy-start.5 = (bf16[144,3072]{1,0:T(8,128)(2,1)S(1)}, bf16[144,3072]{1,0:T(8,128)(2,1)}, u32[]{:S(2)}) copy-start(bf16[144,3072]{1,0:T(8,128)(2,1)} %copy-done.4) | copy-start | bytes 2654212
  85.3 7.4 %copy-start.9 = (bf16[8,96,128]{2,1,0:T(8,128)(2,1)S(1)}, bf16[8,96,128]{2,1,0:T(8,128)(2,1)}, u32[]{:S(2)}) copy-start(bf16[8,96,128]{2,1,0:T(8,128)(2,1)} %copy-done.8) | copy-start | bytes 589828
  85.3 1.7 %collective-permute-start.11 = (f32[584,64]{1,0:T(8,128)S(1)}, f32[584,64]{1,0:T(8,128)S(1)}, u32[]{:S(2)}, u32[]{:S(2)}) collective-permute-start(f32[584,64]{1,0:T(8,128)S(1)} %up_project.1.mine_ref), channel_id=1, source_target_pairs={{0,1},{1,0},{2,3},{3,2},{4,5},{5,4},{6,7},{7,6},{8,9},{9,8},{10,11... | collective-permute-start | bytes 448520 | tf_op jit(solution)/shard_map/expert/ppermute | solution.py:513
  87.0 31.0 %copy-start.7 = (bf16[128,128]{1,0:T(8,128)(2,1)S(1)}, bf16[128,128]{1,0:T(8,128)(2,1)}, u32[]{:S(2)}) copy-start(bf16[128,128]{1,0:T(8,128)(2,1)} %copy-done.6) | copy-start | bytes 98308
  87.0 31.0 %copy-start.11 = (f32[128,1]{1,0:T(8,128)S(1)}, f32[128,1]{1,0:T(8,128)}, u32[]{:S(2)}) copy-start(f32[128,1]{1,0:T(8,128)} %copy-done.10) | copy-start | bytes 1540
  87.0 31.0 %copy-start.13 = (bf16[128,128]{1,0:T(8,128)(2,1)S(1)}, bf16[128,128]{1,0:T(8,128)(2,1)}, u32[]{:S(2)}) copy-start(bf16[128,128]{1,0:T(8,128)(2,1)} %copy-done.12) | copy-start | bytes 98308
  87.9 5.0 %collective-permute-start.12 = (bf16[64,768]{1,0:T(8,128)(2,1)S(1)}, bf16[64,768]{1,0:T(8,128)(2,1)S(1)}, u32[]{:S(2)}, u32[]{:S(2)}) collective-permute-start(bf16[64,768]{1,0:T(8,128)(2,1)S(1)} %get-tuple-element.46), channel_id=1, source_target_pairs={{0,16},{16,32},{32,48},{48,0},{1,17},{17,33},{33,49},{49,1},{2,18}... | collective-permute-start | bytes 294920 | tf_op jit(solution)/shard_map/expert/ppermute | solution.py:519
  89.5 7.1 %collective-permute-start.13 = (bf16[64,768]{1,0:T(8,128)(2,1)S(1)}, bf16[64,768]{1,0:T(8,128)(2,1)S(1)}, u32[]{:S(2)}, u32[]{:S(2)}) collective-permute-start(bf16[64,768]{1,0:T(8,128)(2,1)S(1)} %get-tuple-element.47), channel_id=1, source_target_pairs={{0,32},{16,48},{32,0},{48,16},{1,33},{17,49},{33,1},{49,17},{2,34}... | collective-permute-start | bytes 294920 | tf_op jit(solution)/shard_map/expert/ppermute | solution.py:519
  91.7 6.0 %collective-permute-start.14 = (bf16[64,768]{1,0:T(8,128)(2,1)S(1)}, bf16[64,768]{1,0:T(8,128)(2,1)S(1)}, u32[]{:S(2)}, u32[]{:S(2)}) collective-permute-start(bf16[64,768]{1,0:T(8,128)(2,1)S(1)} %get-tuple-element.48), channel_id=1, source_target_pairs={{0,48},{16,0},{32,16},{48,32},{1,49},{17,1},{33,17},{49,33},{2,50}... | collective-permute-start | bytes 294920 | tf_op jit(solution)/shard_map/expert/ppermute | solution.py:519

commit v6 on v4

--- a/solution.py
+++ b/solution.py
@@ -440,7 +440,8 @@
 
 def merge_kernel(rest_ref, *refs):
     in_refs, out_ref = refs[:-1], refs[-1]
-    out_ref[:, :, :32] = rest_ref[...]
+    for block in range(NZ):
+        out_ref[block, :, :32] = rest_ref[:, block]
     row = lax.broadcasted_iota(jnp.int32, (384, 512), 0)
     lane = lax.broadcasted_iota(jnp.int32, (384, 512), 1)
     spread = one_hot((row == lane // 128 * 96 + lane % 128) & (lane % 128 < 96))
@@ -449,7 +450,7 @@
         total = jnp.dot(total, spread, preferred_element_type=F32).astype(BF16)
         for block in range(4):
             part = total[:, block * 128 : block * 128 + 128]
-            out_ref[:, half * 4 + block, 32:] = part.reshape(4, 16, 128)
+            out_ref[half * 4 + block, :, 32:] = part.reshape(4, 16, 128)
 
 
 def merge(rest, parts):
@@ -457,7 +458,7 @@
         merge_kernel,
         in_specs=[vmem_spec()] * (1 + NX),
         out_specs=vmem_spec(),
-        out_shape=shape((4, NZ, 48, 128)),
+        out_shape=shape((NZ, 4, 48, 128)),
         cost_estimate=cost(MIB, MIB),
         compiler_params=params(),
         name="merge",
@@ -465,7 +466,7 @@
 
 
 def combine_kernel(parts_ref, place_ref, weight_ref, hidden_ref, out_ref):
-    parts = jnp.sum(parts_ref[...].astype(F32), 1)
+    parts = jnp.sum(parts_ref[...].astype(F32), 0)
     residual = hidden_ref[...].astype(F32) + parts[:, :32].reshape(128, 128)
     result = parts[:, 32:].astype(BF16).reshape(64, 128)
     fetched = jnp.dot(place_ref[:, :64], result, preferred_element_type=F32)
@@ -544,9 +545,9 @@
         results = down_project(products, swap(products), keep_down, other_down)
         rest = add_rest(rest)
         merged = merge(rest, shifted(results, "x")).reshape(32, 48, 128)
-        returned = lax.all_to_all(merged, ("dp", "z"), 0, 0, tiled=True)
+        returned = lax.all_to_all(merged, ("z", "dp"), 0, 0, tiled=True)
     with jax.named_scope("output"):
-        mixed = combine(returned.reshape(4, NZ, 48, 128), place, weight, hidden)
+        mixed = combine(returned.reshape(NZ, 4, 48, 128), place, weight, hidden)
         return mixed.reshape(32, 4, 96).transpose(2, 0, 1)
 
 

time: 121 us -> 121 us (level)
  no operation moved by 1% of the time
where the time goes in v6:
time: 121 us; the launch traced here: 120 us
  starting transfers between devices  40.2 us (33%)
  Pallas kernels  27.4 us (23%)
  waiting for transfers between devices  23.1 us (19%)
  blocking collectives  21 us (17%)
  local copies, waits for them, and re-layouts  6.95 us (6%)
    all_to_all x1, blocking collectives, per_device(): returned = lax.all_to_all(merged, ('z', 'dp'), 0, 0, tiled=True)  21 us
    ppermute x9, starting transfers between devices, shifted(): lax.ppermute(blocks[far], axis, [(i, (i + far) % count) for i in range(co...  15.1 us
    all_to_all x1, starting transfers between devices, per_device(): parts = lax.all_to_all(local, HEAD, 0, 0, tiled=True)  12.1 us
    ppermute x9, waiting for transfers between devices, shifted(): lax.ppermute(blocks[far], axis, [(i, (i + far) % count) for i in range(co...  11.3 us
    unnamed x46, local copies, waits for them, and re-layouts  6.79 us
    pallas_call x1, Pallas kernels, split_up(): pl.pallas_call(split_up_kernel, grid=(width // 1536,), in_specs=[smem_spe...  6.43 us
    all_to_all x1, starting transfers between devices, per_device(): lax.all_to_all(routed, ('z', 'x'), 0, 0, tiled=True)  6.22 us
    all_to_all x1, starting transfers between devices, per_device(): lax.all_to_all(partial.reshape(NZ * NX, 48, 128), ('z', 'x'), 0, 0, tiled...  6.04 us
  transfers between devices with their start and end apart: 18, of which 12 were waited for; matrix products, arithmetic and copies ran while one was open for 0% of the time, Pallas kernels for 20%

profile of v6, /device:TPU:2, one launch (start us, length us, event | category | flops | bytes accessed | tf_op | source)
XLA Modules:
  0.0 119.7 jit_solution(12105810400080916618)
XLA Ops:
  0.0 0.1 collective-permute-start.9
  0.1 0.5 collective-permute-start
  0.6 0.1 collective-permute-start.8
  0.7 2.7 %attend.1.after_ref = bf16[64,3,4,128]{3,2,1,0:T(4,128)(2,1)} custom-call(bf16[64,128,128]{2,1,0:T(8,128)(2,1)} %bitcast.38, bf16[64,3,4,128]{3,2,1,0:T(4,128)(2,1)} %bitcast.39), custom_call_target="tpu_custom_call" | custom-call | flops 16777216 | bytes 3145728 | tf_op jit(solution)/shard_map/attention/attend/pallas_call | solution.py:85
  3.4 12.1 %all-to-all-start = ((bf16[64,3,4,128]{3,2,1,0:T(4,128)(2,1)}), bf16[64,3,4,128]{3,2,1,0:T(4,128)(2,1)S(1)}, u32[]{:S(2)}, u32[]{:S(2)}) async-start(bf16[64,3,4,128]{3,2,1,0:T(4,128)(2,1)} %attend.1.after_ref), calls=%async_computation | async-start | bytes 393216 | tf_op jit(solution)/shard_map/attention/all_to_all | solution.py:521
  16.1 0.1 broadcast_in_dim.3
  16.2 0.1 reshape.52.row_ref
  16.3 0.1 copy.14
  16.4 0.1 copy.15
  16.5 0.0 copy-done.18
  16.6 0.6 route.1
  17.2 0.6 copy-done.10
  17.8 0.6 copy-done.12
  18.4 0.1 pad_add_fusion.where_ref
  18.5 0.0 collective-permute-done.theirs_ref
  18.5 2.9 %split_out.1 = (bf16[32,96,128]{2,1,0:T(8,128)(2,1)S(1)}, bf16[32,96,128]{2,1,0:T(8,128)(2,1)S(1)}) custom-call(s32[3]{0:T(128)S(1)} %pad_add_fusion.where_ref, bf16[128,6144]{1,0:T(8,128)(2,1)S(1)} %copy-done.3, bf16[128,6144]{1,0:T(8,128)(2,1)} %collective-permute-done.theirs_ref, bf16[64,3,4,128]{3,2,1,0:T(4,128)(2,1)} %attend.1.after_ref), custom_call_target="tpu_custom_call" | custom-call | flops 603979776 | bytes 3145728 | tf_op jit(solution)/shard_map/weights/split_out/pallas_call | solution.py:214
  21.4 4.3 %all-to-all-done.parts_ref = bf16[64,3,4,128]{3,2,1,0:T(4,128)(2,1)S(1)} async-done(((bf16[64,3,4,128]{3,2,1,0:T(4,128)(2,1)}), bf16[64,3,4,128]{3,2,1,0:T(4,128)(2,1)S(1)}, u32[]{:S(2)}, u32[]{:S(2)}) %all-to-all-start) | async-done | bytes 196640 | tf_op jit(solution)/shard_map/attention/all_to_all | solution.py:521
  25.7 1.1 decay_heads.1
  26.8 1.7 %collective-permute-start.1 = (bf16[68,4,128]{2,1,0:T(4,128)(2,1)S(1)}, bf16[68,4,128]{2,1,0:T(4,128)(2,1)S(1)}, u32[]{:S(2)}, u32[]{:S(2)}) collective-permute-start(bf16[68,4,128]{2,1,0:T(4,128)(2,1)S(1)} %get-tuple-element.32), channel_id=1, source_target_pairs={{0,64},{64,128},{128,192},{192,0},{1,65},{65,129},{129,193},{193,1... | collective-permute-start | bytes 208904 | tf_op jit(solution)/shard_map/heads/ppermute | solution.py:510
  28.4 2.9 %collective-permute-start.2 = (bf16[68,4,128]{2,1,0:T(4,128)(2,1)S(1)}, bf16[68,4,128]{2,1,0:T(4,128)(2,1)S(1)}, u32[]{:S(2)}, u32[]{:S(2)}) collective-permute-start(bf16[68,4,128]{2,1,0:T(4,128)(2,1)S(1)} %get-tuple-element.33), channel_id=1, source_target_pairs={{0,128},{64,192},{128,0},{192,64},{1,129},{65,193},{129,1},{193,65... | collective-permute-start | bytes 208904 | tf_op jit(solution)/shard_map/heads/ppermute | solution.py:510
  31.3 1.3 %collective-permute-start.3 = (bf16[68,4,128]{2,1,0:T(4,128)(2,1)S(1)}, bf16[68,4,128]{2,1,0:T(4,128)(2,1)S(1)}, u32[]{:S(2)}, u32[]{:S(2)}) collective-permute-start(bf16[68,4,128]{2,1,0:T(4,128)(2,1)S(1)} %get-tuple-element.34), channel_id=1, source_target_pairs={{0,192},{64,0},{128,64},{192,128},{1,193},{65,1},{129,65},{193,129... | collective-permute-start | bytes 208904 | tf_op jit(solution)/shard_map/heads/ppermute | solution.py:510
  32.7 0.0 collective-permute-done.1
  32.7 2.4 %collective-permute-done.2 = bf16[68,4,128]{2,1,0:T(4,128)(2,1)S(1)} collective-permute-done((bf16[68,4,128]{2,1,0:T(4,128)(2,1)S(1)}, bf16[68,4,128]{2,1,0:T(4,128)(2,1)S(1)}, u32[]{:S(2)}, u32[]{:S(2)}) %collective-permute-start.2) | collective-permute-done | bytes 69664 | tf_op jit(solution)/shard_map/heads/ppermute | solution.py:510
  35.1 0.6 collective-permute-done.3
  35.6 1.1 select.2
  36.8 0.6 copy-done.14
  37.4 0.0 collective-permute-start.4
  37.4 1.2 %collective-permute-done.4.theirs_ref = bf16[192,128]{1,0:T(8,128)(2,1)S(1)} collective-permute-done((bf16[192,128]{1,0:T(8,128)(2,1)S(1)}, bf16[192,128]{1,0:T(8,128)(2,1)S(1)}, u32[]{:S(2)}, u32[]{:S(2)}) %collective-permute-start.4) | collective-permute-done | bytes 49184 | tf_op jit(solution)/shard_map/heads/ppermute | solution.py:504
  38.6 1.4 %project.1.after_ref = bf16[8,4,48,128]{3,2,1,0:T(8,128)(2,1)} custom-call(bf16[32,96,128]{2,1,0:T(8,128)(2,1)S(1)} %get-tuple-element.28.after_ref.keep_ref, bf16[32,96,128]{2,1,0:T(8,128)(2,1)S(1)} %get-tuple-element.29.other_ref, bf16[192,128]{1,0:T(8,128)(2,1)S(1)} %get-tuple-element.35.mine_ref, bf16[192,128]{1,0:T(8,128)(2,1)S(1)} %collective-permute-done.4.theirs_ref), custom_call_target="tpu_custom_call" | custom-call | flops 201326592 | bytes 2097152 | tf_op jit(solution)/shard_map/projection/project/pallas_call | solution.py:301
  40.1 6.0 %all-to-all-start.1 = ((bf16[32,48,128]{2,1,0:T(8,128)(2,1)}), bf16[32,48,128]{2,1,0:T(8,128)(2,1)}, u32[]{:S(2)}, u32[]{:S(2)}) async-start(bf16[32,48,128]{2,1,0:T(8,128)(2,1)} %bitcast.14), calls=%async_computation.1 | async-start | bytes 786432 | tf_op jit(solution)/shard_map/projection/all_to_all | solution.py:535
  46.1 1.1 project_rest.1
  47.3 1.5 %collective-permute-start.5 = (bf16[8,96,128]{2,1,0:T(8,128)(2,1)S(1)}, bf16[8,96,128]{2,1,0:T(8,128)(2,1)S(1)}, u32[]{:S(2)}, u32[]{:S(2)}) collective-permute-start(bf16[8,96,128]{2,1,0:T(8,128)(2,1)S(1)} %get-tuple-element.37), channel_id=1, source_target_pairs={{0,16},{16,32},{32,48},{48,0},{1,17},{17,33},{33,49},{49,1},{2,18}... | collective-permute-start | bytes 589832 | tf_op jit(solution)/shard_map/projection/ppermute | solution.py:510
  48.8 0.6 collective-permute-start.7
  49.4 0.0 collective-permute-done.8.theirs_ref
  49.4 4.8 %split_down.1 = (bf16[144,3072]{1,0:T(8,128)(2,1)S(1)}, bf16[144,3072]{1,0:T(8,128)(2,1)S(1)}) custom-call(s32[3]{0:T(128)S(1)} %pad_add_fusion.where_ref, bf16[144,6144]{1,0:T(8,128)(2,1)S(1)} %bitcast.29, bf16[144,6144]{1,0:T(8,128)(2,1)} %collective-permute-done.8.theirs_ref, bf16[8,4,48,128]{3,2,1,0:T(8,128)(2,1)} %project.1.after_ref), custom_call_target="tpu_custom_call" | custom-call | flops 905969664 | bytes 4194304 | tf_op jit(solution)/shard_map/projection/split_down/pallas_call | solution.py:243
  54.2 0.9 copy-done.4
  55.1 1.6 %collective-permute-done.5.refs_1_.one_ref = bf16[8,96,128]{2,1,0:T(8,128)(2,1)S(1)} collective-permute-done((bf16[8,96,128]{2,1,0:T(8,128)(2,1)S(1)}, bf16[8,96,128]{2,1,0:T(8,128)(2,1)S(1)}, u32[]{:S(2)}, u32[]{:S(2)}) %collective-permute-start.5) | collective-permute-done | bytes 196640 | tf_op jit(solution)/shard_map/projection/ppermute | solution.py:510
  56.7 1.7 %collective-permute-done.7.refs_3_.two_ref = bf16[8,96,128]{2,1,0:T(8,128)(2,1)S(1)} collective-permute-done((bf16[8,96,128]{2,1,0:T(8,128)(2,1)S(1)}, bf16[8,96,128]{2,1,0:T(8,128)(2,1)S(1)}, u32[]{:S(2)}, u32[]{:S(2)}) %collective-permute-start.7) | collective-permute-done | bytes 196640 | tf_op jit(solution)/shard_map/projection/ppermute | solution.py:510
  58.4 2.2 %all-to-all-done.1.in_ref = bf16[32,48,128]{2,1,0:T(8,128)(2,1)} async-done(((bf16[32,48,128]{2,1,0:T(8,128)(2,1)}), bf16[32,48,128]{2,1,0:T(8,128)(2,1)}, u32[]{:S(2)}, u32[]{:S(2)}) %all-to-all-start.1) | async-done | bytes 393248 | tf_op jit(solution)/shard_map/projection/all_to_all | solution.py:535
  60.5 1.8 %routed_residual.1.after_ref = bf16[32,48,128]{2,1,0:T(8,128)(2,1)} custom-call(bf16[32,48,128]{2,1,0:T(8,128)(2,1)} %all-to-all-done.1.in_ref, f32[48,128]{1,0:T(8,128)S(1)} %copy-done.15, bf16[8,96,128]{2,1,0:T(8,128)(2,1)S(1)} %collective-permute-done.5.refs_1_.one_ref, bf16[8,96,128]{2,1,0:T(8,128)(2,1)S(1)} %collective-permute-done.7.refs_3_.two_ref, ...), custom_call_target="tpu_custom_call" | custom-call | flops 1048576 | bytes 1048576 | tf_op jit(solution)/shard_map/projection/routed_residual/pallas_call | solution.py:361
  62.4 6.2 %all-to-all-start.2 = ((bf16[32,48,128]{2,1,0:T(8,128)(2,1)}), bf16[32,48,128]{2,1,0:T(8,128)(2,1)S(1)}, u32[]{:S(2)}, u32[]{:S(2)}) async-start(bf16[32,48,128]{2,1,0:T(8,128)(2,1)} %routed_residual.1.after_ref), calls=%async_computation.2 | async-start | bytes 786432 | tf_op jit(solution)/shard_map/expert/all_to_all | solution.py:543
  68.6 2.3 %collective-permute-start.6 = (bf16[8,96,128]{2,1,0:T(8,128)(2,1)S(1)}, bf16[8,96,128]{2,1,0:T(8,128)(2,1)S(1)}, u32[]{:S(2)}, u32[]{:S(2)}) collective-permute-start(bf16[8,96,128]{2,1,0:T(8,128)(2,1)S(1)} %copy-done.17), channel_id=1, source_target_pairs={{0,32},{16,48},{32,0},{48,16},{1,33},{17,49},{33,1},{49,17},{2,34}... | collective-permute-start | bytes 589832 | tf_op jit(solution)/shard_map/projection/ppermute | solution.py:510
  70.9 0.0 collective-permute-done.9.theirs_ref
  70.9 6.4 %split_up.1 = (bf16[576,3072]{1,0:T(8,128)(2,1)S(1)}, f32[8,128]{1,0:T(8,128)S(1)}) custom-call(s32[3]{0:T(128)S(1)} %pad_add_fusion.where_ref, bf16[288,6144]{1,0:T(8,128)(2,1)} %bitcast.42, bf16[288,6144]{1,0:T(8,128)(2,1)} %collective-permute-done.9.theirs_ref, bf16[32,48,128]{2,1,0:T(8,128)(2,1)} %routed_residual.1.after_ref), custom_call_target="tpu_custom_call" | custom-call | flops 5435817984 | bytes 11534336 | tf_op jit(solution)/shard_map/expert/split_up/pallas_call | solution.py:273
  77.4 1.7 %copy-done = bf16[576,3072]{1,0:T(8,128)(2,1)} copy-done((bf16[576,3072]{1,0:T(8,128)(2,1)}, bf16[576,3072]{1,0:T(8,128)(2,1)S(1)}, u32[]{:S(2)}) %copy-start) | copy-done | bytes 3538968
  79.1 0.0 collective-permute-start.10
  79.1 0.4 collective-permute-done.6.refs_2_.after_ref
  79.5 2.5 %all-to-all-done.2.value_ref = bf16[32,48,128]{2,1,0:T(8,128)(2,1)S(1)} async-done(((bf16[32,48,128]{2,1,0:T(8,128)(2,1)}), bf16[32,48,128]{2,1,0:T(8,128)(2,1)S(1)}, u32[]{:S(2)}, u32[]{:S(2)}) %all-to-all-start.2) | async-done | bytes 393248 | tf_op jit(solution)/shard_map/expert/all_to_all | solution.py:543
  82.1 0.0 collective-permute-done.10.after_ref
  82.1 2.0 %copy-done.1 = bf16[576,3072]{1,0:T(8,128)(2,1)S(1)} copy-done((bf16[576,3072]{1,0:T(8,128)(2,1)S(1)}, bf16[576,3072]{1,0:T(8,128)(2,1)}, u32[]{:S(2)}) %copy-start.1) | copy-done | bytes 3538968
  84.1 1.1 up_project.1.mine_ref
  85.3 0.1 collective-permute-start.11
  85.4 1.6 %collective-permute-done.11.theirs_ref = f32[584,64]{1,0:T(8,128)S(1)} collective-permute-done((f32[584,64]{1,0:T(8,128)S(1)}, f32[584,64]{1,0:T(8,128)S(1)}, u32[]{:S(2)}, u32[]{:S(2)}) %collective-permute-start.11) | collective-permute-done | bytes 149536 | tf_op jit(solution)/shard_map/expert/ppermute | solution.py:504
  86.9 0.9 down_project.1
  87.9 1.5 %collective-permute-start.12 = (bf16[64,768]{1,0:T(8,128)(2,1)S(1)}, bf16[64,768]{1,0:T(8,128)(2,1)S(1)}, u32[]{:S(2)}, u32[]{:S(2)}) collective-permute-start(bf16[64,768]{1,0:T(8,128)(2,1)S(1)} %get-tuple-element.46), channel_id=1, source_target_pairs={{0,16},{16,32},{32,48},{48,0},{1,17},{17,33},{33,49},{49,1},{2,18}... | collective-permute-start | bytes 294920 | tf_op jit(solution)/shard_map/expert/ppermute | solution.py:510
  89.4 2.2 %collective-permute-start.13 = (bf16[64,768]{1,0:T(8,128)(2,1)S(1)}, bf16[64,768]{1,0:T(8,128)(2,1)S(1)}, u32[]{:S(2)}, u32[]{:S(2)}) collective-permute-start(bf16[64,768]{1,0:T(8,128)(2,1)S(1)} %get-tuple-element.47), channel_id=1, source_target_pairs={{0,32},{16,48},{32,0},{48,16},{1,33},{17,49},{33,1},{49,17},{2,34}... | collective-permute-start | bytes 294920 | tf_op jit(solution)/shard_map/expert/ppermute | solution.py:510
  91.6 1.1 collective-permute-start.14
  92.6 0.2 add_rest.1.rest_ref
  92.8 0.0 collective-permute-done.12.refs_1_
  92.8 3.7 %collective-permute-done.13.refs_2_ = bf16[64,768]{1,0:T(8,128)(2,1)S(1)} collective-permute-done((bf16[64,768]{1,0:T(8,128)(2,1)S(1)}, bf16[64,768]{1,0:T(8,128)(2,1)S(1)}, u32[]{:S(2)}, u32[]{:S(2)}) %collective-permute-start.13) | collective-permute-done | bytes 98336 | tf_op jit(solution)/shard_map/expert/ppermute | solution.py:510
  96.5 1.0 collective-permute-done.14.refs_3_
  97.6 0.3 merge.1
  97.9 21.0 %all_to_all.20 = bf16[32,48,128]{2,1,0:T(8,128)(2,1)S(1)} all-to-all(bf16[32,48,128]{2,1,0:T(8,128)(2,1)S(1)} %bitcast.31), channel_id=1, replica_groups=mesh['dp'=4,'x'=4,'z'=8,'core'=2] {'z','dp'}, dimensions={0} | all-to-all | bytes 786432 | tf_op jit(solution)/shard_map/expert/all_to_all | solution.py:548
  119.0 0.8 combine.1
  (39 shorter events, 0.1 us)
Async XLA Ops:
  0.0 18.5 %copy-start.3 = (bf16[128,6144]{1,0:T(8,128)(2,1)S(1)}, bf16[128,6144]{1,0:T(8,128)(2,1)}, u32[]{:S(2)}) copy-start(bf16[128,6144]{1,0:T(8,128)(2,1)} %mine_ref.1) | copy-start | bytes 4718596
  0.0 16.1 %copy-start.21 = (s32[32]{0:T(128)S(1)}, s32[32]{0:T(128)}, u32[]{:S(2)}) copy-start(s32[32]{0:T(128)} %param.10) | copy-start | bytes 388
  0.0 16.3 %copy-start.19 = (s32[32,4,2]{0,2,1:T(2,128)S(1)}, s32[32,4,2]{0,2,1:T(2,128)}, u32[]{:S(2)}) copy-start(s32[32,4,2]{0,2,1:T(2,128)} %param.16) | copy-start | bytes 3076
  0.0 16.4 %copy-start.20 = (f32[32,4,2]{0,2,1:T(2,128)S(1)}, f32[32,4,2]{0,2,1:T(2,128)}, u32[]{:S(2)}) copy-start(f32[32,4,2]{0,2,1:T(2,128)} %param.17) | copy-start | bytes 3076
  0.0 16.5 %copy-start.18 = (bf16[96,32,4]{0,2,1:T(4,128)(2,1)S(1)}, bf16[96,32,4]{0,2,1:T(4,128)(2,1)}, u32[]{:S(2)}) copy-start(bf16[96,32,4]{0,2,1:T(4,128)(2,1)} %param.15) | copy-start | bytes 73732
  0.0 70.9 %collective-permute-start.9 = (bf16[288,6144]{1,0:T(8,128)(2,1)}, bf16[288,6144]{1,0:T(8,128)(2,1)}, u32[]{:S(2)}, u32[]{:S(2)}) collective-permute-start(bf16[288,6144]{1,0:T(8,128)(2,1)} %bitcast.41), channel_id=1, source_target_pairs={{0,1},{1,0},{2,3},{3,2},{4,5},{5,4},{6,7},{7,6},{8,9},{9,8},{10,11... | collective-permute-start | bytes 10616840 | tf_op jit(solution)/shard_map/expert/ppermute | solution.py:504
  0.1 18.4 %collective-permute-start = (bf16[128,6144]{1,0:T(8,128)(2,1)}, bf16[128,6144]{1,0:T(8,128)(2,1)}, u32[]{:S(2)}, u32[]{:S(2)}) collective-permute-start(bf16[128,6144]{1,0:T(8,128)(2,1)} %mine_ref.1), channel_id=1, source_target_pairs={{0,1},{1,0},{2,3},{3,2},{4,5},{5,4},{6,7},{7,6},{8,9},{9,8},{10,11... | collective-permute-start | bytes 4718600 | tf_op jit(solution)/shard_map/weights/ppermute | solution.py:504
  0.6 48.7 %collective-permute-start.8 = (bf16[144,6144]{1,0:T(8,128)(2,1)}, bf16[144,6144]{1,0:T(8,128)(2,1)}, u32[]{:S(2)}, u32[]{:S(2)}) collective-permute-start(bf16[144,6144]{1,0:T(8,128)(2,1)} %bitcast.28), channel_id=1, source_target_pairs={{0,1},{1,0},{2,3},{3,2},{4,5},{5,4},{6,7},{7,6},{8,9},{9,8},{10,11... | collective-permute-start | bytes 5308424 | tf_op jit(solution)/shard_map/projection/ppermute | solution.py:504
  3.4 22.3 %all-to-all-start = ((bf16[64,3,4,128]{3,2,1,0:T(4,128)(2,1)}), bf16[64,3,4,128]{3,2,1,0:T(4,128)(2,1)S(1)}, u32[]{:S(2)}, u32[]{:S(2)}) async-start(bf16[64,3,4,128]{3,2,1,0:T(4,128)(2,1)} %attend.1.after_ref), calls=%async_computation | async-start | bytes 393216 | tf_op jit(solution)/shard_map/attention/all_to_all | solution.py:521
  16.6 1.9 %copy-start.6 = (bf16[128,128]{1,0:T(8,128)(2,1)}, bf16[128,128]{1,0:T(8,128)(2,1)S(1)}, u32[]{:S(2)}) copy-start(bf16[128,128]{1,0:T(8,128)(2,1)S(1)} %pad.4.hidden_ref) | copy-start | bytes 98308
  17.2 0.6 copy-start.10
  17.8 0.6 copy-start.12
  26.8 5.9 %collective-permute-start.1 = (bf16[68,4,128]{2,1,0:T(4,128)(2,1)S(1)}, bf16[68,4,128]{2,1,0:T(4,128)(2,1)S(1)}, u32[]{:S(2)}, u32[]{:S(2)}) collective-permute-start(bf16[68,4,128]{2,1,0:T(4,128)(2,1)S(1)} %get-tuple-element.32), channel_id=1, source_target_pairs={{0,64},{64,128},{128,192},{192,0},{1,65},{65,129},{129,193},{193,1... | collective-permute-start | bytes 208904 | tf_op jit(solution)/shard_map/heads/ppermute | solution.py:510
  28.4 6.6 %collective-permute-start.2 = (bf16[68,4,128]{2,1,0:T(4,128)(2,1)S(1)}, bf16[68,4,128]{2,1,0:T(4,128)(2,1)S(1)}, u32[]{:S(2)}, u32[]{:S(2)}) collective-permute-start(bf16[68,4,128]{2,1,0:T(4,128)(2,1)S(1)} %get-tuple-element.33), channel_id=1, source_target_pairs={{0,128},{64,192},{128,0},{192,64},{1,129},{65,193},{129,1},{193,65... | collective-permute-start | bytes 208904 | tf_op jit(solution)/shard_map/heads/ppermute | solution.py:510
  31.3 4.3 %collective-permute-start.3 = (bf16[68,4,128]{2,1,0:T(4,128)(2,1)S(1)}, bf16[68,4,128]{2,1,0:T(4,128)(2,1)S(1)}, u32[]{:S(2)}, u32[]{:S(2)}) collective-permute-start(bf16[68,4,128]{2,1,0:T(4,128)(2,1)S(1)} %get-tuple-element.34), channel_id=1, source_target_pairs={{0,192},{64,0},{128,64},{192,128},{1,193},{65,1},{129,65},{193,129... | collective-permute-start | bytes 208904 | tf_op jit(solution)/shard_map/heads/ppermute | solution.py:510
  36.8 0.6 copy-start.14
  37.4 1.2 %collective-permute-start.4 = (bf16[192,128]{1,0:T(8,128)(2,1)S(1)}, bf16[192,128]{1,0:T(8,128)(2,1)S(1)}, u32[]{:S(2)}, u32[]{:S(2)}) collective-permute-start(bf16[192,128]{1,0:T(8,128)(2,1)S(1)} %get-tuple-element.35.mine_ref), channel_id=1, source_target_pairs={{0,1},{1,0},{2,3},{3,2},{4,5},{5,4},{6,7},{7,6},{8,9},{9,8},{10,11... | collective-permute-start | bytes 147464 | tf_op jit(solution)/shard_map/heads/ppermute | solution.py:504
  38.6 10.7 %copy-start.2 = (bf16[1,144,6144]{2,1,0:T(8,128)(2,1)S(1)}, bf16[1,144,6144]{2,1,0:T(8,128)(2,1)}, u32[]{:S(2)}) copy-start(bf16[1,144,6144]{2,1,0:T(8,128)(2,1)} %param.19) | copy-start | bytes 5308420
  40.1 20.4 %all-to-all-start.1 = ((bf16[32,48,128]{2,1,0:T(8,128)(2,1)}), bf16[32,48,128]{2,1,0:T(8,128)(2,1)}, u32[]{:S(2)}, u32[]{:S(2)}) async-start(bf16[32,48,128]{2,1,0:T(8,128)(2,1)} %bitcast.14), calls=%async_computation.1 | async-start | bytes 786432 | tf_op jit(solution)/shard_map/projection/all_to_all | solution.py:535
  47.2 9.4 %copy-start.8 = (bf16[8,96,128]{2,1,0:T(8,128)(2,1)}, bf16[8,96,128]{2,1,0:T(8,128)(2,1)S(1)}, u32[]{:S(2)}) copy-start(bf16[8,96,128]{2,1,0:T(8,128)(2,1)S(1)} %get-tuple-element.36.refs_0_) | copy-start | bytes 589828
  47.2 9.4 %copy-start.16 = (bf16[8,96,128]{2,1,0:T(8,128)(2,1)}, bf16[8,96,128]{2,1,0:T(8,128)(2,1)S(1)}, u32[]{:S(2)}) copy-start(bf16[8,96,128]{2,1,0:T(8,128)(2,1)S(1)} %get-tuple-element.38) | copy-start | bytes 589828
  47.3 13.3 %copy-start.15 = (f32[48,128]{1,0:T(8,128)S(1)}, f32[48,128]{1,0:T(8,128)}, u32[]{:S(2)}) copy-start(f32[48,128]{1,0:T(8,128)} %copy-done.14) | copy-start | bytes 73732
  47.3 9.4 %collective-permute-start.5 = (bf16[8,96,128]{2,1,0:T(8,128)(2,1)S(1)}, bf16[8,96,128]{2,1,0:T(8,128)(2,1)S(1)}, u32[]{:S(2)}, u32[]{:S(2)}) collective-permute-start(bf16[8,96,128]{2,1,0:T(8,128)(2,1)S(1)} %get-tuple-element.37), channel_id=1, source_target_pairs={{0,16},{16,32},{32,48},{48,0},{1,17},{17,33},{33,49},{49,1},{2,18}... | collective-permute-start | bytes 589832 | tf_op jit(solution)/shard_map/projection/ppermute | solution.py:510
  48.8 9.6 %collective-permute-start.7 = (bf16[8,96,128]{2,1,0:T(8,128)(2,1)S(1)}, bf16[8,96,128]{2,1,0:T(8,128)(2,1)S(1)}, u32[]{:S(2)}, u32[]{:S(2)}) collective-permute-start(bf16[8,96,128]{2,1,0:T(8,128)(2,1)S(1)} %get-tuple-element.39), channel_id=1, source_target_pairs={{0,48},{16,0},{32,16},{48,32},{1,49},{17,1},{33,17},{49,33},{2,50}... | collective-permute-start | bytes 589832 | tf_op jit(solution)/shard_map/projection/ppermute | solution.py:510
  54.2 0.9 copy-start.4
  58.4 10.2 %copy-start.17 = (bf16[8,96,128]{2,1,0:T(8,128)(2,1)S(1)}, bf16[8,96,128]{2,1,0:T(8,128)(2,1)}, u32[]{:S(2)}) copy-start(bf16[8,96,128]{2,1,0:T(8,128)(2,1)} %copy-done.16) | copy-start | bytes 589828
  62.4 19.7 %all-to-all-start.2 = ((bf16[32,48,128]{2,1,0:T(8,128)(2,1)}), bf16[32,48,128]{2,1,0:T(8,128)(2,1)S(1)}, u32[]{:S(2)}, u32[]{:S(2)}) async-start(bf16[32,48,128]{2,1,0:T(8,128)(2,1)} %routed_residual.1.after_ref), calls=%async_computation.2 | async-start | bytes 786432 | tf_op jit(solution)/shard_map/expert/all_to_all | solution.py:543
  68.6 10.9 %collective-permute-start.6 = (bf16[8,96,128]{2,1,0:T(8,128)(2,1)S(1)}, bf16[8,96,128]{2,1,0:T(8,128)(2,1)S(1)}, u32[]{:S(2)}, u32[]{:S(2)}) collective-permute-start(bf16[8,96,128]{2,1,0:T(8,128)(2,1)S(1)} %copy-done.17), channel_id=1, source_target_pairs={{0,32},{16,48},{32,0},{48,16},{1,33},{17,49},{33,1},{49,17},{2,34}... | collective-permute-start | bytes 589832 | tf_op jit(solution)/shard_map/projection/ppermute | solution.py:510
  77.4 1.8 %copy-start = (bf16[576,3072]{1,0:T(8,128)(2,1)}, bf16[576,3072]{1,0:T(8,128)(2,1)S(1)}, u32[]{:S(2)}) copy-start(bf16[576,3072]{1,0:T(8,128)(2,1)S(1)} %get-tuple-element.42.weight_ref) | copy-start | bytes 10616836
  79.1 2.9 %collective-permute-start.10 = (f32[8,128]{1,0:T(8,128)S(1)}, f32[8,128]{1,0:T(8,128)S(1)}, u32[]{:S(2)}, u32[]{:S(2)}) collective-permute-start(f32[8,128]{1,0:T(8,128)S(1)} %get-tuple-element.43), channel_id=1, source_target_pairs={{0,1},{1,0},{2,3},{3,2},{4,5},{5,4},{6,7},{7,6},{8,9},{9,8},{10,11... | collective-permute-start | bytes 12296 | tf_op jit(solution)/shard_map/expert/ppermute | solution.py:504
  82.1 2.0 %copy-start.1 = (bf16[576,3072]{1,0:T(8,128)(2,1)S(1)}, bf16[576,3072]{1,0:T(8,128)(2,1)}, u32[]{:S(2)}) copy-start(bf16[576,3072]{1,0:T(8,128)(2,1)} %copy-done) | copy-start | bytes 10616836
  84.1 2.8 %copy-start.5 = (bf16[144,3072]{1,0:T(8,128)(2,1)S(1)}, bf16[144,3072]{1,0:T(8,128)(2,1)}, u32[]{:S(2)}) copy-start(bf16[144,3072]{1,0:T(8,128)(2,1)} %copy-done.4) | copy-start | bytes 2654212
  85.2 7.4 %copy-start.9 = (bf16[8,96,128]{2,1,0:T(8,128)(2,1)S(1)}, bf16[8,96,128]{2,1,0:T(8,128)(2,1)}, u32[]{:S(2)}) copy-start(bf16[8,96,128]{2,1,0:T(8,128)(2,1)} %copy-done.8) | copy-start | bytes 589828
  85.3 1.7 %collective-permute-start.11 = (f32[584,64]{1,0:T(8,128)S(1)}, f32[584,64]{1,0:T(8,128)S(1)}, u32[]{:S(2)}, u32[]{:S(2)}) collective-permute-start(f32[584,64]{1,0:T(8,128)S(1)} %up_project.1.mine_ref), channel_id=1, source_target_pairs={{0,1},{1,0},{2,3},{3,2},{4,5},{5,4},{6,7},{7,6},{8,9},{9,8},{10,11... | collective-permute-start | bytes 448520 | tf_op jit(solution)/shard_map/expert/ppermute | solution.py:504
  86.9 32.0 %copy-start.7 = (bf16[128,128]{1,0:T(8,128)(2,1)S(1)}, bf16[128,128]{1,0:T(8,128)(2,1)}, u32[]{:S(2)}) copy-start(bf16[128,128]{1,0:T(8,128)(2,1)} %copy-done.6) | copy-start | bytes 98308
  86.9 32.0 %copy-start.11 = (f32[128,1]{1,0:T(8,128)S(1)}, f32[128,1]{1,0:T(8,128)}, u32[]{:S(2)}) copy-start(f32[128,1]{1,0:T(8,128)} %copy-done.10) | copy-start | bytes 1540
  86.9 32.0 %copy-start.13 = (bf16[128,128]{1,0:T(8,128)(2,1)S(1)}, bf16[128,128]{1,0:T(8,128)(2,1)}, u32[]{:S(2)}) copy-start(bf16[128,128]{1,0:T(8,128)(2,1)} %copy-done.12) | copy-start | bytes 98308
  87.9 5.0 %collective-permute-start.12 = (bf16[64,768]{1,0:T(8,128)(2,1)S(1)}, bf16[64,768]{1,0:T(8,128)(2,1)S(1)}, u32[]{:S(2)}, u32[]{:S(2)}) collective-permute-start(bf16[64,768]{1,0:T(8,128)(2,1)S(1)} %get-tuple-element.46), channel_id=1, source_target_pairs={{0,16},{16,32},{32,48},{48,0},{1,17},{17,33},{33,49},{49,1},{2,18}... | collective-permute-start | bytes 294920 | tf_op jit(solution)/shard_map/expert/ppermute | solution.py:510
  89.4 7.1 %collective-permute-start.13 = (bf16[64,768]{1,0:T(8,128)(2,1)S(1)}, bf16[64,768]{1,0:T(8,128)(2,1)S(1)}, u32[]{:S(2)}, u32[]{:S(2)}) collective-permute-start(bf16[64,768]{1,0:T(8,128)(2,1)S(1)} %get-tuple-element.47), channel_id=1, source_target_pairs={{0,32},{16,48},{32,0},{48,16},{1,33},{17,49},{33,1},{49,17},{2,34}... | collective-permute-start | bytes 294920 | tf_op jit(solution)/shard_map/expert/ppermute | solution.py:510
  91.6 6.0 %collective-permute-start.14 = (bf16[64,768]{1,0:T(8,128)(2,1)S(1)}, bf16[64,768]{1,0:T(8,128)(2,1)S(1)}, u32[]{:S(2)}, u32[]{:S(2)}) collective-permute-start(bf16[64,768]{1,0:T(8,128)(2,1)S(1)} %get-tuple-element.48), channel_id=1, source_target_pairs={{0,48},{16,0},{32,16},{48,32},{1,49},{17,1},{33,17},{49,33},{2,50}... | collective-permute-start | bytes 294920 | tf_op jit(solution)/shard_map/expert/ppermute | solution.py:510
